TPU v7x, 1024 devices: a whole 4x4x32 slice. The times are simulated.
1024 devices in a mesh: dp: 128 (over z, y), expert: 8 (over x, core).
Axes of the slice: x: 4, y: 4, z: 32, core: 2. Of those that a mesh axis runs over, the one named last changes fastest.
Arguments:
- tokens: bfloat16 [131072, 1024], P(('dp', 'expert')), may hold values from -6 to 6
- expert_ids: int32 [131072, 2], P(('dp', 'expert')), may hold values from 0 to 7, all different within a row; in each aligned block of 128 rows (0 to 127, 128 to 255, ...) at most 48 rows name the same one
- combine: float32 [131072, 2], P(('dp', 'expert')), may hold values from 0.2 to 1
- w_gate: bfloat16 [8, 1024, 768], P('expert', 'dp'), may hold values from -0.1875 to 0.1875
- w_up: bfloat16 [8, 1024, 768], P('expert', 'dp'), may hold values from -0.1875 to 0.1875
- w_down: bfloat16 [8, 1024, 768], P('expert', 'dp'), may hold values from -0.21875 to 0.21875
- cotangent: bfloat16 [131072, 1024], P(('dp', 'expert')), may hold values from -6 to 6
Outputs:
- mixed: bfloat16 [131072, 1024], P(('dp', 'expert'))
- input_grad: bfloat16 [131072, 1024], P(('dp', 'expert'))
- combine_grad: float32 [131072, 2], P(('dp', 'expert'))
Inputs may be any that keep to these rules, and one draw needn't show every extreme that they name: `expert_ids`: among the rows of one device (128 tokens) no expert is named more than 48 times, and in every draw some expert is named exactly 48 times by the rows of some device; a token names 2 different experts.
All inputs are finite; a program needn't handle non-finite values.
Results may differ from a plain program's by a relative error of at most 0.0065.
Values may be sent and summed in bfloat16 or wider, within the bound.
No kernel may reach another device: no remote copies, remote signals or barrier semaphores. Data moves between devices by JAX's collectives and lax.ppermute only.
A program may use at most 32 MiB of HBM per device.

v0:
```python
import jax
import jax.numpy as jnp
from jax import lax
from jax.sharding import PartitionSpec as P


def place_rows(expert_ids, experts, capacity):
    flat_ids = expert_ids.reshape(-1)
    onehot = (flat_ids[:, None] == jnp.arange(experts, dtype=jnp.int32)[None, :]).astype(jnp.int32)
    before = jnp.cumsum(onehot, axis=0) - onehot
    ranks = jnp.sum(before * onehot, axis=1)
    return flat_ids * capacity + ranks


def expert_forward(arrived, gate_w, up_w, down_w):
    gate = jnp.einsum("shcd,hdf->shcf", arrived, gate_w, preferred_element_type=jnp.float32)
    up = jnp.einsum("shcd,hdf->shcf", arrived, up_w, preferred_element_type=jnp.float32)
    hidden = (jax.nn.silu(gate) * up).astype(jnp.bfloat16)
    out_rows = jnp.einsum("shcf,hdf->shcd", hidden, down_w, preferred_element_type=jnp.float32)
    return (out_rows.astype(jnp.bfloat16), gate, up)


def expert_backward(arrived_grads, gate, up, gate_w, up_w, down_w):
    hidden_grad = jnp.einsum(
        "shcd,hdf->shcf", arrived_grads, down_w, preferred_element_type=jnp.float32
    )
    sigma = jax.nn.sigmoid(gate)
    gate_grad = (hidden_grad * up * sigma * (1.0 + gate * (1.0 - sigma))).astype(jnp.bfloat16)
    up_grad = (hidden_grad * gate * sigma).astype(jnp.bfloat16)
    row_grad = jnp.einsum("shcf,hdf->shcd", gate_grad, gate_w, preferred_element_type=jnp.float32)
    row_grad = row_grad + jnp.einsum(
        "shcf,hdf->shcd", up_grad, up_w, preferred_element_type=jnp.float32
    )
    return row_grad.astype(jnp.bfloat16)


def on_device(tokens, expert_ids, combine, w_gate, w_up, w_down, cotangent):
    groups = lax.axis_size("expert")
    held_count = w_gate.shape[0]
    experts = groups * held_count
    rows_tok, top_count = expert_ids.shape
    width = tokens.shape[1]
    capacity = 3 * rows_tok * top_count // (2 * experts)
    slot_index = place_rows(expert_ids, experts, capacity)
    token_copies = jnp.repeat(tokens, top_count, axis=0)
    scaled = (combine[:, :, None] * cotangent.astype(jnp.float32)[:, None, :]).astype(jnp.bfloat16)
    scaled = scaled.reshape(rows_tok * top_count, width)

    def pack(values):
        buffer = jnp.zeros((experts * capacity, width), jnp.bfloat16).at[slot_index].set(values)
        return buffer.reshape(groups, held_count, capacity, width)

    def unpack(values):
        return values.reshape(experts * capacity, width)[slot_index].reshape(
            rows_tok, top_count, width
        )

    sent_tokens = pack(token_copies)
    sent_grads = pack(scaled)
    full_gate, full_up, full_down = (
        lax.all_gather(w_gate, "dp", axis=1, tiled=True),
        lax.all_gather(w_up, "dp", axis=1, tiled=True),
        lax.all_gather(w_down, "dp", axis=1, tiled=True),
    )
    arrived = lax.all_to_all(sent_tokens, "expert", split_axis=0, concat_axis=0, tiled=True)
    out_rows, gate, up = expert_forward(arrived, full_gate, full_up, full_down)
    back_out = lax.all_to_all(out_rows, "expert", split_axis=0, concat_axis=0, tiled=True)
    arrived_grads = lax.all_to_all(sent_grads, "expert", split_axis=0, concat_axis=0, tiled=True)
    grad_rows = expert_backward(arrived_grads, gate, up, full_gate, full_up, full_down)
    back_grad = lax.all_to_all(grad_rows, "expert", split_axis=0, concat_axis=0, tiled=True)
    expert_out = unpack(back_out).astype(jnp.float32)
    row_grad = unpack(back_grad).astype(jnp.float32)
    mixed = jnp.sum(combine[:, :, None] * expert_out, axis=1).astype(jnp.bfloat16)
    combine_grad = jnp.sum(cotangent.astype(jnp.float32)[:, None, :] * expert_out, axis=2)
    input_grad = jnp.sum(row_grad, axis=1).astype(jnp.bfloat16)
    return (mixed, input_grad, combine_grad)


def solution(mesh):
    in_specs = (
        P(("dp", "expert"), None),
        P(("dp", "expert"), None),
        P(("dp", "expert"), None),
        P("expert", "dp", None),
        P("expert", "dp", None),
        P("expert", "dp", None),
        P(("dp", "expert"), None),
    )
    out_specs = (P(("dp", "expert"), None), P(("dp", "expert"), None), P(("dp", "expert"), None))
    return jax.shard_map(
        on_device, mesh=mesh, in_specs=in_specs, out_specs=out_specs, check_vma=False
    )
```

profile of v0, /device:TPU:1, one launch (start us, length us, event | category | flops | bytes accessed | tf_op | source)
XLA Modules:
  0.0 857.2 jit_solution(4367008588843652384)
XLA Ops:
  7.2 0.7 all-gather.6.cloned.1.call-update
  7.9 0.7 all-gather.4.cloned.1.call-update
  8.7 0.7 all-gather.8.cloned.1.call-update
  9.4 0.8 copy.18
  10.5 0.7 broadcast_multiply_fusion
  12.2 1.2 broadcast_in_dim.2
  13.8 2.6 scatter_custom_fusion
  16.4 17.6 %all-to-all-start = ((bf16[8,1,48,1024]{3,2,1,0:T(8,128)(2,1)}), bf16[8,1,48,1024]{3,2,1,0:T(8,128)(2,1)S(1)}, u32[]{:S(2)}, u32[]{:S(2)}) async-start(bf16[8,1,48,1024]{3,2,1,0:T(8,128)(2,1)} %bitcast.4), calls=%async_computation | async-start | bytes 1572864 | tf_op jit(solution)/shard_map/all_to_all | solution.py:65
  34.4 0.7 mul.91
  35.3 2.7 scatter_custom_fusion.1
  38.0 8.3 all-to-all-done
  46.3 4.3 all-to-all-start.2
  50.6 216.0 %all-gather.6.cloned.1.call-done = bf16[1,1024,768]{2,1,0:T(8,128)(2,1)} async-done(((bf16[1,8,768]{2,1,0:T(8,128)(2,1)}), bf16[1,1024,768]{2,1,0:T(8,128)(2,1)}) %all-gather.6.cloned.1.call-update) | async-done | bytes 1572880 | tf_op jit(solution)/shard_map/all_gather | solution.py:62
  266.6 2.2 fusion.20
  268.8 258.0 %all-gather.4.cloned.1.call-done = bf16[1,1024,768]{2,1,0:T(8,128)(2,1)} async-done(((bf16[1,8,768]{2,1,0:T(8,128)(2,1)}), bf16[1,1024,768]{2,1,0:T(8,128)(2,1)}) %all-gather.4.cloned.1.call-update) | async-done | bytes 1572880 | tf_op jit(solution)/shard_map/all_gather | solution.py:61
  526.8 3.2 fusion.17
  530.0 257.0 %all-gather.8.cloned.1.call-done = bf16[1,1024,768]{2,1,0:T(8,128)(2,1)} async-done(((bf16[1,8,768]{2,1,0:T(8,128)(2,1)}), bf16[1,1024,768]{2,1,0:T(8,128)(2,1)}) %all-gather.8.cloned.1.call-update) | async-done | bytes 1572880 | tf_op jit(solution)/shard_map/all_gather | solution.py:63
  787.0 3.5 fusion.26
  790.4 24.6 %all-to-all-start.1 = ((bf16[8,1,48,1024]{3,2,1,0:T(8,128)(2,1)}), bf16[8,1,48,1024]{3,2,1,0:T(8,128)(2,1)S(1)}, u32[]{:S(2)}, u32[]{:S(2)}) async-start(bf16[8,1,48,1024]{3,2,1,0:T(8,128)(2,1)} %fusion.26), calls=%async_computation.1 | async-start | bytes 1572864 | tf_op jit(solution)/shard_map/all_to_all | solution.py:67
  815.1 0.8 fusion.23
  816.8 0.9 fusion.4
  818.6 2.0 fusion.29
  820.6 6.8 all-to-all-done.1
  827.4 4.3 all-to-all-start.3
  831.7 0.8 convert_element_type.73
  832.5 1.2 gather_fusion
  833.7 0.7 reshape.140
  834.4 9.6 %all-to-all-done.3 = bf16[8,1,48,1024]{3,2,1,0:T(8,128)(2,1)S(1)} async-done(((bf16[8,1,48,1024]{3,2,1,0:T(8,128)(2,1)}), bf16[8,1,48,1024]{3,2,1,0:T(8,128)(2,1)S(1)}, u32[]{:S(2)}, u32[]{:S(2)}) %all-to-all-start.3) | async-done | bytes 786464 | tf_op jit(solution)/shard_map/all_to_all | solution.py:70
  844.0 1.2 gather_fusion.1
  845.4 2.1 reduce_sum.44
  847.5 2.6 multiply_reduce_fusion
  850.0 0.6 copy.23
  (39 shorter events, 4.4 us)
Async XLA Ops:
  7.2 259.5 %all-gather.6.cloned.1.call-start = ((), (), s32[]{:S(2)}) async-start(), calls=%async_computation.5 | async-start | bytes 1585152 | tf_op jit(solution)/shard_map/all_gather | solution.py:62
  7.9 518.9 %all-gather.4.cloned.1.call-start = ((), (), s32[]{:S(2)}) async-start(), calls=%async_computation.4 | async-start | bytes 1585152 | tf_op jit(solution)/shard_map/all_gather | solution.py:61
  8.6 778.3 %all-gather.8.cloned.1.call-start = ((), (), s32[]{:S(2)}) async-start(), calls=%async_computation.6 | async-start | bytes 1585152 | tf_op jit(solution)/shard_map/all_gather | solution.py:63
  13.8 20.2 %copy-start.2 = (f32[128,2]{0,1:T(2,128)S(1)}, f32[128,2]{0,1:T(2,128)}, u32[]{:S(2)}) copy-start(f32[128,2]{0,1:T(2,128)} %param.9) | copy-start | bytes 3076
  13.8 20.3 %copy-start.1 = (bf16[128,1024]{1,0:T(8,128)(2,1)S(1)}, bf16[128,1024]{1,0:T(8,128)(2,1)}, u32[]{:S(2)}) copy-start(bf16[128,1024]{1,0:T(8,128)(2,1)} %param.13) | copy-start | bytes 786436
  16.4 29.9 %all-to-all-start = ((bf16[8,1,48,1024]{3,2,1,0:T(8,128)(2,1)}), bf16[8,1,48,1024]{3,2,1,0:T(8,128)(2,1)S(1)}, u32[]{:S(2)}, u32[]{:S(2)}) async-start(bf16[8,1,48,1024]{3,2,1,0:T(8,128)(2,1)} %bitcast.4), calls=%async_computation | async-start | bytes 1572864 | tf_op jit(solution)/shard_map/all_to_all | solution.py:65
  46.3 744.1 %all-to-all-start.2 = ((bf16[8,1,48,1024]{3,2,1,0:T(8,128)(2,1)}), bf16[8,1,48,1024]{3,2,1,0:T(8,128)(2,1)S(1)}, u32[]{:S(2)}, u32[]{:S(2)}) async-start(bf16[8,1,48,1024]{3,2,1,0:T(8,128)(2,1)} %bitcast.26), calls=%async_computation.2 | async-start | bytes 1572864 | tf_op jit(solution)/shard_map/all_to_all | solution.py:68
  268.8 518.1 %copy-start.6 = (f32[8,1,48,768]{3,2,0,1:T(8,128)}, f32[8,1,48,768]{3,2,0,1:T(8,128)S(1)}, u32[]{:S(2)}) copy-start(f32[8,1,48,768]{3,2,0,1:T(8,128)S(1)} %fusion.20) | copy-start | bytes 3538948
  790.4 24.6 %copy-start.5 = (bf16[1,1024,768]{2,1,0:T(8,128)(2,1)S(1)}, bf16[1,1024,768]{2,1,0:T(8,128)(2,1)}, u32[]{:S(2)}) copy-start(bf16[1,1024,768]{2,1,0:T(8,128)(2,1)} %all-gather.8.cloned.1.call-done) | copy-start | bytes 4718596
  790.4 36.9 %all-to-all-start.1 = ((bf16[8,1,48,1024]{3,2,1,0:T(8,128)(2,1)}), bf16[8,1,48,1024]{3,2,1,0:T(8,128)(2,1)S(1)}, u32[]{:S(2)}, u32[]{:S(2)}) async-start(bf16[8,1,48,1024]{3,2,1,0:T(8,128)(2,1)} %fusion.26), calls=%async_computation.1 | async-start | bytes 1572864 | tf_op jit(solution)/shard_map/all_to_all | solution.py:67
  815.1 1.4 copy-start.3
  815.1 1.7 copy-start.8
  816.8 1.4 copy-start.4
  816.8 1.7 copy-start.7
  827.4 16.6 %all-to-all-start.3 = ((bf16[8,1,48,1024]{3,2,1,0:T(8,128)(2,1)}), bf16[8,1,48,1024]{3,2,1,0:T(8,128)(2,1)S(1)}, u32[]{:S(2)}, u32[]{:S(2)}) async-start(bf16[8,1,48,1024]{3,2,1,0:T(8,128)(2,1)} %fusion.29), calls=%async_computation.3 | async-start | bytes 1572864 | tf_op jit(solution)/shard_map/all_to_all | solution.py:70
  845.2 2.3 copy-start
Sparse Core Ops, SparseCore 0:
  12.1 254.4 all-gather.5
  270.7 255.9 all-gather.3
  530.9 255.9 all-gather.7
where the time goes:
time: 858 us; the launch traced here: 857 us
  waiting for transfers between devices  758 us (88%)
  starting transfers between devices  51 us (6%)
  between operations  13.9 us (2%)
  local copies, waits for them, and re-layouts  12.5 us (1%)
  matrix products  12.5 us (1%)
  other arithmetic  9.64 us (1%)
    all_gather x1, waiting for transfers between devices, on_device(): lax.all_gather(w_gate, 'dp', axis=1, tiled=True)  258 us
    all_gather x1, waiting for transfers between devices, on_device(): lax.all_gather(w_down, 'dp', axis=1, tiled=True)  257 us
    all_gather x1, waiting for transfers between devices, on_device(): lax.all_gather(w_up, 'dp', axis=1, tiled=True)  216 us
    all_to_all x1, starting transfers between devices, on_device(): lax.all_to_all(out_rows, 'expert', split_axis=0, concat_axis=0, tiled=True)  24.6 us
    all_to_all x1, starting transfers between devices, on_device(): lax.all_to_all(sent_tokens, 'expert', split_axis=0, concat_axis=0, tiled=...  17.6 us
  transfers between devices with their start and end apart: 7, of which 6 were waited for; matrix products, arithmetic and copies ran while one was open for 3% of the time, Pallas kernels for 0%

commit v1 on v0

v1 whole, which is shorter than its diff:
```python
import jax
import jax.numpy as jnp
from jax import lax
from jax.experimental import pallas as pl
from jax.experimental.pallas import tpu as pltpu
from jax.sharding import PartitionSpec as P

F32 = jnp.float32
BF16 = jnp.bfloat16
ALL = ("dp", "expert")
NY, CORES, PAR = 4, 2, 2


def call(body, name, out_shape, *args, mib=16):
    spec = pl.BlockSpec(memory_space=pltpu.VMEM)
    many = isinstance(out_shape, tuple)
    return pl.pallas_call(
        body,
        out_shape=out_shape,
        in_specs=[spec] * len(args),
        out_specs=(spec,) * len(out_shape) if many else spec,
        compiler_params=pltpu.CompilerParams(vmem_limit_bytes=mib * 1024 * 1024),
        name=name,
    )(*args)


def nt(left, right):
    return lax.dot_general(left, right, (((1,), (1,)), ((), ())), preferred_element_type=F32)


def nn(left, right):
    return jnp.dot(left, right, preferred_element_type=F32)


def pack_kernel(experts, ids_ref, comb_ref, tok_ref, cot_ref, sent_ref, grad_ref, pick_ref, ccol_ref):
    top, rows = ids_ref.shape
    slots = sent_ref.shape[0]
    capacity = slots // experts
    ids = ids_ref[...]
    kinds = lax.broadcasted_iota(jnp.int32, (experts, rows), 0)
    named = jnp.zeros((experts, rows), F32)
    for k in range(top):
        named = named + jnp.where(ids[k : k + 1, :] == kinds, 1.0, 0.0)
    earlier = jnp.where(
        lax.broadcasted_iota(jnp.int32, (rows, rows), 0)
        < lax.broadcasted_iota(jnp.int32, (rows, rows), 1),
        1.0,
        0.0,
    )
    before = nn(named.astype(BF16), earlier.astype(BF16))
    place = before + kinds.astype(F32) * capacity
    slot_iota = lax.broadcasted_iota(jnp.int32, (slots, rows), 0).astype(F32)
    spread = jnp.zeros((slots, rows), F32)
    weight = jnp.zeros((slots, rows), F32)
    for k in range(top):
        slot = jnp.sum(jnp.where(ids[k : k + 1, :] == kinds, place, 0.0), axis=0, keepdims=True)
        hot = jnp.where(slot_iota == slot, 1.0, 0.0)
        spread = spread + hot
        weight = weight + hot * comb_ref[k : k + 1, :]
        pick_ref[k] = jnp.transpose(hot).astype(BF16)
    spread = spread.astype(BF16)
    sent_ref[...] = nn(spread, tok_ref[...]).astype(BF16)
    cot_rows = nn(spread, cot_ref[...])
    grad_ref[...] = (cot_rows * jnp.sum(weight, axis=1, keepdims=True)).astype(BF16)
    padded = jnp.concatenate([comb_ref[...], jnp.zeros((rows - top, rows), F32)], axis=0)
    ccol_ref[...] = jnp.transpose(padded)


def order_kernel(zs, order_ref):
    width = order_ref.shape[0]
    dp = lax.axis_index("dp")
    core = lax.rem(lax.axis_index("expert"), CORES)
    my_z, my_y = dp // NY, lax.rem(dp, NY)
    depth = width // (zs * NY)
    i = lax.broadcasted_iota(jnp.int32, (1, width), 1)
    r = lax.rem(i, depth)
    pos = lax.rem(i // depth, zs // PAR)
    step = i // (depth * zs)
    other = lax.rem(i // (depth * (zs // PAR)), PAR)
    zi = jnp.where(core == 0, pos, zs // PAR - 1 - pos)
    y = lax.rem(jnp.where(core == 0, my_y + NY - step, my_y + step), NY)
    z = zi * PAR + lax.rem(my_z + other, PAR)
    feature = (z * NY + y) * depth + r
    tile = 128

    def one(t, carry):
        d = lax.broadcasted_iota(jnp.int32, (tile, width), 0) + t * tile
        order_ref[pl.ds(pl.multiple_of(t * tile, tile), tile), :] = jnp.where(
            d == feature, 1.0, 0.0
        ).astype(BF16)
        return carry

    lax.fori_loop(0, width // tile, one, 0)


def turn_kernel(rows_ref, order_ref, out_ref):
    out_ref[...] = nn(rows_ref[...], order_ref[...]).astype(BF16)


def pieces_dot(rows_ref, pieces, columns):
    start, total = 0, None
    for piece in pieces:
        size = piece.shape[0]
        part = nn(rows_ref[:, start : start + size], piece[:, columns])
        total = part if total is None else total + part
        start += size
    return total


def hidden_kernel(count, rows_ref, *refs):
    gates, ups = refs[:count], refs[count : 2 * count]
    hidden_ref, to_gate_ref, to_up_ref = refs[2 * count :]
    tile = 256
    for t in range(hidden_ref.shape[1] // tile):
        columns = slice(t * tile, (t + 1) * tile)
        gate = pieces_dot(rows_ref, gates, columns)
        up = pieces_dot(rows_ref, ups, columns)
        sigma = 1.0 / (1.0 + jnp.exp(-gate))
        silu = gate * sigma
        hidden_ref[:, columns] = (silu * up).astype(BF16)
        to_up_ref[:, columns] = silu
        to_gate_ref[:, columns] = up * sigma * (1.0 + gate * (1.0 - sigma))


def out_kernel(count, hidden_ref, order_ref, *refs):
    downs, out_ref, held_ref = refs[:count], refs[count], refs[count + 1]
    start = 0
    for piece in downs:
        size = piece.shape[0]
        held_ref[:, start : start + size] = nt(hidden_ref[...], piece[...]).astype(BF16)
        start += size
    out_ref[...] = nt(held_ref[...], order_ref[...]).astype(BF16)


def rows_kernel(count, grads_ref, to_gate_ref, to_up_ref, order_ref, *refs):
    gates, ups, downs = refs[:count], refs[count : 2 * count], refs[2 * count : 3 * count]
    out_ref, gate_grad_ref, up_grad_ref, held_ref = refs[3 * count :]
    tile = 256
    for t in range(to_up_ref.shape[1] // tile):
        columns = slice(t * tile, (t + 1) * tile)
        hidden_grad = pieces_dot(grads_ref, downs, columns)
        gate_grad_ref[:, columns] = (hidden_grad * to_gate_ref[:, columns]).astype(BF16)
        up_grad_ref[:, columns] = (hidden_grad * to_up_ref[:, columns]).astype(BF16)
    start = 0
    for gate, up in zip(gates, ups):
        size = gate.shape[0]
        total = nt(gate_grad_ref[...], gate[...]) + nt(up_grad_ref[...], up[...])
        held_ref[:, start : start + size] = total.astype(BF16)
        start += size
    out_ref[...] = nt(held_ref[...], order_ref[...]).astype(BF16)


def mixed_kernel(pick_ref, ccol_ref, cot_ref, back_ref, mixed_ref, cgrad_ref):
    top, rows, _ = pick_ref.shape
    cot = cot_ref[...].astype(F32)
    back = back_ref[...]
    lane = lax.broadcasted_iota(jnp.int32, (rows, rows), 1)
    mixed = jnp.zeros(cot.shape, F32)
    grads = jnp.zeros((rows, rows), F32)
    for k in range(top):
        out = nn(pick_ref[k], back)
        mixed = mixed + ccol_ref[:, k : k + 1] * out
        grads = jnp.where(lane == k, jnp.sum(cot * out, axis=1, keepdims=True), grads)
    mixed_ref[...] = mixed.astype(BF16)
    cgrad_ref[...] = jnp.transpose(grads)[:top, :]


def sum_kernel(pick_ref, back_ref, grad_ref):
    both = pick_ref[0]
    for k in range(1, pick_ref.shape[0]):
        both = both + pick_ref[k]
    grad_ref[...] = nn(both, back_ref[...]).astype(BF16)


def on_device(tokens, expert_ids, combine, w_gate, w_up, w_down, cotangent):
    groups = lax.axis_size("expert")
    zs = lax.axis_size("dp") // NY
    rows, top = expert_ids.shape
    width = tokens.shape[1]
    ff = w_gate.shape[2]
    capacity = 3 * rows * top // (2 * groups)
    slots = groups * capacity
    shape = jax.ShapeDtypeStruct

    def device(z, y, e):
        return ((z % zs) * NY + y % NY) * groups + e

    def shifted(dz, dy):
        return [
            (device(z, y, e), device(z + s * dz, y + s * dy, e))
            for z in range(zs)
            for y in range(NY)
            for e in range(groups)
            for s in ((1, -1)[e % CORES],)
        ]

    far_groups = [
        [device(z, y, e) for z in range(par, zs, PAR)][:: (1, -1)[e % CORES]]
        for par in range(PAR)
        for y in range(NY)
        for e in range(groups)
    ]
    near_perm, y_perm = shifted(1, 0), shifted(0, 1)

    def swap(values):
        split = values.reshape(groups, capacity, width)
        return lax.all_to_all(split, "expert", 0, 0, tiled=True).reshape(slots, width)

    joined = jnp.concatenate([w_gate[0], w_up[0], w_down[0]], axis=1)
    far = lax.all_gather(joined, ALL, axis=0, tiled=True, axis_index_groups=far_groups)
    sent_tokens, sent_grads, pick, ccol = call(
        lambda *refs: pack_kernel(groups, *refs),
        "pack",
        (
            shape((slots, width), BF16),
            shape((slots, width), BF16),
            shape((top, rows, slots), BF16),
            shape((rows, rows), F32),
        ),
        expert_ids.T,
        combine.T,
        tokens,
        cotangent,
    )
    order = call(lambda ref: order_kernel(zs, ref), "order", shape((width, width), BF16))
    arrived = swap(sent_tokens)
    arrived_grads = swap(sent_grads)
    kept = [far[:, m * ff : (m + 1) * ff] for m in range(3)]
    near = [lax.ppermute(k, ALL, near_perm) for k in kept]
    pieces = [[jnp.concatenate([k, n], axis=0)] for k, n in zip(kept, near)]
    for _ in range(NY - 1):
        for held in pieces:
            held.append(lax.ppermute(held[-1], ALL, y_perm))
    gates, ups, downs = pieces
    count = len(gates)
    turned = call(turn_kernel, "turn", shape((slots, width), BF16), arrived, order)
    turned_grads = call(turn_kernel, "turn", shape((slots, width), BF16), arrived_grads, order)
    hidden, to_gate, to_up = call(
        lambda *refs: hidden_kernel(count, *refs),
        "hidden",
        (shape((slots, ff), BF16), shape((slots, ff), F32), shape((slots, ff), F32)),
        turned,
        *gates,
        *ups,
        mib=20,
    )
    spec = pl.BlockSpec(memory_space=pltpu.VMEM)
    out_rows = pl.pallas_call(
        lambda *refs: out_kernel(count, *refs),
        out_shape=shape((slots, width), BF16),
        in_specs=[spec] * (2 + count),
        out_specs=spec,
        scratch_shapes=[pltpu.VMEM((slots, width), BF16)],
        compiler_params=pltpu.CompilerParams(vmem_limit_bytes=16 * 1024 * 1024),
        name="out_rows",
    )(hidden, order, *downs)
    back_out = swap(out_rows)
    row_grads = pl.pallas_call(
        lambda *refs: rows_kernel(count, *refs),
        out_shape=shape((slots, width), BF16),
        in_specs=[spec] * (4 + 3 * count),
        out_specs=spec,
        scratch_shapes=[
            pltpu.VMEM((slots, ff), BF16),
            pltpu.VMEM((slots, ff), BF16),
            pltpu.VMEM((slots, width), BF16),
        ],
        compiler_params=pltpu.CompilerParams(vmem_limit_bytes=24 * 1024 * 1024),
        name="row_grads",
    )(turned_grads, to_gate, to_up, order, *gates, *ups, *downs)
    back_grad = swap(row_grads)
    mixed, combine_grad = call(
        mixed_kernel,
        "mixed",
        (shape((rows, width), BF16), shape((top, rows), F32)),
        pick,
        ccol,
        cotangent,
        back_out,
    )
    input_grad = call(sum_kernel, "summed", shape((rows, width), BF16), pick, back_grad)
    return mixed, input_grad, combine_grad.T


def solution(mesh):
    rows = P(ALL, None)
    weights = P("expert", "dp", None)
    return jax.shard_map(
        on_device,
        mesh=mesh,
        in_specs=(rows, rows, rows, weights, weights, weights, rows),
        out_specs=(rows, rows, rows),
        check_vma=False,
    )
```

time: 858 us -> 160 us (0.19)
  waiting for transfers between devices: 758 us -> 19 us
  blocking collectives: 0 us -> 44.9 us
  Pallas kernels: 0 us -> 18.4 us
  starting transfers between devices: 51 us -> 65.5 us
  between operations: 13.9 us -> 1.05 us
  matrix products: 12.5 us -> 0 us
  other arithmetic: 9.64 us -> 0.88 us
    all_gather x3 -> x0, waiting for transfers between devices: 731 us -> none  [the longest x1 258 us: on_device(): lax.all_gather(w_gate, 'dp', axis=1, tiled=True)]
    all_gather x0 -> x1, blocking collectives: none -> 44.9 us  [on_device(): lax.all_gather(joined, ALL, axis=0, tiled=True, axis_index_groups=far_gro...]
    ppermute x0 -> x12, starting transfers between devices: none -> 40 us  [the longest x9 30.1 us: on_device(): held.append(lax.ppermute(held[-1], ALL, y_perm))]
    all_to_all x4, starting transfers between devices: 50.9 us -> 25.5 us  [swap(): lax.all_to_all(split, 'expert', 0, 0, tiled=True).reshape(slots, width)]
    pallas_call x0 -> x9, Pallas kernels: none -> 18.4 us  [the longest x7 10.4 us: call(): pl.pallas_call(body, out_shape=out_shape, in_specs=[spec] * len(args), ou...]
    dot_general x6 -> x0, matrix products: 12.5 us -> none  [the longest x1 3.49 us: expert_forward(): jnp.einsum('shcf,hdf->shcd', hidden, down_w, preferred_element_type=jnp.f...]
  transfers between devices with their start and end apart: 7 -> 16, of which waited for: 6 -> 4; matrix products, arithmetic and copies ran while one was open for 3% -> 0% of each run, Pallas kernels for 0% -> 8%
where the time goes in v1:
time: 160 us; the launch traced here: 158 us
  starting transfers between devices  65.5 us (41%)
  blocking collectives  44.9 us (28%)
  waiting for transfers between devices  19 us (12%)
  Pallas kernels  18.4 us (11%)
  local copies, waits for them, and re-layouts  8.37 us (5%)
    all_gather x1, blocking collectives, on_device(): lax.all_gather(joined, ALL, axis=0, tiled=True, axis_index_groups=far_gro...  44.9 us
    ppermute x9, starting transfers between devices, on_device(): held.append(lax.ppermute(held[-1], ALL, y_perm))  30.1 us
    all_to_all x4, starting transfers between devices, swap(): lax.all_to_all(split, 'expert', 0, 0, tiled=True).reshape(slots, width)  25.5 us
    all_to_all x4, waiting for transfers between devices, swap(): lax.all_to_all(split, 'expert', 0, 0, tiled=True).reshape(slots, width)  18.8 us
    pallas_call x7, Pallas kernels, call(): pl.pallas_call(body, out_shape=out_shape, in_specs=[spec] * len(args), ou...  10.4 us
    ppermute x3, starting transfers between devices, on_device(): near = [lax.ppermute(k, ALL, near_perm) for k in kept]  9.84 us
    unnamed x46, local copies, waits for them, and re-layouts  8.33 us
    pallas_call x1, Pallas kernels, on_device(): pl.pallas_call(lambda *refs: rows_kernel(count, *refs), out_shape=shape((...  4.39 us
  transfers between devices with their start and end apart: 16, of which 4 were waited for; matrix products, arithmetic and copies ran while one was open for 0% of the time, Pallas kernels for 8%

profile of v1, /device:TPU:1, one launch (start us, length us, event | category | flops | bytes accessed | tf_op | source)
XLA Modules:
  0.0 158.1 jit_solution(18137799510250066538)
XLA Ops:
  1.5 44.9 %all_gather.3 = bf16[128,2304]{1,0:T(8,128)(2,1)S(1)} all-gather(bf16[8,2304]{1,0:T(8,128)(2,1)S(1)} %pad_maximum_fusion.3), channel_id=1, replica_groups={{0,64,128,192,256,320,384,448,512,576,640,704,768,832,896,960},{961,897..., dimensions={0}, use_global_device_ids=true | all-gather | bytes 626688 | tf_op jit(solution)/shard_map/all_gather | solution.py:210
  46.4 3.7 %collective-permute-start = (bf16[128,768]{1,0:T(8,128)(2,1)S(1)}, bf16[128,768]{1,0:T(8,128)(2,1)S(1)}, u32[]{:S(2)}, u32[]{:S(2)}) collective-permute-start(bf16[128,768]{1,0:T(8,128)(2,1)S(1)} %get-tuple-element.23), channel_id=1, source_target_pairs={{0,32},{1,993},{2,34},{3,995},{4,36},{5,997},{6,38},{7,999},{8,40}... | collective-permute-start | bytes 589832 | tf_op jit(solution)/shard_map/ppermute | solution.py:229
  50.1 3.5 %collective-permute-start.4 = (bf16[128,768]{1,0:T(8,128)(2,1)S(1)}, bf16[128,768]{1,0:T(8,128)(2,1)S(1)}, u32[]{:S(2)}, u32[]{:S(2)}) collective-permute-start(bf16[128,768]{1,0:T(8,128)(2,1)S(1)} %get-tuple-element.22), channel_id=1, source_target_pairs={{0,32},{1,993},{2,34},{3,995},{4,36},{5,997},{6,38},{7,999},{8,40}... | collective-permute-start | bytes 589832 | tf_op jit(solution)/shard_map/ppermute | solution.py:229
  53.6 2.7 %collective-permute-start.8 = (bf16[128,768]{1,0:T(8,128)(2,1)S(1)}, bf16[128,768]{1,0:T(8,128)(2,1)S(1)}, u32[]{:S(2)}, u32[]{:S(2)}) collective-permute-start(bf16[128,768]{1,0:T(8,128)(2,1)S(1)} %get-tuple-element.21), channel_id=1, source_target_pairs={{0,32},{1,993},{2,34},{3,995},{4,36},{5,997},{6,38},{7,999},{8,40}... | collective-permute-start | bytes 589832 | tf_op jit(solution)/shard_map/ppermute | solution.py:229
  56.3 1.6 %pack.1 = (bf16[384,1024]{1,0:T(8,128)(2,1)S(1)}, bf16[384,1024]{1,0:T(8,128)(2,1)}, bf16[2,128,384]{2,1,0:T(8,128)(2,1)S(1)}, f32[128,128]{1,0:T(8,128)S(1)}) custom-call(s32[2,128]{1,0:T(2,128)S(1)} %bitcast.19, f32[2,128]{1,0:T(2,128)S(1)} %bitcast.20, bf16[128,1024]{1,0:T(8,128)(2,1)S(1)} %copy-done.18, bf16[128,1024]{1,0:T(8,128)(2,1)S(1)} %copy-done.12), custom_call_target="tpu_custom_call" | custom-call | tf_op jit(solution)/shard_map/pack/pallas_call | solution.py:17
  58.5 0.9 copy-done.15
  60.1 10.6 %all-to-all-start.2 = ((bf16[8,48,1024]{2,1,0:T(8,128)(2,1)}), bf16[8,48,1024]{2,1,0:T(8,128)(2,1)S(1)}, u32[]{:S(2)}, u32[]{:S(2)}) async-start(bf16[8,48,1024]{2,1,0:T(8,128)(2,1)} %bitcast.9), calls=%async_computation.2 | async-start | bytes 1572864 | tf_op jit(solution)/shard_map/all_to_all | solution.py:207
  70.7 4.7 %collective-permute-start.1 = (bf16[256,768]{1,0:T(8,128)(2,1)S(1)}, bf16[256,768]{1,0:T(8,128)(2,1)S(1)}, u32[]{:S(2)}, u32[]{:S(2)}) collective-permute-start(bf16[256,768]{1,0:T(8,128)(2,1)S(1)} %pad_maximum_fusion.refs_1_.refs_4_), channel_id=1, source_target_pairs={{0,8},{1,25},{2,10},{3,27},{4,12},{5,29},{6,14},{7,31},{8,16},{9,1... | collective-permute-start | bytes 1179656 | tf_op jit(solution)/shard_map/ppermute | solution.py:233
  75.4 2.4 %collective-permute-start.5 = (bf16[256,768]{1,0:T(8,128)(2,1)S(1)}, bf16[256,768]{1,0:T(8,128)(2,1)S(1)}, u32[]{:S(2)}, u32[]{:S(2)}) collective-permute-start(bf16[256,768]{1,0:T(8,128)(2,1)S(1)} %pad_maximum_fusion.1.refs_5_.refs_8_), channel_id=1, source_target_pairs={{0,8},{1,25},{2,10},{3,27},{4,12},{5,29},{6,14},{7,31},{8,16},{9,1... | collective-permute-start | bytes 1179656 | tf_op jit(solution)/shard_map/ppermute | solution.py:233
  77.8 2.1 %collective-permute-start.9 = (bf16[256,768]{1,0:T(8,128)(2,1)S(1)}, bf16[256,768]{1,0:T(8,128)(2,1)S(1)}, u32[]{:S(2)}, u32[]{:S(2)}) collective-permute-start(bf16[256,768]{1,0:T(8,128)(2,1)S(1)} %pad_maximum_fusion.2.refs_2_.refs_12_), channel_id=1, source_target_pairs={{0,8},{1,25},{2,10},{3,27},{4,12},{5,29},{6,14},{7,31},{8,16},{9,1... | collective-permute-start | bytes 1179656 | tf_op jit(solution)/shard_map/ppermute | solution.py:233
  80.0 5.0 %collective-permute-start.2 = (bf16[256,768]{1,0:T(8,128)(2,1)S(1)}, bf16[256,768]{1,0:T(8,128)(2,1)}, u32[]{:S(2)}, u32[]{:S(2)}) collective-permute-start(bf16[256,768]{1,0:T(8,128)(2,1)S(1)} %collective-permute-done.1.refs_2_.refs_5_), channel_id=1, source_target_pairs={{0,8},{1,25},{2,10},{3,27},{4,12},{5,29},{6,14},{7,31},{8,16},{9,1... | collective-permute-start | bytes 1179656 | tf_op jit(solution)/shard_map/ppermute | solution.py:233
  85.1 4.2 %collective-permute-start.6 = (bf16[256,768]{1,0:T(8,128)(2,1)S(1)}, bf16[256,768]{1,0:T(8,128)(2,1)}, u32[]{:S(2)}, u32[]{:S(2)}) collective-permute-start(bf16[256,768]{1,0:T(8,128)(2,1)S(1)} %collective-permute-done.5.refs_6_.refs_9_), channel_id=1, source_target_pairs={{0,8},{1,25},{2,10},{3,27},{4,12},{5,29},{6,14},{7,31},{8,16},{9,1... | collective-permute-start | bytes 1179656 | tf_op jit(solution)/shard_map/ppermute | solution.py:233
  90.0 3.4 %collective-permute-start.10 = (bf16[256,768]{1,0:T(8,128)(2,1)S(1)}, bf16[256,768]{1,0:T(8,128)(2,1)}, u32[]{:S(2)}, u32[]{:S(2)}) collective-permute-start(bf16[256,768]{1,0:T(8,128)(2,1)S(1)} %collective-permute-done.9.refs_3_.refs_13_), channel_id=1, source_target_pairs={{0,8},{1,25},{2,10},{3,27},{4,12},{5,29},{6,14},{7,31},{8,16},{9,1... | collective-permute-start | bytes 1179656 | tf_op jit(solution)/shard_map/ppermute | solution.py:233
  93.5 4.6 %all-to-all-start = ((bf16[8,48,1024]{2,1,0:T(8,128)(2,1)}), bf16[8,48,1024]{2,1,0:T(8,128)(2,1)}, u32[]{:S(2)}, u32[]{:S(2)}) async-start(bf16[8,48,1024]{2,1,0:T(8,128)(2,1)} %bitcast.18), calls=%async_computation | async-start | bytes 1572864 | tf_op jit(solution)/shard_map/all_to_all | solution.py:207
  98.1 3.5 %collective-permute-start.3 = (bf16[256,768]{1,0:T(8,128)(2,1)}, bf16[256,768]{1,0:T(8,128)(2,1)}, u32[]{:S(2)}, u32[]{:S(2)}) collective-permute-start(bf16[256,768]{1,0:T(8,128)(2,1)} %collective-permute-done.2.refs_3_.refs_6_), channel_id=1, source_target_pairs={{0,8},{1,25},{2,10},{3,27},{4,12},{5,29},{6,14},{7,31},{8,16},{9,1... | collective-permute-start | bytes 1179656 | tf_op jit(solution)/shard_map/ppermute | solution.py:233
  101.6 2.2 %collective-permute-start.7 = (bf16[256,768]{1,0:T(8,128)(2,1)}, bf16[256,768]{1,0:T(8,128)(2,1)}, u32[]{:S(2)}, u32[]{:S(2)}) collective-permute-start(bf16[256,768]{1,0:T(8,128)(2,1)} %collective-permute-done.6.refs_7_.refs_10_), channel_id=1, source_target_pairs={{0,8},{1,25},{2,10},{3,27},{4,12},{5,29},{6,14},{7,31},{8,16},{9,1... | collective-permute-start | bytes 1179656 | tf_op jit(solution)/shard_map/ppermute | solution.py:233
  103.9 2.7 %collective-permute-start.11 = (bf16[256,768]{1,0:T(8,128)(2,1)}, bf16[256,768]{1,0:T(8,128)(2,1)}, u32[]{:S(2)}, u32[]{:S(2)}) collective-permute-start(bf16[256,768]{1,0:T(8,128)(2,1)} %collective-permute-done.10.refs_4_.refs_14_), channel_id=1, source_target_pairs={{0,8},{1,25},{2,10},{3,27},{4,12},{5,29},{6,14},{7,31},{8,16},{9,1... | collective-permute-start | bytes 1179656 | tf_op jit(solution)/shard_map/ppermute | solution.py:233
  107.7 1.0 turn.3.refs_0_
  108.7 0.9 copy-done.2
  109.5 0.9 all-to-all-done
  110.5 2.2 %turn.2.refs_0_ = bf16[384,1024]{1,0:T(8,128)(2,1)S(1)} custom-call(bf16[384,1024]{1,0:T(8,128)(2,1)} %bitcast.3.rows_ref, bf16[1024,1024]{1,0:T(8,128)(2,1)S(1)} %order.1.order_ref.refs_1_.refs_3_), custom_call_target="tpu_custom_call" | custom-call | tf_op jit(solution)/shard_map/turn/pallas_call | solution.py:17
  112.7 3.0 %hidden.1 = (bf16[384,768]{1,0:T(8,128)(2,1)S(1)}, f32[384,768]{1,0:T(8,128)S(1)}, f32[384,768]{1,0:T(8,128)S(1)}) custom-call(bf16[384,1024]{1,0:T(8,128)(2,1)S(1)} %turn.2.refs_0_, bf16[256,768]{1,0:T(8,128)(2,1)S(1)} %pad_maximum_fusion.refs_1_.refs_4_, bf16[256,768]{1,0:T(8,128)(2,1)S(1)} %copy-done.9, ...), custom_call_target="tpu_custom_call" | custom-call | tf_op jit(solution)/shard_map/hidden/pallas_call | solution.py:17
  116.5 4.4 %row_grads.1 = bf16[384,1024]{1,0:T(8,128)(2,1)S(1)} custom-call(bf16[384,1024]{1,0:T(8,128)(2,1)S(1)} %copy-done.3, f32[384,768]{1,0:T(8,128)S(1)} %get-tuple-element.18.refs_1_, f32[384,768]{1,0:T(8,128)S(1)} %get-tuple-element.19.refs_2_, bf16[1024,1024]{1,0:T(8,128)(2,1)S(1)} %order.1.order_ref.refs_1_.refs_3_, ...), custom_call_target="tpu_custom_call" | custom-call | tf_op jit(solution)/shard_map/row_grads/pallas_call | solution.py:258
  121.8 5.9 %all-to-all-start.3 = ((bf16[8,48,1024]{2,1,0:T(8,128)(2,1)}), bf16[8,48,1024]{2,1,0:T(8,128)(2,1)S(1)}, u32[]{:S(2)}, u32[]{:S(2)}) async-start(bf16[8,48,1024]{2,1,0:T(8,128)(2,1)} %bitcast.17), calls=%async_computation.3 | async-start | bytes 1572864 | tf_op jit(solution)/shard_map/all_to_all | solution.py:207
  127.8 1.0 copy-done.7
  128.8 1.1 copy-done.17
  129.8 3.6 %out_rows.1 = bf16[384,1024]{1,0:T(8,128)(2,1)} custom-call(bf16[384,768]{1,0:T(8,128)(2,1)S(1)} %copy-done.17, bf16[1024,1024]{1,0:T(8,128)(2,1)S(1)} %order.1.order_ref.refs_1_.refs_3_, bf16[256,768]{1,0:T(8,128)(2,1)S(1)} %pad_maximum_fusion.2.refs_2_.refs_12_, bf16[256,768]{1,0:T(8,128)(2,1)S(1)} %copy-done.7, ...), custom_call_target="tpu_custom_call" | custom-call | tf_op jit(solution)/shard_map/out_rows/pallas_call | solution.py:248
  133.4 6.6 %all-to-all-done.3 = bf16[8,48,1024]{2,1,0:T(8,128)(2,1)S(1)} async-done(((bf16[8,48,1024]{2,1,0:T(8,128)(2,1)}), bf16[8,48,1024]{2,1,0:T(8,128)(2,1)S(1)}, u32[]{:S(2)}, u32[]{:S(2)}) %all-to-all-start.3) | async-done | bytes 786464 | tf_op jit(solution)/shard_map/all_to_all | solution.py:207
  140.1 4.5 %all-to-all-start.1 = ((bf16[8,48,1024]{2,1,0:T(8,128)(2,1)}), bf16[8,48,1024]{2,1,0:T(8,128)(2,1)S(1)}, u32[]{:S(2)}, u32[]{:S(2)}) async-start(bf16[8,48,1024]{2,1,0:T(8,128)(2,1)} %bitcast.7), calls=%async_computation.1 | async-start | bytes 1572864 | tf_op jit(solution)/shard_map/all_to_all | solution.py:207
  144.5 1.0 summed.1
  145.5 11.3 %all-to-all-done.1 = bf16[8,48,1024]{2,1,0:T(8,128)(2,1)S(1)} async-done(((bf16[8,48,1024]{2,1,0:T(8,128)(2,1)}), bf16[8,48,1024]{2,1,0:T(8,128)(2,1)S(1)}, u32[]{:S(2)}, u32[]{:S(2)}) %all-to-all-start.1) | async-done | bytes 786464 | tf_op jit(solution)/shard_map/all_to_all | solution.py:207
  156.8 1.2 mixed.1
  (61 shorter events, 6.0 us)
Async XLA Ops:
  0.6 55.6 %copy-start.12 = (bf16[128,1024]{1,0:T(8,128)(2,1)S(1)}, bf16[128,1024]{1,0:T(8,128)(2,1)}, u32[]{:S(2)}) copy-start(bf16[128,1024]{1,0:T(8,128)(2,1)} %cot_ref.1) | copy-start | bytes 786436
  0.6 55.6 %copy-start.22 = (f32[128,2]{0,1:T(2,128)S(1)}, f32[128,2]{0,1:T(2,128)}, u32[]{:S(2)}) copy-start(f32[128,2]{0,1:T(2,128)} %param.9) | copy-start | bytes 3076
  0.7 55.6 %copy-start.21 = (s32[128,2]{0,1:T(2,128)S(1)}, s32[128,2]{0,1:T(2,128)}, u32[]{:S(2)}) copy-start(s32[128,2]{0,1:T(2,128)} %param.8) | copy-start | bytes 3076
  0.7 55.6 %copy-start.18 = (bf16[128,1024]{1,0:T(8,128)(2,1)S(1)}, bf16[128,1024]{1,0:T(8,128)(2,1)}, u32[]{:S(2)}) copy-start(bf16[128,1024]{1,0:T(8,128)(2,1)} %refs_2_.1) | copy-start | bytes 786436
  46.4 24.3 %collective-permute-start = (bf16[128,768]{1,0:T(8,128)(2,1)S(1)}, bf16[128,768]{1,0:T(8,128)(2,1)S(1)}, u32[]{:S(2)}, u32[]{:S(2)}) collective-permute-start(bf16[128,768]{1,0:T(8,128)(2,1)S(1)} %get-tuple-element.23), channel_id=1, source_target_pairs={{0,32},{1,993},{2,34},{3,995},{4,36},{5,997},{6,38},{7,999},{8,40}... | collective-permute-start | bytes 589832 | tf_op jit(solution)/shard_map/ppermute | solution.py:229
  50.1 25.2 %collective-permute-start.4 = (bf16[128,768]{1,0:T(8,128)(2,1)S(1)}, bf16[128,768]{1,0:T(8,128)(2,1)S(1)}, u32[]{:S(2)}, u32[]{:S(2)}) collective-permute-start(bf16[128,768]{1,0:T(8,128)(2,1)S(1)} %get-tuple-element.22), channel_id=1, source_target_pairs={{0,32},{1,993},{2,34},{3,995},{4,36},{5,997},{6,38},{7,999},{8,40}... | collective-permute-start | bytes 589832 | tf_op jit(solution)/shard_map/ppermute | solution.py:229
  53.6 24.2 %collective-permute-start.8 = (bf16[128,768]{1,0:T(8,128)(2,1)S(1)}, bf16[128,768]{1,0:T(8,128)(2,1)S(1)}, u32[]{:S(2)}, u32[]{:S(2)}) collective-permute-start(bf16[128,768]{1,0:T(8,128)(2,1)S(1)} %get-tuple-element.21), channel_id=1, source_target_pairs={{0,32},{1,993},{2,34},{3,995},{4,36},{5,997},{6,38},{7,999},{8,40}... | collective-permute-start | bytes 589832 | tf_op jit(solution)/shard_map/ppermute | solution.py:229
  60.1 33.4 %all-to-all-start.2 = ((bf16[8,48,1024]{2,1,0:T(8,128)(2,1)}), bf16[8,48,1024]{2,1,0:T(8,128)(2,1)S(1)}, u32[]{:S(2)}, u32[]{:S(2)}) async-start(bf16[8,48,1024]{2,1,0:T(8,128)(2,1)} %bitcast.9), calls=%async_computation.2 | async-start | bytes 1572864 | tf_op jit(solution)/shard_map/all_to_all | solution.py:207
  70.7 9.4 %collective-permute-start.1 = (bf16[256,768]{1,0:T(8,128)(2,1)S(1)}, bf16[256,768]{1,0:T(8,128)(2,1)S(1)}, u32[]{:S(2)}, u32[]{:S(2)}) collective-permute-start(bf16[256,768]{1,0:T(8,128)(2,1)S(1)} %pad_maximum_fusion.refs_1_.refs_4_), channel_id=1, source_target_pairs={{0,8},{1,25},{2,10},{3,27},{4,12},{5,29},{6,14},{7,31},{8,16},{9,1... | collective-permute-start | bytes 1179656 | tf_op jit(solution)/shard_map/ppermute | solution.py:233
  75.4 9.7 %collective-permute-start.5 = (bf16[256,768]{1,0:T(8,128)(2,1)S(1)}, bf16[256,768]{1,0:T(8,128)(2,1)S(1)}, u32[]{:S(2)}, u32[]{:S(2)}) collective-permute-start(bf16[256,768]{1,0:T(8,128)(2,1)S(1)} %pad_maximum_fusion.1.refs_5_.refs_8_), channel_id=1, source_target_pairs={{0,8},{1,25},{2,10},{3,27},{4,12},{5,29},{6,14},{7,31},{8,16},{9,1... | collective-permute-start | bytes 1179656 | tf_op jit(solution)/shard_map/ppermute | solution.py:233
  77.8 12.2 %collective-permute-start.9 = (bf16[256,768]{1,0:T(8,128)(2,1)S(1)}, bf16[256,768]{1,0:T(8,128)(2,1)S(1)}, u32[]{:S(2)}, u32[]{:S(2)}) collective-permute-start(bf16[256,768]{1,0:T(8,128)(2,1)S(1)} %pad_maximum_fusion.2.refs_2_.refs_12_), channel_id=1, source_target_pairs={{0,8},{1,25},{2,10},{3,27},{4,12},{5,29},{6,14},{7,31},{8,16},{9,1... | collective-permute-start | bytes 1179656 | tf_op jit(solution)/shard_map/ppermute | solution.py:233
  80.0 23.8 %copy-start.8 = (bf16[256,768]{1,0:T(8,128)(2,1)}, bf16[256,768]{1,0:T(8,128)(2,1)S(1)}, u32[]{:S(2)}) copy-start(bf16[256,768]{1,0:T(8,128)(2,1)S(1)} %collective-permute-done.1.refs_2_.refs_5_) | copy-start | bytes 1179652
  80.0 18.0 %collective-permute-start.2 = (bf16[256,768]{1,0:T(8,128)(2,1)S(1)}, bf16[256,768]{1,0:T(8,128)(2,1)}, u32[]{:S(2)}, u32[]{:S(2)}) collective-permute-start(bf16[256,768]{1,0:T(8,128)(2,1)S(1)} %collective-permute-done.1.refs_2_.refs_5_), channel_id=1, source_target_pairs={{0,8},{1,25},{2,10},{3,27},{4,12},{5,29},{6,14},{7,31},{8,16},{9,1... | collective-permute-start | bytes 1179656 | tf_op jit(solution)/shard_map/ppermute | solution.py:233
  85.1 16.5 %collective-permute-start.6 = (bf16[256,768]{1,0:T(8,128)(2,1)S(1)}, bf16[256,768]{1,0:T(8,128)(2,1)}, u32[]{:S(2)}, u32[]{:S(2)}) collective-permute-start(bf16[256,768]{1,0:T(8,128)(2,1)S(1)} %collective-permute-done.5.refs_6_.refs_9_), channel_id=1, source_target_pairs={{0,8},{1,25},{2,10},{3,27},{4,12},{5,29},{6,14},{7,31},{8,16},{9,1... | collective-permute-start | bytes 1179656 | tf_op jit(solution)/shard_map/ppermute | solution.py:233
  90.0 13.8 %copy-start.5 = (bf16[256,768]{1,0:T(8,128)(2,1)}, bf16[256,768]{1,0:T(8,128)(2,1)S(1)}, u32[]{:S(2)}) copy-start(bf16[256,768]{1,0:T(8,128)(2,1)S(1)} %collective-permute-done.9.refs_3_.refs_13_) | copy-start | bytes 1179652
  90.0 13.8 %collective-permute-start.10 = (bf16[256,768]{1,0:T(8,128)(2,1)S(1)}, bf16[256,768]{1,0:T(8,128)(2,1)}, u32[]{:S(2)}, u32[]{:S(2)}) collective-permute-start(bf16[256,768]{1,0:T(8,128)(2,1)S(1)} %collective-permute-done.9.refs_3_.refs_13_), channel_id=1, source_target_pairs={{0,8},{1,25},{2,10},{3,27},{4,12},{5,29},{6,14},{7,31},{8,16},{9,1... | collective-permute-start | bytes 1179656 | tf_op jit(solution)/shard_map/ppermute | solution.py:233
  93.5 10.4 %copy-start = (bf16[8,48,1024]{2,1,0:T(8,128)(2,1)}, bf16[8,48,1024]{2,1,0:T(8,128)(2,1)S(1)}, u32[]{:S(2)}) copy-start(bf16[8,48,1024]{2,1,0:T(8,128)(2,1)S(1)} %all-to-all-done.2) | copy-start | bytes 2359300
  93.5 17.0 %all-to-all-start = ((bf16[8,48,1024]{2,1,0:T(8,128)(2,1)}), bf16[8,48,1024]{2,1,0:T(8,128)(2,1)}, u32[]{:S(2)}, u32[]{:S(2)}) async-start(bf16[8,48,1024]{2,1,0:T(8,128)(2,1)} %bitcast.18), calls=%async_computation | async-start | bytes 1572864 | tf_op jit(solution)/shard_map/all_to_all | solution.py:207
  98.1 14.6 %collective-permute-start.3 = (bf16[256,768]{1,0:T(8,128)(2,1)}, bf16[256,768]{1,0:T(8,128)(2,1)}, u32[]{:S(2)}, u32[]{:S(2)}) collective-permute-start(bf16[256,768]{1,0:T(8,128)(2,1)} %collective-permute-done.2.refs_3_.refs_6_), channel_id=1, source_target_pairs={{0,8},{1,25},{2,10},{3,27},{4,12},{5,29},{6,14},{7,31},{8,16},{9,1... | collective-permute-start | bytes 1179656 | tf_op jit(solution)/shard_map/ppermute | solution.py:233
  101.6 11.1 %collective-permute-start.7 = (bf16[256,768]{1,0:T(8,128)(2,1)}, bf16[256,768]{1,0:T(8,128)(2,1)}, u32[]{:S(2)}, u32[]{:S(2)}) collective-permute-start(bf16[256,768]{1,0:T(8,128)(2,1)} %collective-permute-done.6.refs_7_.refs_10_), channel_id=1, source_target_pairs={{0,8},{1,25},{2,10},{3,27},{4,12},{5,29},{6,14},{7,31},{8,16},{9,1... | collective-permute-start | bytes 1179656 | tf_op jit(solution)/shard_map/ppermute | solution.py:233
  103.9 12.7 %collective-permute-start.11 = (bf16[256,768]{1,0:T(8,128)(2,1)}, bf16[256,768]{1,0:T(8,128)(2,1)}, u32[]{:S(2)}, u32[]{:S(2)}) collective-permute-start(bf16[256,768]{1,0:T(8,128)(2,1)} %collective-permute-done.10.refs_4_.refs_14_), channel_id=1, source_target_pairs={{0,8},{1,25},{2,10},{3,27},{4,12},{5,29},{6,14},{7,31},{8,16},{9,1... | collective-permute-start | bytes 1179656 | tf_op jit(solution)/shard_map/ppermute | solution.py:233
  106.5 1.1 copy-start.1
  110.5 2.2 %copy-start.9 = (bf16[256,768]{1,0:T(8,128)(2,1)S(1)}, bf16[256,768]{1,0:T(8,128)(2,1)}, u32[]{:S(2)}) copy-start(bf16[256,768]{1,0:T(8,128)(2,1)} %copy-done.8) | copy-start | bytes 1179652
  110.5 2.2 %copy-start.11 = (bf16[256,768]{1,0:T(8,128)(2,1)S(1)}, bf16[256,768]{1,0:T(8,128)(2,1)}, u32[]{:S(2)}) copy-start(bf16[256,768]{1,0:T(8,128)(2,1)} %copy-done.10) | copy-start | bytes 1179652
  112.6 3.9 %copy-start.3 = (bf16[384,1024]{1,0:T(8,128)(2,1)S(1)}, bf16[384,1024]{1,0:T(8,128)(2,1)}, u32[]{:S(2)}) copy-start(bf16[384,1024]{1,0:T(8,128)(2,1)} %copy-done.2) | copy-start | bytes 2359300
  112.7 3.9 %copy-start.6 = (bf16[256,768]{1,0:T(8,128)(2,1)S(1)}, bf16[256,768]{1,0:T(8,128)(2,1)}, u32[]{:S(2)}) copy-start(bf16[256,768]{1,0:T(8,128)(2,1)} %copy-done.5) | copy-start | bytes 1179652
  121.8 18.2 %all-to-all-start.3 = ((bf16[8,48,1024]{2,1,0:T(8,128)(2,1)}), bf16[8,48,1024]{2,1,0:T(8,128)(2,1)S(1)}, u32[]{:S(2)}, u32[]{:S(2)}) async-start(bf16[8,48,1024]{2,1,0:T(8,128)(2,1)} %bitcast.17), calls=%async_computation.3 | async-start | bytes 1572864 | tf_op jit(solution)/shard_map/all_to_all | solution.py:207
  127.8 1.0 copy-start.7
  128.8 1.1 copy-start.17
  133.4 11.1 %copy-start.14 = (bf16[2,128,384]{2,1,0:T(8,128)(2,1)S(1)}, bf16[2,128,384]{2,1,0:T(8,128)(2,1)}, u32[]{:S(2)}) copy-start(bf16[2,128,384]{2,1,0:T(8,128)(2,1)} %copy-done.13) | copy-start | bytes 589828
  140.1 16.8 %copy-start.20 = (f32[128,128]{1,0:T(8,128)S(1)}, f32[128,128]{1,0:T(8,128)}, u32[]{:S(2)}) copy-start(f32[128,128]{1,0:T(8,128)} %copy-done.19) | copy-start | bytes 196612
  140.1 16.8 %all-to-all-start.1 = ((bf16[8,48,1024]{2,1,0:T(8,128)(2,1)}), bf16[8,48,1024]{2,1,0:T(8,128)(2,1)S(1)}, u32[]{:S(2)}, u32[]{:S(2)}) async-start(bf16[8,48,1024]{2,1,0:T(8,128)(2,1)} %bitcast.7), calls=%async_computation.1 | async-start | bytes 1572864 | tf_op jit(solution)/shard_map/all_to_all | solution.py:207
  (7 other events, 5.6 us)

commit v2 on v1

v2 whole, which is shorter than its diff:
```python
import jax
import jax.numpy as jnp
from jax import lax
from jax.experimental import pallas as pl
from jax.experimental.pallas import tpu as pltpu
from jax.sharding import PartitionSpec as P

F32 = jnp.float32
BF16 = jnp.bfloat16
ALL = ("dp", "expert")
NY, CORES, PAR = 4, 2, 2


def call(body, name, out_shape, *args, mib=16):
    spec = pl.BlockSpec(memory_space=pltpu.VMEM)
    many = isinstance(out_shape, tuple)
    return pl.pallas_call(
        body,
        out_shape=out_shape,
        in_specs=[spec] * len(args),
        out_specs=(spec,) * len(out_shape) if many else spec,
        compiler_params=pltpu.CompilerParams(vmem_limit_bytes=mib * 1024 * 1024),
        name=name,
    )(*args)


def nt(left, right):
    return lax.dot_general(left, right, (((1,), (1,)), ((), ())), preferred_element_type=F32)


def nn(left, right):
    return jnp.dot(left, right, preferred_element_type=F32)


def places(ids, experts, capacity):
    top, rows = ids.shape
    kinds = lax.broadcasted_iota(jnp.int32, (experts, rows), 0)
    named = jnp.zeros((experts, rows), F32)
    for k in range(top):
        named = named + jnp.where(ids[k : k + 1, :] == kinds, 1.0, 0.0)
    earlier = jnp.where(
        lax.broadcasted_iota(jnp.int32, (rows, rows), 0)
        < lax.broadcasted_iota(jnp.int32, (rows, rows), 1),
        1.0,
        0.0,
    )
    before = nn(named.astype(BF16), earlier.astype(BF16))
    place = before + kinds.astype(F32) * capacity
    return [
        jnp.sum(jnp.where(ids[k : k + 1, :] == kinds, place, 0.0), axis=0, keepdims=True)
        for k in range(top)
    ]


def pack_kernel(ids_ref, comb_ref, tok_ref, cot_ref, sent_ref, held_ref, sems):
    top, rows = ids_ref.shape
    experts, capacity = sent_ref.shape[0], sent_ref.shape[1] // 2
    slots = experts * capacity
    slot_iota = lax.broadcasted_iota(jnp.int32, (slots, rows), 0).astype(F32)
    spread = jnp.zeros((slots, rows), F32)
    weight = jnp.zeros((slots, rows), F32)
    for k, slot in enumerate(places(ids_ref[...], experts, capacity)):
        hot = jnp.where(slot_iota == slot, 1.0, 0.0)
        spread = spread + hot
        weight = weight + hot * comb_ref[k : k + 1, :]
    spread = spread.astype(BF16)
    put_rows(held_ref, 0, nn(spread, tok_ref[...]).astype(BF16))
    first = send_out(held_ref, sent_ref, sems, 0)
    cot_rows = nn(spread, cot_ref[...])
    put_rows(held_ref, 1, (cot_rows * jnp.sum(weight, axis=1, keepdims=True)).astype(BF16))
    second = send_out(held_ref, sent_ref, sems, 1)
    first.wait()
    second.wait()


def put_rows(held_ref, half, values, columns=slice(None)):
    experts, capacity = held_ref.shape[0], held_ref.shape[1] // 2
    for e in range(experts):
        held_ref[e, half * capacity : (half + 1) * capacity, columns] = values[
            e * capacity : (e + 1) * capacity
        ]


def take_rows(ref, half):
    experts, capacity = ref.shape[0], ref.shape[1] // 2
    return jnp.concatenate(
        [ref[e, half * capacity : (half + 1) * capacity] for e in range(experts)], axis=0
    )


def send_out(held_ref, out_ref, sems, half):
    capacity = held_ref.shape[1] // 2
    part = pl.ds(half * capacity, capacity)
    copy = pltpu.make_async_copy(held_ref.at[:, part], out_ref.at[:, part], sems.at[half])
    copy.start()
    return copy


def pick_kernel(experts, capacity, ids_ref, comb_ref, late_ref, pick_ref, ccol_ref):
    del late_ref
    top, rows = ids_ref.shape
    slots = experts * capacity
    slot_iota = lax.broadcasted_iota(jnp.int32, (slots, rows), 0).astype(F32)
    for k, slot in enumerate(places(ids_ref[...], experts, capacity)):
        pick_ref[k] = jnp.transpose(jnp.where(slot_iota == slot, 1.0, 0.0)).astype(BF16)
    padded = jnp.concatenate([comb_ref[...], jnp.zeros((rows - top, rows), F32)], axis=0)
    ccol_ref[...] = jnp.transpose(padded)


def order_kernel(zs, order_ref):
    width = order_ref.shape[0]
    dp = lax.axis_index("dp")
    core = lax.rem(lax.axis_index("expert"), CORES)
    my_z, my_y = dp // NY, lax.rem(dp, NY)
    depth = width // (zs * NY)
    i = lax.broadcasted_iota(jnp.int32, (1, width), 1)
    r = lax.rem(i, depth)
    pos = lax.rem(i // depth, zs // PAR)
    step = i // (depth * zs)
    other = lax.rem(i // (depth * (zs // PAR)), PAR)
    zi = jnp.where(core == 0, pos, zs // PAR - 1 - pos)
    ahead = jnp.where(step == 1, -1, jnp.where(step == 2, 1, step - step // 3))
    y = lax.rem(my_y + NY + jnp.where(core == 0, ahead, -ahead), NY)
    z = zi * PAR + lax.rem(my_z + other, PAR)
    feature = (z * NY + y) * depth + r
    tile = 128

    def one(t, carry):
        d = lax.broadcasted_iota(jnp.int32, (tile, width), 0) + t * tile
        order_ref[pl.ds(pl.multiple_of(t * tile, tile), tile), :] = jnp.where(
            d == feature, 1.0, 0.0
        ).astype(BF16)
        return carry

    lax.fori_loop(0, width // tile, one, 0)


def turn_kernel(rows_ref, order_ref, tok_ref, grad_ref):
    tok_ref[...] = nn(take_rows(rows_ref, 0), order_ref[...]).astype(BF16)
    grad_ref[...] = nn(take_rows(rows_ref, 1), order_ref[...]).astype(BF16)


def pair(pieces, columns):
    return jnp.concatenate([piece[:, columns] for piece in pieces], axis=0)


def partial_kernel(tok_ref, grad_ref, *refs):
    pieces, sums = refs[:-3], refs[-3:]
    ff = sums[0].shape[1]
    tile, depth = 256, 2 * pieces[0].shape[0]
    for m, (out_ref, rows_ref) in enumerate(zip(sums, (tok_ref, tok_ref, grad_ref))):
        for t in range(ff // tile):
            columns = slice(m * ff + t * tile, m * ff + (t + 1) * tile)
            total = None
            for j in range(len(pieces) // 2):
                part = nn(
                    rows_ref[:, j * depth : (j + 1) * depth],
                    pair(pieces[2 * j : 2 * j + 2], columns),
                )
                total = part if total is None else total + part
            out_ref[:, t * tile : (t + 1) * tile] = total


def final_kernel(count, tok_ref, grad_ref, order_ref, *refs):
    sums, pieces = refs[:3], refs[3 : 3 + count]
    out_ref, late_ref, hidden_ref, gate_grad_ref, up_grad_ref, arr_ref, held_ref, sems = refs[3 + count :]
    late_ref[...] = jnp.zeros_like(late_ref)
    ff, width = hidden_ref.shape[1], order_ref.shape[0]
    tile, depth = 256, 2 * pieces[0].shape[0]
    last = slice(width - depth, width)
    for t in range(ff // tile):
        here = slice(t * tile, (t + 1) * tile)
        gate, up, hidden_grad = (
            sums[m][:, here]
            + nn(rows_ref[:, last], pair(pieces[-2:], slice(m * ff + t * tile, m * ff + (t + 1) * tile)))
            for m, rows_ref in enumerate((tok_ref, tok_ref, grad_ref))
        )
        sigma = 1.0 / (1.0 + jnp.exp(-gate))
        silu = gate * sigma
        hidden_ref[:, here] = (silu * up).astype(BF16)
        up_grad_ref[:, here] = (hidden_grad * silu).astype(BF16)
        gate_grad_ref[:, here] = (hidden_grad * up * sigma * (1.0 + gate * (1.0 - sigma))).astype(BF16)
    copies = []
    for half, terms in enumerate((((hidden_ref, 2),), ((gate_grad_ref, 0), (up_grad_ref, 1)))):
        for j in range(count // 2):
            total = None
            for left_ref, m in terms:
                part = nt(left_ref[...], pair(pieces[2 * j : 2 * j + 2], slice(m * ff, (m + 1) * ff)))
                total = part if total is None else total + part
            arr_ref[half, :, j * depth : (j + 1) * depth] = total.astype(BF16)
        for t in range(width // tile):
            here = slice(t * tile, (t + 1) * tile)
            put_rows(held_ref, half, nt(arr_ref[half], order_ref[here, :]).astype(BF16), here)
        copies.append(send_out(held_ref, out_ref, sems, half))
    for copy in copies:
        copy.wait()


def post_kernel(pick_ref, ccol_ref, cot_ref, back_ref, mixed_ref, igrad_ref, cgrad_ref):
    top, rows, _ = pick_ref.shape
    cot = cot_ref[...].astype(F32)
    back = take_rows(back_ref, 0)
    lane = lax.broadcasted_iota(jnp.int32, (rows, rows), 1)
    mixed = jnp.zeros(cot.shape, F32)
    grads = jnp.zeros((rows, rows), F32)
    both = None
    for k in range(top):
        out = nn(pick_ref[k], back)
        mixed = mixed + ccol_ref[:, k : k + 1] * out
        grads = jnp.where(lane == k, jnp.sum(cot * out, axis=1, keepdims=True), grads)
        both = pick_ref[k] if both is None else both + pick_ref[k]
    mixed_ref[...] = mixed.astype(BF16)
    cgrad_ref[...] = jnp.transpose(grads)[:top, :]
    igrad_ref[...] = nn(both, take_rows(back_ref, 1)).astype(BF16)


def on_device(tokens, expert_ids, combine, w_gate, w_up, w_down, cotangent):
    groups = lax.axis_size("expert")
    zs = lax.axis_size("dp") // NY
    rows, top = expert_ids.shape
    width = tokens.shape[1]
    ff = w_gate.shape[2]
    capacity = 3 * rows * top // (2 * groups)
    slots = groups * capacity
    shape = jax.ShapeDtypeStruct

    def device(z, y, e):
        return ((z % zs) * NY + y % NY) * groups + e

    def shifted(dz, dy):
        return [
            (device(z, y, e), device(z + s * dz, y + s * dy, e))
            for z in range(zs)
            for y in range(NY)
            for e in range(groups)
            for s in ((1, -1)[e % CORES],)
        ]

    far_groups = [
        [device(z, y, e) for z in range(par, zs, PAR)][:: (1, -1)[e % CORES]]
        for par in range(PAR)
        for y in range(NY)
        for e in range(groups)
    ]

    def swap(values):
        return lax.all_to_all(values, "expert", 0, 0, tiled=True)

    def send(values, dz, dy):
        return lax.ppermute(values, ALL, shifted(dz, dy))

    joined = jnp.concatenate([w_gate[0], w_up[0], w_down[0]], axis=1)
    own = lax.all_gather(joined, ALL, axis=0, tiled=True, axis_index_groups=far_groups)
    ahead, behind = send(own, 0, 1), send(own, 0, -1)
    by_y = [own, ahead, behind, send(ahead, 0, 1)]
    pieces = [p for held in by_y for p in (held, send(held, 1, 0))]
    count = len(pieces)
    spec = pl.BlockSpec(memory_space=pltpu.VMEM)
    far_out = pl.BlockSpec(memory_space=pltpu.HBM)
    both = shape((groups, 2 * capacity, width), BF16)
    ids, weights = expert_ids.T, combine.T
    sent = pl.pallas_call(
        pack_kernel,
        out_shape=both,
        in_specs=[spec] * 4,
        out_specs=far_out,
        scratch_shapes=[pltpu.VMEM(both.shape, BF16), pltpu.SemaphoreType.DMA((2,))],
        compiler_params=pltpu.CompilerParams(vmem_limit_bytes=16 * 1024 * 1024),
        name="pack",
    )(ids, weights, tokens, cotangent)
    order = call(lambda ref: order_kernel(zs, ref), "order", shape((width, width), BF16))
    rows_shape, sum_shape = shape((slots, width), BF16), shape((slots, ff), F32)
    turned = call(turn_kernel, "turn", (rows_shape,) * 2, swap(sent), order)
    sums = call(partial_kernel, "partial", (sum_shape,) * 3, *turned, *pieces[:-2], mib=12)
    results, late = pl.pallas_call(
        lambda *refs: final_kernel(count, *refs),
        out_shape=(both, shape((8, 128), F32)),
        in_specs=[spec] * (6 + count),
        out_specs=(far_out, spec),
        scratch_shapes=[pltpu.VMEM((slots, ff), BF16)] * 3
        + [
            pltpu.VMEM((2, slots, width), BF16),
            pltpu.VMEM(both.shape, BF16),
            pltpu.SemaphoreType.DMA((2,)),
        ],
        compiler_params=pltpu.CompilerParams(vmem_limit_bytes=20 * 1024 * 1024),
        name="final",
    )(*turned, order, *sums, *pieces)
    back = swap(results)
    pick, ccol = pl.pallas_call(
        lambda *refs: pick_kernel(groups, capacity, *refs),
        out_shape=(shape((top, rows, slots), BF16), shape((rows, rows), F32)),
        in_specs=[spec] * 3,
        out_specs=(spec,) * 2,
        compiler_params=pltpu.CompilerParams(vmem_limit_bytes=8 * 1024 * 1024),
        name="pick",
    )(ids, weights, late)
    mixed, input_grad, combine_grad = call(
        post_kernel,
        "post",
        (shape((rows, width), BF16),) * 2 + (shape((top, rows), F32),),
        pick,
        ccol,
        cotangent,
        back,
    )
    return mixed, input_grad, combine_grad.T


def solution(mesh):
    rows = P(ALL, None)
    weights = P("expert", "dp", None)
    return jax.shard_map(
        on_device,
        mesh=mesh,
        in_specs=(rows, rows, rows, weights, weights, weights, rows),
        out_specs=(rows, rows, rows),
        check_vma=False,
    )
```

time: 160 us -> 146 us (0.912)
  starting transfers between devices: 65.5 us -> 41.6 us
  waiting for transfers between devices: 19 us -> 35.4 us
  local copies, waits for them, and re-layouts: 8.37 us -> 4.42 us
    ppermute x12 -> x7, starting transfers between devices: 40 us -> 21.1 us  [send(): return lax.ppermute(values, ALL, shifted(dz, dy))]
    ppermute x12 -> x7, waiting for transfers between devices: 0.17 us -> 15 us  [send(): return lax.ppermute(values, ALL, shifted(dz, dy))]
    all_to_all x4 -> x2, starting transfers between devices: 25.5 us -> 20.5 us  [swap(): return lax.all_to_all(values, 'expert', 0, 0, tiled=True)]
    unnamed x46 -> x16, local copies, waits for them, and re-layouts: 8.33 us -> 4.42 us
    pallas_call x7 -> x4, Pallas kernels: 10.4 us -> 8.13 us  [call(): pl.pallas_call(body, out_shape=out_shape, in_specs=[spec] * len(args), ou...]
    all_to_all x4 -> x2, waiting for transfers between devices: 18.8 us -> 20.4 us  [swap(): return lax.all_to_all(values, 'expert', 0, 0, tiled=True)]
    pallas_call x2 -> x3, Pallas kernels: 8 us -> 8.68 us  [the longest x1 6.75 us: on_device(): pl.pallas_call(lambda *refs: final_kernel(count, *refs), out_shape=(both,...]
  transfers between devices with their start and end apart: 16 -> 9, of which waited for: 4 -> 4; matrix products, arithmetic and copies ran while one was open for 0% -> 0% of each run, Pallas kernels for 8% -> 6%
where the time goes in v2:
time: 146 us; the launch traced here: 145 us
  blocking collectives  44.9 us (31%)
  starting transfers between devices  41.6 us (28%)
  waiting for transfers between devices  35.4 us (24%)
  Pallas kernels  16.8 us (12%)
  local copies, waits for them, and re-layouts  4.42 us (3%)
    all_gather x1, blocking collectives, on_device(): lax.all_gather(joined, ALL, axis=0, tiled=True, axis_index_groups=far_gro...  44.9 us
    ppermute x7, starting transfers between devices, send(): return lax.ppermute(values, ALL, shifted(dz, dy))  21.1 us
    all_to_all x2, starting transfers between devices, swap(): return lax.all_to_all(values, 'expert', 0, 0, tiled=True)  20.5 us
    all_to_all x2, waiting for transfers between devices, swap(): return lax.all_to_all(values, 'expert', 0, 0, tiled=True)  20.4 us
    ppermute x7, waiting for transfers between devices, send(): return lax.ppermute(values, ALL, shifted(dz, dy))  15 us
    pallas_call x4, Pallas kernels, call(): pl.pallas_call(body, out_shape=out_shape, in_specs=[spec] * len(args), ou...  8.13 us
    pallas_call x1, Pallas kernels, on_device(): pl.pallas_call(lambda *refs: final_kernel(count, *refs), out_shape=(both,...  6.75 us
    unnamed x16, local copies, waits for them, and re-layouts  4.42 us
  transfers between devices with their start and end apart: 9, of which 4 were waited for; matrix products, arithmetic and copies ran while one was open for 0% of the time, Pallas kernels for 6%

profile of v2, /device:TPU:1, one launch (start us, length us, event | category | flops | bytes accessed | tf_op | source)
XLA Modules:
  0.0 144.6 jit_solution(15240455797618684009)
XLA Ops:
  0.6 0.7 pad_maximum_fusion
  1.4 44.9 %all_gather.3.refs_0_.refs_6_ = bf16[128,2304]{1,0:T(8,128)(2,1)S(1)} all-gather(bf16[8,2304]{1,0:T(8,128)(2,1)S(1)} %pad_maximum_fusion), channel_id=1, replica_groups={{0,64,128,192,256,320,384,448,512,576,640,704,768,832,896,960},{961,897..., dimensions={0}, use_global_device_ids=true | all-gather | bytes 626688 | tf_op jit(solution)/shard_map/all_gather | solution.py:253
  46.2 4.6 %collective-permute-start.1 = (bf16[128,2304]{1,0:T(8,128)(2,1)S(1)}, bf16[128,2304]{1,0:T(8,128)(2,1)S(1)}, u32[]{:S(2)}, u32[]{:S(2)}) collective-permute-start(bf16[128,2304]{1,0:T(8,128)(2,1)S(1)} %all_gather.3.refs_0_.refs_6_), channel_id=1, source_target_pairs={{0,8},{1,25},{2,10},{3,27},{4,12},{5,29},{6,14},{7,31},{8,16},{9,1... | collective-permute-start | bytes 1769480 | tf_op jit(solution)/shard_map/ppermute | solution.py:250
  50.9 0.0 copy-start.1
  50.9 0.9 copy-done.1
  51.8 0.9 copy-done.3
  52.8 0.7 copy-done.4
  53.5 0.7 copy-done.6
  54.1 1.7 %pack.1 = bf16[8,96,1024]{2,1,0:T(8,128)(2,1)} custom-call(s32[2,128]{1,0:T(2,128)S(1)} %bitcast.6, f32[2,128]{1,0:T(2,128)S(1)} %bitcast.8, bf16[128,1024]{1,0:T(8,128)(2,1)S(1)} %copy-done.3, bf16[128,1024]{1,0:T(8,128)(2,1)S(1)} %copy-done.1), custom_call_target="tpu_custom_call" | custom-call | tf_op jit(solution)/shard_map/pack/pallas_call | solution.py:262
  55.8 12.2 %all-to-all-start = ((bf16[8,96,1024]{2,1,0:T(8,128)(2,1)}), bf16[8,96,1024]{2,1,0:T(8,128)(2,1)}, u32[]{:S(2)}, u32[]{:S(2)}) async-start(bf16[8,96,1024]{2,1,0:T(8,128)(2,1)} %pack.1), calls=%async_computation | async-start | bytes 3145728 | tf_op jit(solution)/shard_map/all_to_all | solution.py:247
  68.0 3.2 %collective-permute-start.3 = (bf16[128,2304]{1,0:T(8,128)(2,1)S(1)}, bf16[128,2304]{1,0:T(8,128)(2,1)}, u32[]{:S(2)}, u32[]{:S(2)}) collective-permute-start(bf16[128,2304]{1,0:T(8,128)(2,1)S(1)} %all_gather.3.refs_0_.refs_6_), channel_id=1, source_target_pairs={{0,24},{1,9},{2,26},{3,11},{4,28},{5,13},{6,30},{7,15},{8,0},{9,17... | collective-permute-start | bytes 1769480 | tf_op jit(solution)/shard_map/ppermute | solution.py:250
  71.2 0.0 collective-permute-done.1.refs_2_.refs_8_
  71.2 3.3 %collective-permute-start.5 = (bf16[128,2304]{1,0:T(8,128)(2,1)S(1)}, bf16[128,2304]{1,0:T(8,128)(2,1)}, u32[]{:S(2)}, u32[]{:S(2)}) collective-permute-start(bf16[128,2304]{1,0:T(8,128)(2,1)S(1)} %collective-permute-done.1.refs_2_.refs_8_), channel_id=1, source_target_pairs={{0,8},{1,25},{2,10},{3,27},{4,12},{5,29},{6,14},{7,31},{8,16},{9,1... | collective-permute-start | bytes 1769480 | tf_op jit(solution)/shard_map/ppermute | solution.py:250
  74.5 1.9 %collective-permute-start = (bf16[128,2304]{1,0:T(8,128)(2,1)S(1)}, bf16[128,2304]{1,0:T(8,128)(2,1)}, u32[]{:S(2)}, u32[]{:S(2)}) collective-permute-start(bf16[128,2304]{1,0:T(8,128)(2,1)S(1)} %all_gather.3.refs_0_.refs_6_), channel_id=1, source_target_pairs={{0,32},{1,993},{2,34},{3,995},{4,36},{5,997},{6,38},{7,999},{8,40}... | collective-permute-start | bytes 1769480 | tf_op jit(solution)/shard_map/ppermute | solution.py:250
  76.4 6.0 %collective-permute-done.3.refs_4_.refs_10_ = bf16[128,2304]{1,0:T(8,128)(2,1)} collective-permute-done((bf16[128,2304]{1,0:T(8,128)(2,1)S(1)}, bf16[128,2304]{1,0:T(8,128)(2,1)}, u32[]{:S(2)}, u32[]{:S(2)}) %collective-permute-start.3) | collective-permute-done | bytes 589856 | tf_op jit(solution)/shard_map/ppermute | solution.py:250
  82.4 1.9 %collective-permute-start.4 = (bf16[128,2304]{1,0:T(8,128)(2,1)}, bf16[128,2304]{1,0:T(8,128)(2,1)}, u32[]{:S(2)}, u32[]{:S(2)}) collective-permute-start(bf16[128,2304]{1,0:T(8,128)(2,1)} %collective-permute-done.3.refs_4_.refs_10_), channel_id=1, source_target_pairs={{0,32},{1,993},{2,34},{3,995},{4,36},{5,997},{6,38},{7,999},{8,40}... | collective-permute-start | bytes 1769480 | tf_op jit(solution)/shard_map/ppermute | solution.py:250
  84.3 2.5 %collective-permute-start.2 = (bf16[128,2304]{1,0:T(8,128)(2,1)S(1)}, bf16[128,2304]{1,0:T(8,128)(2,1)}, u32[]{:S(2)}, u32[]{:S(2)}) collective-permute-start(bf16[128,2304]{1,0:T(8,128)(2,1)S(1)} %collective-permute-done.1.refs_2_.refs_8_), channel_id=1, source_target_pairs={{0,32},{1,993},{2,34},{3,995},{4,36},{5,997},{6,38},{7,999},{8,40}... | collective-permute-start | bytes 1769480 | tf_op jit(solution)/shard_map/ppermute | solution.py:250
  86.8 0.0 collective-permute-done.5.refs_12_
  86.8 3.7 %collective-permute-start.6 = (bf16[128,2304]{1,0:T(8,128)(2,1)}, bf16[128,2304]{1,0:T(8,128)(2,1)}, u32[]{:S(2)}, u32[]{:S(2)}) collective-permute-start(bf16[128,2304]{1,0:T(8,128)(2,1)} %collective-permute-done.5.refs_12_), channel_id=1, source_target_pairs={{0,32},{1,993},{2,34},{3,995},{4,36},{5,997},{6,38},{7,999},{8,40}... | collective-permute-start | bytes 1769480 | tf_op jit(solution)/shard_map/ppermute | solution.py:250
  90.5 0.4 order.1.order_ref.refs_2_
  90.9 0.0 all-to-all-done.rows_ref
  90.9 3.2 %turn.1 = (bf16[384,1024]{1,0:T(8,128)(2,1)S(1)}, bf16[384,1024]{1,0:T(8,128)(2,1)S(1)}) custom-call(bf16[8,96,1024]{2,1,0:T(8,128)(2,1)} %all-to-all-done.rows_ref, bf16[1024,1024]{1,0:T(8,128)(2,1)S(1)} %order.1.order_ref.refs_2_), custom_call_target="tpu_custom_call" | custom-call | tf_op jit(solution)/shard_map/turn/pallas_call | solution.py:17
  94.1 0.0 collective-permute-done.refs_1_.refs_7_
  94.2 5.8 %collective-permute-done.2.refs_3_.refs_9_ = bf16[128,2304]{1,0:T(8,128)(2,1)} collective-permute-done((bf16[128,2304]{1,0:T(8,128)(2,1)S(1)}, bf16[128,2304]{1,0:T(8,128)(2,1)}, u32[]{:S(2)}, u32[]{:S(2)}) %collective-permute-start.2) | collective-permute-done | bytes 589856 | tf_op jit(solution)/shard_map/ppermute | solution.py:250
  100.0 3.1 %partial.1 = (f32[384,768]{1,0:T(8,128)S(1)}, f32[384,768]{1,0:T(8,128)S(1)}, f32[384,768]{1,0:T(8,128)S(1)}) custom-call(bf16[384,1024]{1,0:T(8,128)(2,1)S(1)} %get-tuple-element.15.tok_ref.refs_0_, bf16[384,1024]{1,0:T(8,128)(2,1)S(1)} %get-tuple-element.16.grad_ref.refs_1_, bf16[128,2304]{1,0:T(8,128)(2,1)S(1)} %all_gather.3.refs_0_.refs_6_, ...), custom_call_target="tpu_custom_call" | custom-call | tf_op jit(solution)/shard_map/partial/pallas_call | solution.py:17
  103.1 3.2 %collective-permute-done.6.refs_13_ = bf16[128,2304]{1,0:T(8,128)(2,1)} collective-permute-done((bf16[128,2304]{1,0:T(8,128)(2,1)}, bf16[128,2304]{1,0:T(8,128)(2,1)}, u32[]{:S(2)}, u32[]{:S(2)}) %collective-permute-start.6) | collective-permute-done | bytes 589856 | tf_op jit(solution)/shard_map/ppermute | solution.py:250
  106.3 6.7 %final.1 = (bf16[8,96,1024]{2,1,0:T(8,128)(2,1)S(1)}, f32[8,128]{1,0:T(8,128)S(1)}) custom-call(bf16[384,1024]{1,0:T(8,128)(2,1)S(1)} %get-tuple-element.15.tok_ref.refs_0_, bf16[384,1024]{1,0:T(8,128)(2,1)S(1)} %get-tuple-element.16.grad_ref.refs_1_, bf16[1024,1024]{1,0:T(8,128)(2,1)S(1)} %order.1.order_ref.refs_2_, ...), custom_call_target="tpu_custom_call" | custom-call | tf_op jit(solution)/shard_map/final/pallas_call | solution.py:275
  113.0 1.2 copy-done
  114.2 8.3 %all-to-all-start.1 = ((bf16[8,96,1024]{2,1,0:T(8,128)(2,1)}), bf16[8,96,1024]{2,1,0:T(8,128)(2,1)S(1)}, u32[]{:S(2)}, u32[]{:S(2)}) async-start(bf16[8,96,1024]{2,1,0:T(8,128)(2,1)} %copy-done), calls=%async_computation.1 | async-start | bytes 3145728 | tf_op jit(solution)/shard_map/all_to_all | solution.py:247
  122.5 0.3 pick.1
  122.8 20.4 %all-to-all-done.1.back_ref = bf16[8,96,1024]{2,1,0:T(8,128)(2,1)S(1)} async-done(((bf16[8,96,1024]{2,1,0:T(8,128)(2,1)}), bf16[8,96,1024]{2,1,0:T(8,128)(2,1)S(1)}, u32[]{:S(2)}, u32[]{:S(2)}) %all-to-all-start.1) | async-done | bytes 1572896 | tf_op jit(solution)/shard_map/all_to_all | solution.py:247
  143.2 1.4 post.1
  (11 shorter events, 0.0 us)
Async XLA Ops:
  46.2 25.0 %collective-permute-start.1 = (bf16[128,2304]{1,0:T(8,128)(2,1)S(1)}, bf16[128,2304]{1,0:T(8,128)(2,1)S(1)}, u32[]{:S(2)}, u32[]{:S(2)}) collective-permute-start(bf16[128,2304]{1,0:T(8,128)(2,1)S(1)} %all_gather.3.refs_0_.refs_6_), channel_id=1, source_target_pairs={{0,8},{1,25},{2,10},{3,27},{4,12},{5,29},{6,14},{7,31},{8,16},{9,1... | collective-permute-start | bytes 1769480 | tf_op jit(solution)/shard_map/ppermute | solution.py:250
  50.9 1.0 copy-start.1
  51.8 0.9 copy-start.3
  52.8 0.7 copy-start.4
  53.5 0.7 copy-start.6
  55.8 35.1 %all-to-all-start = ((bf16[8,96,1024]{2,1,0:T(8,128)(2,1)}), bf16[8,96,1024]{2,1,0:T(8,128)(2,1)}, u32[]{:S(2)}, u32[]{:S(2)}) async-start(bf16[8,96,1024]{2,1,0:T(8,128)(2,1)} %pack.1), calls=%async_computation | async-start | bytes 3145728 | tf_op jit(solution)/shard_map/all_to_all | solution.py:247
  68.0 14.4 %collective-permute-start.3 = (bf16[128,2304]{1,0:T(8,128)(2,1)S(1)}, bf16[128,2304]{1,0:T(8,128)(2,1)}, u32[]{:S(2)}, u32[]{:S(2)}) collective-permute-start(bf16[128,2304]{1,0:T(8,128)(2,1)S(1)} %all_gather.3.refs_0_.refs_6_), channel_id=1, source_target_pairs={{0,24},{1,9},{2,26},{3,11},{4,28},{5,13},{6,30},{7,15},{8,0},{9,17... | collective-permute-start | bytes 1769480 | tf_op jit(solution)/shard_map/ppermute | solution.py:250
  71.2 15.6 %collective-permute-start.5 = (bf16[128,2304]{1,0:T(8,128)(2,1)S(1)}, bf16[128,2304]{1,0:T(8,128)(2,1)}, u32[]{:S(2)}, u32[]{:S(2)}) collective-permute-start(bf16[128,2304]{1,0:T(8,128)(2,1)S(1)} %collective-permute-done.1.refs_2_.refs_8_), channel_id=1, source_target_pairs={{0,8},{1,25},{2,10},{3,27},{4,12},{5,29},{6,14},{7,31},{8,16},{9,1... | collective-permute-start | bytes 1769480 | tf_op jit(solution)/shard_map/ppermute | solution.py:250
  74.5 19.7 %collective-permute-start = (bf16[128,2304]{1,0:T(8,128)(2,1)S(1)}, bf16[128,2304]{1,0:T(8,128)(2,1)}, u32[]{:S(2)}, u32[]{:S(2)}) collective-permute-start(bf16[128,2304]{1,0:T(8,128)(2,1)S(1)} %all_gather.3.refs_0_.refs_6_), channel_id=1, source_target_pairs={{0,32},{1,993},{2,34},{3,995},{4,36},{5,997},{6,38},{7,999},{8,40}... | collective-permute-start | bytes 1769480 | tf_op jit(solution)/shard_map/ppermute | solution.py:250
  82.4 11.8 %collective-permute-start.4 = (bf16[128,2304]{1,0:T(8,128)(2,1)}, bf16[128,2304]{1,0:T(8,128)(2,1)}, u32[]{:S(2)}, u32[]{:S(2)}) collective-permute-start(bf16[128,2304]{1,0:T(8,128)(2,1)} %collective-permute-done.3.refs_4_.refs_10_), channel_id=1, source_target_pairs={{0,32},{1,993},{2,34},{3,995},{4,36},{5,997},{6,38},{7,999},{8,40}... | collective-permute-start | bytes 1769480 | tf_op jit(solution)/shard_map/ppermute | solution.py:250
  84.3 15.6 %collective-permute-start.2 = (bf16[128,2304]{1,0:T(8,128)(2,1)S(1)}, bf16[128,2304]{1,0:T(8,128)(2,1)}, u32[]{:S(2)}, u32[]{:S(2)}) collective-permute-start(bf16[128,2304]{1,0:T(8,128)(2,1)S(1)} %collective-permute-done.1.refs_2_.refs_8_), channel_id=1, source_target_pairs={{0,32},{1,993},{2,34},{3,995},{4,36},{5,997},{6,38},{7,999},{8,40}... | collective-permute-start | bytes 1769480 | tf_op jit(solution)/shard_map/ppermute | solution.py:250
  86.8 19.5 %collective-permute-start.6 = (bf16[128,2304]{1,0:T(8,128)(2,1)}, bf16[128,2304]{1,0:T(8,128)(2,1)}, u32[]{:S(2)}, u32[]{:S(2)}) collective-permute-start(bf16[128,2304]{1,0:T(8,128)(2,1)} %collective-permute-done.5.refs_12_), channel_id=1, source_target_pairs={{0,32},{1,993},{2,34},{3,995},{4,36},{5,997},{6,38},{7,999},{8,40}... | collective-permute-start | bytes 1769480 | tf_op jit(solution)/shard_map/ppermute | solution.py:250
  113.0 1.2 copy-start
  114.2 8.3 %copy-start.5 = (s32[128,2]{0,1:T(2,128)S(1)}, s32[128,2]{0,1:T(2,128)}, u32[]{:S(2)}) copy-start(s32[128,2]{0,1:T(2,128)} %param.8) | copy-start | bytes 3076
  114.2 8.3 %copy-start.7 = (f32[128,2]{0,1:T(2,128)S(1)}, f32[128,2]{0,1:T(2,128)}, u32[]{:S(2)}) copy-start(f32[128,2]{0,1:T(2,128)} %param.9) | copy-start | bytes 3076
  114.2 29.0 %copy-start.2 = (bf16[128,1024]{1,0:T(8,128)(2,1)S(1)}, bf16[128,1024]{1,0:T(8,128)(2,1)}, u32[]{:S(2)}) copy-start(bf16[128,1024]{1,0:T(8,128)(2,1)} %cot_ref.3) | copy-start | bytes 786436
  114.2 29.0 %all-to-all-start.1 = ((bf16[8,96,1024]{2,1,0:T(8,128)(2,1)}), bf16[8,96,1024]{2,1,0:T(8,128)(2,1)S(1)}, u32[]{:S(2)}, u32[]{:S(2)}) async-start(bf16[8,96,1024]{2,1,0:T(8,128)(2,1)} %copy-done), calls=%async_computation.1 | async-start | bytes 3145728 | tf_op jit(solution)/shard_map/all_to_all | solution.py:247

commit v3 on v2

--- a/solution.py
+++ b/solution.py
@@ -22,6 +22,19 @@
         compiler_params=pltpu.CompilerParams(vmem_limit_bytes=mib * 1024 * 1024),
         name=name,
     )(*args)
+
+
+def after(values, earlier):
+    anywhere = pl.BlockSpec(memory_space=pl.ANY)
+    return pl.pallas_call(
+        lambda *refs: None,
+        out_shape=jax.ShapeDtypeStruct(values.shape, values.dtype),
+        in_specs=[anywhere] * 2,
+        out_specs=anywhere,
+        input_output_aliases={0: 0},
+        compiler_params=pltpu.CompilerParams(vmem_limit_bytes=1024 * 1024),
+        name="after",
+    )(values, earlier)
 
 
 def nt(left, right):
@@ -52,20 +65,38 @@
     ]
 
 
-def pack_kernel(ids_ref, comb_ref, tok_ref, cot_ref, sent_ref, held_ref, sems):
+def pack_kernel(*refs):
+    sources, (sent_ref, joined_ref), targets = refs[:7], refs[7:9], refs[9:16]
+    ids_ref, comb_ref, tok_ref, cot_ref = targets[3:]
+    held_ref, sems, load_sems = refs[16:]
+    loads = [
+        pltpu.make_async_copy(source, target, load_sems.at[n])
+        for n, (source, target) in enumerate(zip(sources, targets))
+    ]
+    for load in loads:
+        load.start()
+    ff = joined_ref.shape[1] // 3
+    for m, load in enumerate(loads[:3]):
+        load.wait()
+        joined_ref[:, m * ff : (m + 1) * ff] = targets[m][0]
+    loads = loads[3:]
     top, rows = ids_ref.shape
     experts, capacity = sent_ref.shape[0], sent_ref.shape[1] // 2
     slots = experts * capacity
     slot_iota = lax.broadcasted_iota(jnp.int32, (slots, rows), 0).astype(F32)
     spread = jnp.zeros((slots, rows), F32)
     weight = jnp.zeros((slots, rows), F32)
+    loads[0].wait()
+    loads[1].wait()
     for k, slot in enumerate(places(ids_ref[...], experts, capacity)):
         hot = jnp.where(slot_iota == slot, 1.0, 0.0)
         spread = spread + hot
         weight = weight + hot * comb_ref[k : k + 1, :]
     spread = spread.astype(BF16)
+    loads[2].wait()
     put_rows(held_ref, 0, nn(spread, tok_ref[...]).astype(BF16))
     first = send_out(held_ref, sent_ref, sems, 0)
+    loads[3].wait()
     cot_rows = nn(spread, cot_ref[...])
     put_rows(held_ref, 1, (cot_rows * jnp.sum(weight, axis=1, keepdims=True)).astype(BF16))
     second = send_out(held_ref, sent_ref, sems, 1)
@@ -249,34 +280,43 @@
     def send(values, dz, dy):
         return lax.ppermute(values, ALL, shifted(dz, dy))
 
-    joined = jnp.concatenate([w_gate[0], w_up[0], w_down[0]], axis=1)
-    own = lax.all_gather(joined, ALL, axis=0, tiled=True, axis_index_groups=far_groups)
-    ahead, behind = send(own, 0, 1), send(own, 0, -1)
-    by_y = [own, ahead, behind, send(ahead, 0, 1)]
-    pieces = [p for held in by_y for p in (held, send(held, 1, 0))]
-    count = len(pieces)
     spec = pl.BlockSpec(memory_space=pltpu.VMEM)
-    far_out = pl.BlockSpec(memory_space=pltpu.HBM)
     both = shape((groups, 2 * capacity, width), BF16)
     ids, weights = expert_ids.T, combine.T
-    sent = pl.pallas_call(
+    depth = w_gate.shape[1]
+    hbm = pl.BlockSpec(memory_space=pltpu.HBM)
+    sources = (w_gate, w_up, w_down, ids, weights, tokens, cotangent)
+    sent, joined = pl.pallas_call(
         pack_kernel,
-        out_shape=both,
-        in_specs=[spec] * 4,
-        out_specs=far_out,
-        scratch_shapes=[pltpu.VMEM(both.shape, BF16), pltpu.SemaphoreType.DMA((2,))],
-        compiler_params=pltpu.CompilerParams(vmem_limit_bytes=16 * 1024 * 1024),
+        out_shape=(both, shape((depth, 3 * ff), BF16)),
+        in_specs=[hbm] * len(sources),
+        out_specs=(hbm, spec),
+        scratch_shapes=[pltpu.VMEM(v.shape, v.dtype) for v in sources]
+        + [
+            pltpu.VMEM(both.shape, BF16),
+            pltpu.SemaphoreType.DMA((2,)),
+            pltpu.SemaphoreType.DMA((len(sources),)),
+        ],
+        compiler_params=pltpu.CompilerParams(vmem_limit_bytes=12 * 1024 * 1024),
         name="pack",
-    )(ids, weights, tokens, cotangent)
+    )(*(pltpu.with_memory_space_constraint(v, pltpu.HBM) for v in sources))
+    arrived = swap(sent)
+    own = lax.all_gather(joined, ALL, axis=0, tiled=True, axis_index_groups=far_groups)
+    own = after(own, arrived)
+    ahead, beside, behind = send(own, 0, 1), send(own, 1, 0), send(own, 0, -1)
+    across = send(ahead, 0, 1)
+    pieces = [own, beside, ahead, send(ahead, 1, 0), behind, send(beside, 0, -1)]
+    pieces += [across, send(across, 1, 0)]
+    count = len(pieces)
     order = call(lambda ref: order_kernel(zs, ref), "order", shape((width, width), BF16))
     rows_shape, sum_shape = shape((slots, width), BF16), shape((slots, ff), F32)
-    turned = call(turn_kernel, "turn", (rows_shape,) * 2, swap(sent), order)
+    turned = call(turn_kernel, "turn", (rows_shape,) * 2, arrived, order)
     sums = call(partial_kernel, "partial", (sum_shape,) * 3, *turned, *pieces[:-2], mib=12)
     results, late = pl.pallas_call(
         lambda *refs: final_kernel(count, *refs),
-        out_shape=(both, shape((8, 128), F32)),
+        out_shape=(pltpu.HBM(both.shape, BF16), shape((8, 128), F32)),
         in_specs=[spec] * (6 + count),
-        out_specs=(far_out, spec),
+        out_specs=(hbm, spec),
         scratch_shapes=[pltpu.VMEM((slots, ff), BF16)] * 3
         + [
             pltpu.VMEM((2, slots, width), BF16),

time: 146 us -> 139 us (0.952)
  starting transfers between devices: 41.6 us -> 58.4 us
  blocking collectives: 44.9 us -> 32.9 us
  local copies, waits for them, and re-layouts: 4.42 us -> 0.02 us
  Pallas kernels: 16.8 us -> 13.5 us
  waiting for transfers between devices: 35.4 us -> 33.3 us
    all_to_all x2, starting transfers between devices: 20.5 us -> 34.3 us  [swap(): return lax.all_to_all(values, 'expert', 0, 0, tiled=True)]
    all_gather x1, blocking collectives: 44.9 us -> 32.9 us  [on_device(): lax.all_gather(joined, ALL, axis=0, tiled=True, axis_index_groups=far_gro...]
    unnamed x16 -> x6, local copies, waits for them, and re-layouts: 4.42 us -> 0.02 us
    ppermute x7, starting transfers between devices: 21.1 us -> 24.1 us  [send(): return lax.ppermute(values, ALL, shifted(dz, dy))]
    pallas_call x4, Pallas kernels: 8.13 us -> 5.13 us  [call(): pl.pallas_call(body, out_shape=out_shape, in_specs=[spec] * len(args), ou...]
    ppermute x7, waiting for transfers between devices: 15 us -> 12.9 us  [send(): return lax.ppermute(values, ALL, shifted(dz, dy))]
    pallas_call x2 -> x3, Pallas kernels: 8.4 us -> 8.08 us  [the longest x1 5.33 us: on_device(): pl.pallas_call(lambda *refs: final_kernel(count, *refs), out_shape=(pltpu...]
  transfers between devices with their start and end apart: 9 -> 9, of which waited for: 4 -> 3; matrix products, arithmetic and copies ran while one was open for 0% -> 0% of each run, Pallas kernels for 6% -> 3%
where the time goes in v3:
time: 139 us
  starting transfers between devices  58.4 us (42%)
  waiting for transfers between devices  33.3 us (24%)
  blocking collectives  32.9 us (24%)
  Pallas kernels  13.5 us (10%)
    all_to_all x2, starting transfers between devices, swap(): return lax.all_to_all(values, 'expert', 0, 0, tiled=True)  34.3 us
    all_gather x1, blocking collectives, on_device(): lax.all_gather(joined, ALL, axis=0, tiled=True, axis_index_groups=far_gro...  32.9 us
    ppermute x7, starting transfers between devices, send(): return lax.ppermute(values, ALL, shifted(dz, dy))  24.1 us
    all_to_all x2, waiting for transfers between devices, swap(): return lax.all_to_all(values, 'expert', 0, 0, tiled=True)  20.4 us
    ppermute x7, waiting for transfers between devices, send(): return lax.ppermute(values, ALL, shifted(dz, dy))  12.9 us
    pallas_call x1, Pallas kernels, on_device(): pl.pallas_call(lambda *refs: final_kernel(count, *refs), out_shape=(pltpu...  5.33 us
    pallas_call x4, Pallas kernels, call(): pl.pallas_call(body, out_shape=out_shape, in_specs=[spec] * len(args), ou...  5.13 us
  transfers between devices with their start and end apart: 9, of which 3 were waited for; matrix products, arithmetic and copies ran while one was open for 0% of the time, Pallas kernels for 3%

profile of v3, /device:TPU:1, one launch (start us, length us, event | category | flops | bytes accessed | tf_op | source)
XLA Modules:
  0.0 138.9 jit_solution(4563305791751825165)
XLA Ops:
  0.6 2.7 %pack.1 = (bf16[8,96,1024]{2,1,0:T(8,128)(2,1)}, bf16[8,2304]{1,0:T(8,128)(2,1)S(1)}) custom-call(bf16[1,8,768]{2,1,0:T(8,128)(2,1)} %refs_0_.1, bf16[1,8,768]{2,1,0:T(8,128)(2,1)} %refs_1_.1, bf16[1,8,768]{2,1,0:T(8,128)(2,1)} %refs_2_.1, s32[2,128]{1,0:T(2,128)} %bitcast.3, f32[2,128]{1,0:T(2,128)} %bitcast.5, bf16[128,1024]{1,0:T(8,128)(2,1)} %refs_5_.1, ...), custom_call_target="tpu_custom_call" | custom-call | tf_op jit(solution)/shard_map/pack/pallas_call | solution.py:289
  3.4 17.6 %all-to-all-start = ((bf16[8,96,1024]{2,1,0:T(8,128)(2,1)}), bf16[8,96,1024]{2,1,0:T(8,128)(2,1)S(1)}, u32[]{:S(2)}, u32[]{:S(2)}) async-start(bf16[8,96,1024]{2,1,0:T(8,128)(2,1)} %get-tuple-element.17), calls=%async_computation | async-start | bytes 3145728 | tf_op jit(solution)/shard_map/all_to_all | solution.py:278
  21.0 32.9 %all_gather.3.refs_0_ = bf16[128,2304]{1,0:T(8,128)(2,1)S(1)} all-gather(bf16[8,2304]{1,0:T(8,128)(2,1)S(1)} %get-tuple-element.20), channel_id=1, replica_groups={{0,64,128,192,256,320,384,448,512,576,640,704,768,832,896,960},{961,897..., dimensions={0}, use_global_device_ids=true | all-gather | bytes 626688 | tf_op jit(solution)/shard_map/all_gather | solution.py:304
  53.9 0.0 all-to-all-done.rows_ref.refs_1_
  53.9 3.5 %collective-permute-start.1 = (bf16[128,2304]{1,0:T(8,128)(2,1)S(1)}, bf16[128,2304]{1,0:T(8,128)(2,1)S(1)}, u32[]{:S(2)}, u32[]{:S(2)}) collective-permute-start(bf16[128,2304]{1,0:T(8,128)(2,1)S(1)} %after.1.refs_0_.refs_6_), channel_id=1, source_target_pairs={{0,8},{1,25},{2,10},{3,27},{4,12},{5,29},{6,14},{7,31},{8,16},{9,1... | collective-permute-start | bytes 1769480 | tf_op jit(solution)/shard_map/ppermute | solution.py:281
  57.5 4.5 %collective-permute-start = (bf16[128,2304]{1,0:T(8,128)(2,1)S(1)}, bf16[128,2304]{1,0:T(8,128)(2,1)S(1)}, u32[]{:S(2)}, u32[]{:S(2)}) collective-permute-start(bf16[128,2304]{1,0:T(8,128)(2,1)S(1)} %after.1.refs_0_.refs_6_), channel_id=1, source_target_pairs={{0,32},{1,993},{2,34},{3,995},{4,36},{5,997},{6,38},{7,999},{8,40}... | collective-permute-start | bytes 1769480 | tf_op jit(solution)/shard_map/ppermute | solution.py:281
  62.0 2.5 %collective-permute-done.1.refs_2_.refs_8_ = bf16[128,2304]{1,0:T(8,128)(2,1)S(1)} collective-permute-done((bf16[128,2304]{1,0:T(8,128)(2,1)S(1)}, bf16[128,2304]{1,0:T(8,128)(2,1)S(1)}, u32[]{:S(2)}, u32[]{:S(2)}) %collective-permute-start.1) | collective-permute-done | bytes 589856 | tf_op jit(solution)/shard_map/ppermute | solution.py:281
  64.6 4.7 %collective-permute-start.5 = (bf16[128,2304]{1,0:T(8,128)(2,1)S(1)}, bf16[128,2304]{1,0:T(8,128)(2,1)S(1)}, u32[]{:S(2)}, u32[]{:S(2)}) collective-permute-start(bf16[128,2304]{1,0:T(8,128)(2,1)S(1)} %collective-permute-done.1.refs_2_.refs_8_), channel_id=1, source_target_pairs={{0,8},{1,25},{2,10},{3,27},{4,12},{5,29},{6,14},{7,31},{8,16},{9,1... | collective-permute-start | bytes 1769480 | tf_op jit(solution)/shard_map/ppermute | solution.py:281
  69.3 1.9 %collective-permute-start.3 = (bf16[128,2304]{1,0:T(8,128)(2,1)S(1)}, bf16[128,2304]{1,0:T(8,128)(2,1)S(1)}, u32[]{:S(2)}, u32[]{:S(2)}) collective-permute-start(bf16[128,2304]{1,0:T(8,128)(2,1)S(1)} %after.1.refs_0_.refs_6_), channel_id=1, source_target_pairs={{0,24},{1,9},{2,26},{3,11},{4,28},{5,13},{6,30},{7,15},{8,0},{9,17... | collective-permute-start | bytes 1769480 | tf_op jit(solution)/shard_map/ppermute | solution.py:281
  71.2 4.5 %collective-permute-start.2 = (bf16[128,2304]{1,0:T(8,128)(2,1)S(1)}, bf16[128,2304]{1,0:T(8,128)(2,1)S(1)}, u32[]{:S(2)}, u32[]{:S(2)}) collective-permute-start(bf16[128,2304]{1,0:T(8,128)(2,1)S(1)} %collective-permute-done.1.refs_2_.refs_8_), channel_id=1, source_target_pairs={{0,32},{1,993},{2,34},{3,995},{4,36},{5,997},{6,38},{7,999},{8,40}... | collective-permute-start | bytes 1769480 | tf_op jit(solution)/shard_map/ppermute | solution.py:281
  75.8 0.0 collective-permute-done.refs_1_.refs_7_
  75.8 1.9 %collective-permute-start.4 = (bf16[128,2304]{1,0:T(8,128)(2,1)S(1)}, bf16[128,2304]{1,0:T(8,128)(2,1)S(1)}, u32[]{:S(2)}, u32[]{:S(2)}) collective-permute-start(bf16[128,2304]{1,0:T(8,128)(2,1)S(1)} %collective-permute-done.refs_1_.refs_7_), channel_id=1, source_target_pairs={{0,24},{1,9},{2,26},{3,11},{4,28},{5,13},{6,30},{7,15},{8,0},{9,17... | collective-permute-start | bytes 1769480 | tf_op jit(solution)/shard_map/ppermute | solution.py:281
  77.7 0.0 collective-permute-done.5.refs_12_
  77.7 2.9 %collective-permute-start.6 = (bf16[128,2304]{1,0:T(8,128)(2,1)S(1)}, bf16[128,2304]{1,0:T(8,128)(2,1)S(1)}, u32[]{:S(2)}, u32[]{:S(2)}) collective-permute-start(bf16[128,2304]{1,0:T(8,128)(2,1)S(1)} %collective-permute-done.5.refs_12_), channel_id=1, source_target_pairs={{0,32},{1,993},{2,34},{3,995},{4,36},{5,997},{6,38},{7,999},{8,40}... | collective-permute-start | bytes 1769480 | tf_op jit(solution)/shard_map/ppermute | solution.py:281
  80.6 0.4 order.1.order_ref.refs_2_
  81.1 1.8 %turn.1 = (bf16[384,1024]{1,0:T(8,128)(2,1)S(1)}, bf16[384,1024]{1,0:T(8,128)(2,1)S(1)}) custom-call(bf16[8,96,1024]{2,1,0:T(8,128)(2,1)S(1)} %all-to-all-done.rows_ref.refs_1_, bf16[1024,1024]{1,0:T(8,128)(2,1)S(1)} %order.1.order_ref.refs_2_), custom_call_target="tpu_custom_call" | custom-call | tf_op jit(solution)/shard_map/turn/pallas_call | solution.py:17
  82.9 0.0 collective-permute-done.3.refs_4_.refs_10_
  82.9 0.0 collective-permute-done.2.refs_3_.refs_9_
  82.9 10.3 %collective-permute-done.4.refs_5_.refs_11_ = bf16[128,2304]{1,0:T(8,128)(2,1)S(1)} collective-permute-done((bf16[128,2304]{1,0:T(8,128)(2,1)S(1)}, bf16[128,2304]{1,0:T(8,128)(2,1)S(1)}, u32[]{:S(2)}, u32[]{:S(2)}) %collective-permute-start.4) | collective-permute-done | bytes 589856 | tf_op jit(solution)/shard_map/ppermute | solution.py:281
  93.2 1.5 %partial.1 = (f32[384,768]{1,0:T(8,128)S(1)}, f32[384,768]{1,0:T(8,128)S(1)}, f32[384,768]{1,0:T(8,128)S(1)}) custom-call(bf16[384,1024]{1,0:T(8,128)(2,1)S(1)} %get-tuple-element.18.tok_ref.refs_0_, bf16[384,1024]{1,0:T(8,128)(2,1)S(1)} %get-tuple-element.19.grad_ref.refs_1_, bf16[128,2304]{1,0:T(8,128)(2,1)S(1)} %after.1.refs_0_.refs_6_, ...), custom_call_target="tpu_custom_call" | custom-call | tf_op jit(solution)/shard_map/partial/pallas_call | solution.py:17
  94.8 0.0 collective-permute-done.6.refs_13_
  94.8 5.3 %final.1 = (bf16[8,96,1024]{2,1,0:T(8,128)(2,1)}, f32[8,128]{1,0:T(8,128)S(1)}) custom-call(bf16[384,1024]{1,0:T(8,128)(2,1)S(1)} %get-tuple-element.18.tok_ref.refs_0_, bf16[384,1024]{1,0:T(8,128)(2,1)S(1)} %get-tuple-element.19.grad_ref.refs_1_, bf16[1024,1024]{1,0:T(8,128)(2,1)S(1)} %order.1.order_ref.refs_2_, f32[384,768]{1,0:T(8,128)S(1)} %get-tuple-element.21.refs_3_, ...), custom_call_target="tpu_custom_call" | custom-call | tf_op jit(solution)/shard_map/final/pallas_call | solution.py:315
  100.1 0.0 copy-start.1
  100.1 0.0 copy-start.2
  100.1 0.0 copy-start
  100.1 16.7 %all-to-all-start.1 = ((bf16[8,96,1024]{2,1,0:T(8,128)(2,1)}), bf16[8,96,1024]{2,1,0:T(8,128)(2,1)S(1)}, u32[]{:S(2)}, u32[]{:S(2)}) async-start(bf16[8,96,1024]{2,1,0:T(8,128)(2,1)} %get-tuple-element.27), calls=%async_computation.1 | async-start | bytes 3145728 | tf_op jit(solution)/shard_map/all_to_all | solution.py:278
  116.8 0.0 copy-done.1
  116.8 0.0 copy-done.2
  116.8 0.3 pick.1
  117.1 20.4 %all-to-all-done.1.back_ref = bf16[8,96,1024]{2,1,0:T(8,128)(2,1)S(1)} async-done(((bf16[8,96,1024]{2,1,0:T(8,128)(2,1)}), bf16[8,96,1024]{2,1,0:T(8,128)(2,1)S(1)}, u32[]{:S(2)}, u32[]{:S(2)}) %all-to-all-start.1) | async-done | bytes 1572896 | tf_op jit(solution)/shard_map/all_to_all | solution.py:278
  137.5 0.0 copy-done
  137.5 1.4 post.1
  (1 shorter events, 0.0 us)
Async XLA Ops:
  3.4 50.6 %all-to-all-start = ((bf16[8,96,1024]{2,1,0:T(8,128)(2,1)}), bf16[8,96,1024]{2,1,0:T(8,128)(2,1)S(1)}, u32[]{:S(2)}, u32[]{:S(2)}) async-start(bf16[8,96,1024]{2,1,0:T(8,128)(2,1)} %get-tuple-element.17), calls=%async_computation | async-start | bytes 3145728 | tf_op jit(solution)/shard_map/all_to_all | solution.py:278
  53.9 10.6 %collective-permute-start.1 = (bf16[128,2304]{1,0:T(8,128)(2,1)S(1)}, bf16[128,2304]{1,0:T(8,128)(2,1)S(1)}, u32[]{:S(2)}, u32[]{:S(2)}) collective-permute-start(bf16[128,2304]{1,0:T(8,128)(2,1)S(1)} %after.1.refs_0_.refs_6_), channel_id=1, source_target_pairs={{0,8},{1,25},{2,10},{3,27},{4,12},{5,29},{6,14},{7,31},{8,16},{9,1... | collective-permute-start | bytes 1769480 | tf_op jit(solution)/shard_map/ppermute | solution.py:281
  57.5 18.3 %collective-permute-start = (bf16[128,2304]{1,0:T(8,128)(2,1)S(1)}, bf16[128,2304]{1,0:T(8,128)(2,1)S(1)}, u32[]{:S(2)}, u32[]{:S(2)}) collective-permute-start(bf16[128,2304]{1,0:T(8,128)(2,1)S(1)} %after.1.refs_0_.refs_6_), channel_id=1, source_target_pairs={{0,32},{1,993},{2,34},{3,995},{4,36},{5,997},{6,38},{7,999},{8,40}... | collective-permute-start | bytes 1769480 | tf_op jit(solution)/shard_map/ppermute | solution.py:281
  64.6 13.2 %collective-permute-start.5 = (bf16[128,2304]{1,0:T(8,128)(2,1)S(1)}, bf16[128,2304]{1,0:T(8,128)(2,1)S(1)}, u32[]{:S(2)}, u32[]{:S(2)}) collective-permute-start(bf16[128,2304]{1,0:T(8,128)(2,1)S(1)} %collective-permute-done.1.refs_2_.refs_8_), channel_id=1, source_target_pairs={{0,8},{1,25},{2,10},{3,27},{4,12},{5,29},{6,14},{7,31},{8,16},{9,1... | collective-permute-start | bytes 1769480 | tf_op jit(solution)/shard_map/ppermute | solution.py:281
  69.3 13.6 %collective-permute-start.3 = (bf16[128,2304]{1,0:T(8,128)(2,1)S(1)}, bf16[128,2304]{1,0:T(8,128)(2,1)S(1)}, u32[]{:S(2)}, u32[]{:S(2)}) collective-permute-start(bf16[128,2304]{1,0:T(8,128)(2,1)S(1)} %after.1.refs_0_.refs_6_), channel_id=1, source_target_pairs={{0,24},{1,9},{2,26},{3,11},{4,28},{5,13},{6,30},{7,15},{8,0},{9,17... | collective-permute-start | bytes 1769480 | tf_op jit(solution)/shard_map/ppermute | solution.py:281
  71.2 11.7 %collective-permute-start.2 = (bf16[128,2304]{1,0:T(8,128)(2,1)S(1)}, bf16[128,2304]{1,0:T(8,128)(2,1)S(1)}, u32[]{:S(2)}, u32[]{:S(2)}) collective-permute-start(bf16[128,2304]{1,0:T(8,128)(2,1)S(1)} %collective-permute-done.1.refs_2_.refs_8_), channel_id=1, source_target_pairs={{0,32},{1,993},{2,34},{3,995},{4,36},{5,997},{6,38},{7,999},{8,40}... | collective-permute-start | bytes 1769480 | tf_op jit(solution)/shard_map/ppermute | solution.py:281
  75.8 17.4 %collective-permute-start.4 = (bf16[128,2304]{1,0:T(8,128)(2,1)S(1)}, bf16[128,2304]{1,0:T(8,128)(2,1)S(1)}, u32[]{:S(2)}, u32[]{:S(2)}) collective-permute-start(bf16[128,2304]{1,0:T(8,128)(2,1)S(1)} %collective-permute-done.refs_1_.refs_7_), channel_id=1, source_target_pairs={{0,24},{1,9},{2,26},{3,11},{4,28},{5,13},{6,30},{7,15},{8,0},{9,17... | collective-permute-start | bytes 1769480 | tf_op jit(solution)/shard_map/ppermute | solution.py:281
  77.7 17.0 %collective-permute-start.6 = (bf16[128,2304]{1,0:T(8,128)(2,1)S(1)}, bf16[128,2304]{1,0:T(8,128)(2,1)S(1)}, u32[]{:S(2)}, u32[]{:S(2)}) collective-permute-start(bf16[128,2304]{1,0:T(8,128)(2,1)S(1)} %collective-permute-done.5.refs_12_), channel_id=1, source_target_pairs={{0,32},{1,993},{2,34},{3,995},{4,36},{5,997},{6,38},{7,999},{8,40}... | collective-permute-start | bytes 1769480 | tf_op jit(solution)/shard_map/ppermute | solution.py:281
  100.1 16.7 %copy-start.1 = (s32[128,2]{0,1:T(2,128)S(1)}, s32[128,2]{0,1:T(2,128)}, u32[]{:S(2)}) copy-start(s32[128,2]{0,1:T(2,128)} %param.8) | copy-start | bytes 3076
  100.1 16.7 %copy-start.2 = (f32[128,2]{0,1:T(2,128)S(1)}, f32[128,2]{0,1:T(2,128)}, u32[]{:S(2)}) copy-start(f32[128,2]{0,1:T(2,128)} %param.9) | copy-start | bytes 3076
  100.1 37.4 %copy-start = (bf16[128,1024]{1,0:T(8,128)(2,1)S(1)}, bf16[128,1024]{1,0:T(8,128)(2,1)}, u32[]{:S(2)}) copy-start(bf16[128,1024]{1,0:T(8,128)(2,1)} %cot_ref.1) | copy-start | bytes 786436
  100.1 37.4 %all-to-all-start.1 = ((bf16[8,96,1024]{2,1,0:T(8,128)(2,1)}), bf16[8,96,1024]{2,1,0:T(8,128)(2,1)S(1)}, u32[]{:S(2)}, u32[]{:S(2)}) async-start(bf16[8,96,1024]{2,1,0:T(8,128)(2,1)} %get-tuple-element.27), calls=%async_computation.1 | async-start | bytes 3145728 | tf_op jit(solution)/shard_map/all_to_all | solution.py:278

commit v4 on v3

--- a/solution.py
+++ b/solution.py
@@ -305,7 +305,7 @@
     own = after(own, arrived)
     ahead, beside, behind = send(own, 0, 1), send(own, 1, 0), send(own, 0, -1)
     across = send(ahead, 0, 1)
-    pieces = [own, beside, ahead, send(ahead, 1, 0), behind, send(beside, 0, -1)]
+    pieces = [own, beside, ahead, send(beside, 0, 1), behind, send(behind, 1, 0)]
     pieces += [across, send(across, 1, 0)]
     count = len(pieces)
     order = call(lambda ref: order_kernel(zs, ref), "order", shape((width, width), BF16))

time: 139 us -> 135 us (0.971)
  waiting for transfers between devices: 33.3 us -> 28.5 us
    ppermute x7, waiting for transfers between devices: 12.9 us -> 8.12 us  [send(): return lax.ppermute(values, ALL, shifted(dz, dy))]
    ppermute x7, starting transfers between devices: 24.1 us -> 27 us  [send(): return lax.ppermute(values, ALL, shifted(dz, dy))]
    all_to_all x2, starting transfers between devices: 34.3 us -> 32.2 us  [swap(): return lax.all_to_all(values, 'expert', 0, 0, tiled=True)]
  transfers between devices with their start and end apart: 9 -> 9, of which waited for: 3 -> 6; matrix products, arithmetic and copies ran while one was open for 0% -> 0% of each run, Pallas kernels for 3% -> 3%
where the time goes in v4:
time: 135 us
  starting transfers between devices  59.2 us (44%)
  blocking collectives  32.9 us (24%)
  waiting for transfers between devices  28.5 us (21%)
  Pallas kernels  13.5 us (10%)
    all_gather x1, blocking collectives, on_device(): lax.all_gather(joined, ALL, axis=0, tiled=True, axis_index_groups=far_gro...  32.9 us
    all_to_all x2, starting transfers between devices, swap(): return lax.all_to_all(values, 'expert', 0, 0, tiled=True)  32.2 us
    ppermute x7, starting transfers between devices, send(): return lax.ppermute(values, ALL, shifted(dz, dy))  27 us
    all_to_all x2, waiting for transfers between devices, swap(): return lax.all_to_all(values, 'expert', 0, 0, tiled=True)  20.4 us
    ppermute x7, waiting for transfers between devices, send(): return lax.ppermute(values, ALL, shifted(dz, dy))  8.12 us
    pallas_call x1, Pallas kernels, on_device(): pl.pallas_call(lambda *refs: final_kernel(count, *refs), out_shape=(pltpu...  5.34 us
    pallas_call x4, Pallas kernels, call(): pl.pallas_call(body, out_shape=out_shape, in_specs=[spec] * len(args), ou...  5.13 us
    pallas_call x1, Pallas kernels, on_device(): pl.pallas_call(pack_kernel, out_shape=(both, shape((depth, 3 * ff), BF16)...  2.74 us
  transfers between devices with their start and end apart: 9, of which 6 were waited for; matrix products, arithmetic and copies ran while one was open for 0% of the time, Pallas kernels for 3%

profile of v4, /device:TPU:1, one launch (start us, length us, event | category | flops | bytes accessed | tf_op | source)
XLA Modules:
  0.0 134.9 jit_solution(17058814635144141396)
XLA Ops:
  0.6 2.7 %pack.1 = (bf16[8,96,1024]{2,1,0:T(8,128)(2,1)}, bf16[8,2304]{1,0:T(8,128)(2,1)S(1)}) custom-call(bf16[1,8,768]{2,1,0:T(8,128)(2,1)} %refs_0_.1, bf16[1,8,768]{2,1,0:T(8,128)(2,1)} %refs_1_.1, bf16[1,8,768]{2,1,0:T(8,128)(2,1)} %refs_2_.1, s32[2,128]{1,0:T(2,128)} %bitcast.3, f32[2,128]{1,0:T(2,128)} %bitcast.5, bf16[128,1024]{1,0:T(8,128)(2,1)} %refs_5_.1, ...), custom_call_target="tpu_custom_call" | custom-call | tf_op jit(solution)/shard_map/pack/pallas_call | solution.py:289
  3.4 17.6 %all-to-all-start = ((bf16[8,96,1024]{2,1,0:T(8,128)(2,1)}), bf16[8,96,1024]{2,1,0:T(8,128)(2,1)S(1)}, u32[]{:S(2)}, u32[]{:S(2)}) async-start(bf16[8,96,1024]{2,1,0:T(8,128)(2,1)} %get-tuple-element.17), calls=%async_computation | async-start | bytes 3145728 | tf_op jit(solution)/shard_map/all_to_all | solution.py:278
  21.0 32.9 %all_gather.3.refs_0_ = bf16[128,2304]{1,0:T(8,128)(2,1)S(1)} all-gather(bf16[8,2304]{1,0:T(8,128)(2,1)S(1)} %get-tuple-element.20), channel_id=1, replica_groups={{0,64,128,192,256,320,384,448,512,576,640,704,768,832,896,960},{961,897..., dimensions={0}, use_global_device_ids=true | all-gather | bytes 626688 | tf_op jit(solution)/shard_map/all_gather | solution.py:304
  53.9 0.0 all-to-all-done.rows_ref.refs_1_
  53.9 3.5 %collective-permute-start.1 = (bf16[128,2304]{1,0:T(8,128)(2,1)S(1)}, bf16[128,2304]{1,0:T(8,128)(2,1)S(1)}, u32[]{:S(2)}, u32[]{:S(2)}) collective-permute-start(bf16[128,2304]{1,0:T(8,128)(2,1)S(1)} %after.1.refs_0_.refs_6_), channel_id=1, source_target_pairs={{0,8},{1,25},{2,10},{3,27},{4,12},{5,29},{6,14},{7,31},{8,16},{9,1... | collective-permute-start | bytes 1769480 | tf_op jit(solution)/shard_map/ppermute | solution.py:281
  57.5 1.9 %collective-permute-start.3 = (bf16[128,2304]{1,0:T(8,128)(2,1)S(1)}, bf16[128,2304]{1,0:T(8,128)(2,1)S(1)}, u32[]{:S(2)}, u32[]{:S(2)}) collective-permute-start(bf16[128,2304]{1,0:T(8,128)(2,1)S(1)} %after.1.refs_0_.refs_6_), channel_id=1, source_target_pairs={{0,24},{1,9},{2,26},{3,11},{4,28},{5,13},{6,30},{7,15},{8,0},{9,17... | collective-permute-start | bytes 1769480 | tf_op jit(solution)/shard_map/ppermute | solution.py:281
  59.4 4.5 %collective-permute-start = (bf16[128,2304]{1,0:T(8,128)(2,1)S(1)}, bf16[128,2304]{1,0:T(8,128)(2,1)S(1)}, u32[]{:S(2)}, u32[]{:S(2)}) collective-permute-start(bf16[128,2304]{1,0:T(8,128)(2,1)S(1)} %after.1.refs_0_.refs_6_), channel_id=1, source_target_pairs={{0,32},{1,993},{2,34},{3,995},{4,36},{5,997},{6,38},{7,999},{8,40}... | collective-permute-start | bytes 1769480 | tf_op jit(solution)/shard_map/ppermute | solution.py:281
  64.0 0.6 collective-permute-done.1.refs_2_.refs_8_
  64.6 4.7 %collective-permute-start.5 = (bf16[128,2304]{1,0:T(8,128)(2,1)S(1)}, bf16[128,2304]{1,0:T(8,128)(2,1)S(1)}, u32[]{:S(2)}, u32[]{:S(2)}) collective-permute-start(bf16[128,2304]{1,0:T(8,128)(2,1)S(1)} %collective-permute-done.1.refs_2_.refs_8_), channel_id=1, source_target_pairs={{0,8},{1,25},{2,10},{3,27},{4,12},{5,29},{6,14},{7,31},{8,16},{9,1... | collective-permute-start | bytes 1769480 | tf_op jit(solution)/shard_map/ppermute | solution.py:281
  69.3 1.1 collective-permute-done.3.refs_4_.refs_10_
  70.4 7.5 %collective-permute-start.4 = (bf16[128,2304]{1,0:T(8,128)(2,1)S(1)}, bf16[128,2304]{1,0:T(8,128)(2,1)S(1)}, u32[]{:S(2)}, u32[]{:S(2)}) collective-permute-start(bf16[128,2304]{1,0:T(8,128)(2,1)S(1)} %collective-permute-done.3.refs_4_.refs_10_), channel_id=1, source_target_pairs={{0,32},{1,993},{2,34},{3,995},{4,36},{5,997},{6,38},{7,999},{8,40}... | collective-permute-start | bytes 1769480 | tf_op jit(solution)/shard_map/ppermute | solution.py:281
  77.9 0.0 collective-permute-done.refs_1_.refs_7_
  77.9 1.9 %collective-permute-start.2 = (bf16[128,2304]{1,0:T(8,128)(2,1)S(1)}, bf16[128,2304]{1,0:T(8,128)(2,1)S(1)}, u32[]{:S(2)}, u32[]{:S(2)}) collective-permute-start(bf16[128,2304]{1,0:T(8,128)(2,1)S(1)} %collective-permute-done.refs_1_.refs_7_), channel_id=1, source_target_pairs={{0,8},{1,25},{2,10},{3,27},{4,12},{5,29},{6,14},{7,31},{8,16},{9,1... | collective-permute-start | bytes 1769480 | tf_op jit(solution)/shard_map/ppermute | solution.py:281
  79.8 2.3 %collective-permute-done.5.refs_12_ = bf16[128,2304]{1,0:T(8,128)(2,1)S(1)} collective-permute-done((bf16[128,2304]{1,0:T(8,128)(2,1)S(1)}, bf16[128,2304]{1,0:T(8,128)(2,1)S(1)}, u32[]{:S(2)}, u32[]{:S(2)}) %collective-permute-start.5) | collective-permute-done | bytes 589856 | tf_op jit(solution)/shard_map/ppermute | solution.py:281
  82.1 2.9 %collective-permute-start.6 = (bf16[128,2304]{1,0:T(8,128)(2,1)S(1)}, bf16[128,2304]{1,0:T(8,128)(2,1)S(1)}, u32[]{:S(2)}, u32[]{:S(2)}) collective-permute-start(bf16[128,2304]{1,0:T(8,128)(2,1)S(1)} %collective-permute-done.5.refs_12_), channel_id=1, source_target_pairs={{0,32},{1,993},{2,34},{3,995},{4,36},{5,997},{6,38},{7,999},{8,40}... | collective-permute-start | bytes 1769480 | tf_op jit(solution)/shard_map/ppermute | solution.py:281
  85.0 0.4 order.1.order_ref.refs_2_
  85.4 1.8 %turn.1 = (bf16[384,1024]{1,0:T(8,128)(2,1)S(1)}, bf16[384,1024]{1,0:T(8,128)(2,1)S(1)}) custom-call(bf16[8,96,1024]{2,1,0:T(8,128)(2,1)S(1)} %all-to-all-done.rows_ref.refs_1_, bf16[1024,1024]{1,0:T(8,128)(2,1)S(1)} %order.1.order_ref.refs_2_), custom_call_target="tpu_custom_call" | custom-call | tf_op jit(solution)/shard_map/turn/pallas_call | solution.py:17
  87.2 0.0 collective-permute-done.4.refs_5_.refs_11_
  87.3 1.5 %collective-permute-done.2.refs_3_.refs_9_ = bf16[128,2304]{1,0:T(8,128)(2,1)S(1)} collective-permute-done((bf16[128,2304]{1,0:T(8,128)(2,1)S(1)}, bf16[128,2304]{1,0:T(8,128)(2,1)S(1)}, u32[]{:S(2)}, u32[]{:S(2)}) %collective-permute-start.2) | collective-permute-done | bytes 589856 | tf_op jit(solution)/shard_map/ppermute | solution.py:281
  88.8 1.5 %partial.1 = (f32[384,768]{1,0:T(8,128)S(1)}, f32[384,768]{1,0:T(8,128)S(1)}, f32[384,768]{1,0:T(8,128)S(1)}) custom-call(bf16[384,1024]{1,0:T(8,128)(2,1)S(1)} %get-tuple-element.18.tok_ref.refs_0_, bf16[384,1024]{1,0:T(8,128)(2,1)S(1)} %get-tuple-element.19.grad_ref.refs_1_, bf16[128,2304]{1,0:T(8,128)(2,1)S(1)} %after.1.refs_0_.refs_6_, ...), custom_call_target="tpu_custom_call" | custom-call | tf_op jit(solution)/shard_map/partial/pallas_call | solution.py:17
  90.3 2.6 %collective-permute-done.6.refs_13_ = bf16[128,2304]{1,0:T(8,128)(2,1)S(1)} collective-permute-done((bf16[128,2304]{1,0:T(8,128)(2,1)S(1)}, bf16[128,2304]{1,0:T(8,128)(2,1)S(1)}, u32[]{:S(2)}, u32[]{:S(2)}) %collective-permute-start.6) | collective-permute-done | bytes 589856 | tf_op jit(solution)/shard_map/ppermute | solution.py:281
  93.0 5.3 %final.1 = (bf16[8,96,1024]{2,1,0:T(8,128)(2,1)}, f32[8,128]{1,0:T(8,128)S(1)}) custom-call(bf16[384,1024]{1,0:T(8,128)(2,1)S(1)} %get-tuple-element.18.tok_ref.refs_0_, bf16[384,1024]{1,0:T(8,128)(2,1)S(1)} %get-tuple-element.19.grad_ref.refs_1_, bf16[1024,1024]{1,0:T(8,128)(2,1)S(1)} %order.1.order_ref.refs_2_, f32[384,768]{1,0:T(8,128)S(1)} %get-tuple-element.21.refs_3_, ...), custom_call_target="tpu_custom_call" | custom-call | tf_op jit(solution)/shard_map/final/pallas_call | solution.py:315
  98.3 0.0 copy-start.1
  98.3 0.0 copy-start.2
  98.3 0.0 copy-start
  98.4 14.5 %all-to-all-start.1 = ((bf16[8,96,1024]{2,1,0:T(8,128)(2,1)}), bf16[8,96,1024]{2,1,0:T(8,128)(2,1)S(1)}, u32[]{:S(2)}, u32[]{:S(2)}) async-start(bf16[8,96,1024]{2,1,0:T(8,128)(2,1)} %get-tuple-element.27), calls=%async_computation.1 | async-start | bytes 3145728 | tf_op jit(solution)/shard_map/all_to_all | solution.py:278
  112.9 0.0 copy-done.1
  112.9 0.0 copy-done.2
  112.9 0.3 pick.1
  113.2 20.4 %all-to-all-done.1.back_ref = bf16[8,96,1024]{2,1,0:T(8,128)(2,1)S(1)} async-done(((bf16[8,96,1024]{2,1,0:T(8,128)(2,1)}), bf16[8,96,1024]{2,1,0:T(8,128)(2,1)S(1)}, u32[]{:S(2)}, u32[]{:S(2)}) %all-to-all-start.1) | async-done | bytes 1572896 | tf_op jit(solution)/shard_map/all_to_all | solution.py:278
  133.6 0.0 copy-done
  133.6 1.4 %post.1 = (bf16[128,1024]{1,0:T(8,128)(2,1)}, bf16[128,1024]{1,0:T(8,128)(2,1)}, f32[2,128]{1,0:T(2,128)}) custom-call(bf16[2,128,384]{2,1,0:T(8,128)(2,1)S(1)} %get-tuple-element.25.pick_ref, f32[128,128]{1,0:T(8,128)S(1)} %get-tuple-element.26.ccol_ref, bf16[128,1024]{1,0:T(8,128)(2,1)S(1)} %copy-done, bf16[8,96,1024]{2,1,0:T(8,128)(2,1)S(1)} %all-to-all-done.1.back_ref), custom_call_target="tpu_custom_call" | custom-call | tf_op jit(solution)/shard_map/post/pallas_call | solution.py:17
  (1 shorter events, 0.0 us)
Async XLA Ops:
  3.4 50.6 %all-to-all-start = ((bf16[8,96,1024]{2,1,0:T(8,128)(2,1)}), bf16[8,96,1024]{2,1,0:T(8,128)(2,1)S(1)}, u32[]{:S(2)}, u32[]{:S(2)}) async-start(bf16[8,96,1024]{2,1,0:T(8,128)(2,1)} %get-tuple-element.17), calls=%async_computation | async-start | bytes 3145728 | tf_op jit(solution)/shard_map/all_to_all | solution.py:278
  53.9 10.6 %collective-permute-start.1 = (bf16[128,2304]{1,0:T(8,128)(2,1)S(1)}, bf16[128,2304]{1,0:T(8,128)(2,1)S(1)}, u32[]{:S(2)}, u32[]{:S(2)}) collective-permute-start(bf16[128,2304]{1,0:T(8,128)(2,1)S(1)} %after.1.refs_0_.refs_6_), channel_id=1, source_target_pairs={{0,8},{1,25},{2,10},{3,27},{4,12},{5,29},{6,14},{7,31},{8,16},{9,1... | collective-permute-start | bytes 1769480 | tf_op jit(solution)/shard_map/ppermute | solution.py:281
  57.5 12.9 %collective-permute-start.3 = (bf16[128,2304]{1,0:T(8,128)(2,1)S(1)}, bf16[128,2304]{1,0:T(8,128)(2,1)S(1)}, u32[]{:S(2)}, u32[]{:S(2)}) collective-permute-start(bf16[128,2304]{1,0:T(8,128)(2,1)S(1)} %after.1.refs_0_.refs_6_), channel_id=1, source_target_pairs={{0,24},{1,9},{2,26},{3,11},{4,28},{5,13},{6,30},{7,15},{8,0},{9,17... | collective-permute-start | bytes 1769480 | tf_op jit(solution)/shard_map/ppermute | solution.py:281
  59.4 18.5 %collective-permute-start = (bf16[128,2304]{1,0:T(8,128)(2,1)S(1)}, bf16[128,2304]{1,0:T(8,128)(2,1)S(1)}, u32[]{:S(2)}, u32[]{:S(2)}) collective-permute-start(bf16[128,2304]{1,0:T(8,128)(2,1)S(1)} %after.1.refs_0_.refs_6_), channel_id=1, source_target_pairs={{0,32},{1,993},{2,34},{3,995},{4,36},{5,997},{6,38},{7,999},{8,40}... | collective-permute-start | bytes 1769480 | tf_op jit(solution)/shard_map/ppermute | solution.py:281
  64.6 17.5 %collective-permute-start.5 = (bf16[128,2304]{1,0:T(8,128)(2,1)S(1)}, bf16[128,2304]{1,0:T(8,128)(2,1)S(1)}, u32[]{:S(2)}, u32[]{:S(2)}) collective-permute-start(bf16[128,2304]{1,0:T(8,128)(2,1)S(1)} %collective-permute-done.1.refs_2_.refs_8_), channel_id=1, source_target_pairs={{0,8},{1,25},{2,10},{3,27},{4,12},{5,29},{6,14},{7,31},{8,16},{9,1... | collective-permute-start | bytes 1769480 | tf_op jit(solution)/shard_map/ppermute | solution.py:281
  70.4 16.9 %collective-permute-start.4 = (bf16[128,2304]{1,0:T(8,128)(2,1)S(1)}, bf16[128,2304]{1,0:T(8,128)(2,1)S(1)}, u32[]{:S(2)}, u32[]{:S(2)}) collective-permute-start(bf16[128,2304]{1,0:T(8,128)(2,1)S(1)} %collective-permute-done.3.refs_4_.refs_10_), channel_id=1, source_target_pairs={{0,32},{1,993},{2,34},{3,995},{4,36},{5,997},{6,38},{7,999},{8,40}... | collective-permute-start | bytes 1769480 | tf_op jit(solution)/shard_map/ppermute | solution.py:281
  77.9 10.9 %collective-permute-start.2 = (bf16[128,2304]{1,0:T(8,128)(2,1)S(1)}, bf16[128,2304]{1,0:T(8,128)(2,1)S(1)}, u32[]{:S(2)}, u32[]{:S(2)}) collective-permute-start(bf16[128,2304]{1,0:T(8,128)(2,1)S(1)} %collective-permute-done.refs_1_.refs_7_), channel_id=1, source_target_pairs={{0,8},{1,25},{2,10},{3,27},{4,12},{5,29},{6,14},{7,31},{8,16},{9,1... | collective-permute-start | bytes 1769480 | tf_op jit(solution)/shard_map/ppermute | solution.py:281
  82.1 10.9 %collective-permute-start.6 = (bf16[128,2304]{1,0:T(8,128)(2,1)S(1)}, bf16[128,2304]{1,0:T(8,128)(2,1)S(1)}, u32[]{:S(2)}, u32[]{:S(2)}) collective-permute-start(bf16[128,2304]{1,0:T(8,128)(2,1)S(1)} %collective-permute-done.5.refs_12_), channel_id=1, source_target_pairs={{0,32},{1,993},{2,34},{3,995},{4,36},{5,997},{6,38},{7,999},{8,40}... | collective-permute-start | bytes 1769480 | tf_op jit(solution)/shard_map/ppermute | solution.py:281
  98.3 14.5 %copy-start.1 = (s32[128,2]{0,1:T(2,128)S(1)}, s32[128,2]{0,1:T(2,128)}, u32[]{:S(2)}) copy-start(s32[128,2]{0,1:T(2,128)} %param.8) | copy-start | bytes 3076
  98.3 14.5 %copy-start.2 = (f32[128,2]{0,1:T(2,128)S(1)}, f32[128,2]{0,1:T(2,128)}, u32[]{:S(2)}) copy-start(f32[128,2]{0,1:T(2,128)} %param.9) | copy-start | bytes 3076
  98.3 35.2 %copy-start = (bf16[128,1024]{1,0:T(8,128)(2,1)S(1)}, bf16[128,1024]{1,0:T(8,128)(2,1)}, u32[]{:S(2)}) copy-start(bf16[128,1024]{1,0:T(8,128)(2,1)} %cot_ref.1) | copy-start | bytes 786436
  98.4 35.2 %all-to-all-start.1 = ((bf16[8,96,1024]{2,1,0:T(8,128)(2,1)}), bf16[8,96,1024]{2,1,0:T(8,128)(2,1)S(1)}, u32[]{:S(2)}, u32[]{:S(2)}) async-start(bf16[8,96,1024]{2,1,0:T(8,128)(2,1)} %get-tuple-element.27), calls=%async_computation.1 | async-start | bytes 3145728 | tf_op jit(solution)/shard_map/all_to_all | solution.py:278

commit v5 on v4

--- a/solution.py
+++ b/solution.py
@@ -150,7 +150,7 @@
     step = i // (depth * zs)
     other = lax.rem(i // (depth * (zs // PAR)), PAR)
     zi = jnp.where(core == 0, pos, zs // PAR - 1 - pos)
-    ahead = jnp.where(step == 1, -1, jnp.where(step == 2, 1, step - step // 3))
+    ahead = jnp.where(step == 1, -1, jnp.where(step == 2, 2, step // 3))
     y = lax.rem(my_y + NY + jnp.where(core == 0, ahead, -ahead), NY)
     z = zi * PAR + lax.rem(my_z + other, PAR)
     feature = (z * NY + y) * depth + r
@@ -304,9 +304,8 @@
     own = lax.all_gather(joined, ALL, axis=0, tiled=True, axis_index_groups=far_groups)
     own = after(own, arrived)
     ahead, beside, behind = send(own, 0, 1), send(own, 1, 0), send(own, 0, -1)
-    across = send(ahead, 0, 1)
-    pieces = [own, beside, ahead, send(beside, 0, 1), behind, send(behind, 1, 0)]
-    pieces += [across, send(across, 1, 0)]
+    pieces = [own, beside, ahead, send(ahead, 1, 0), send(ahead, 0, 1), send(ahead, 1, 1)]
+    pieces += [behind, send(behind, 1, 0)]
     count = len(pieces)
     order = call(lambda ref: order_kernel(zs, ref), "order", shape((width, width), BF16))
     rows_shape, sum_shape = shape((slots, width), BF16), shape((slots, ff), F32)

time: 135 us -> 135 us (level)
    ppermute x7, starting transfers between devices: 27 us -> 25.3 us  [send(): return lax.ppermute(values, ALL, shifted(dz, dy))]
  transfers between devices with their start and end apart: 9 -> 9, of which waited for: 6 -> 3; matrix products, arithmetic and copies ran while one was open for 0% -> 0% of each run, Pallas kernels for 3% -> 3%
where the time goes in v5:
time: 135 us; the launch traced here: 134 us
  starting transfers between devices  58.2 us (43%)
  blocking collectives  32.9 us (24%)
  waiting for transfers between devices  28.7 us (21%)
  Pallas kernels  13.5 us (10%)
    all_gather x1, blocking collectives, on_device(): lax.all_gather(joined, ALL, axis=0, tiled=True, axis_index_groups=far_gro...  32.9 us
    all_to_all x2, starting transfers between devices, swap(): return lax.all_to_all(values, 'expert', 0, 0, tiled=True)  32.9 us
    ppermute x7, starting transfers between devices, send(): return lax.ppermute(values, ALL, shifted(dz, dy))  25.3 us
    all_to_all x2, waiting for transfers between devices, swap(): return lax.all_to_all(values, 'expert', 0, 0, tiled=True)  20.4 us
    ppermute x7, waiting for transfers between devices, send(): return lax.ppermute(values, ALL, shifted(dz, dy))  8.21 us
    pallas_call x1, Pallas kernels, on_device(): pl.pallas_call(lambda *refs: final_kernel(count, *refs), out_shape=(pltpu...  5.33 us
    pallas_call x4, Pallas kernels, call(): pl.pallas_call(body, out_shape=out_shape, in_specs=[spec] * len(args), ou...  5.12 us
    pallas_call x1, Pallas kernels, on_device(): pl.pallas_call(pack_kernel, out_shape=(both, shape((depth, 3 * ff), BF16)...  2.74 us
  transfers between devices with their start and end apart: 9, of which 3 were waited for; matrix products, arithmetic and copies ran while one was open for 0% of the time, Pallas kernels for 3%

profile of v5, /device:TPU:1, one launch (start us, length us, event | category | flops | bytes accessed | tf_op | source)
XLA Modules:
  0.0 134.1 jit_solution(952679186614555933)
XLA Ops:
  0.6 2.7 %pack.1 = (bf16[8,96,1024]{2,1,0:T(8,128)(2,1)}, bf16[8,2304]{1,0:T(8,128)(2,1)S(1)}) custom-call(bf16[1,8,768]{2,1,0:T(8,128)(2,1)} %refs_0_.1, bf16[1,8,768]{2,1,0:T(8,128)(2,1)} %refs_1_.1, bf16[1,8,768]{2,1,0:T(8,128)(2,1)} %refs_2_.1, s32[2,128]{1,0:T(2,128)} %bitcast.3, f32[2,128]{1,0:T(2,128)} %bitcast.5, bf16[128,1024]{1,0:T(8,128)(2,1)} %refs_5_.1, ...), custom_call_target="tpu_custom_call" | custom-call | tf_op jit(solution)/shard_map/pack/pallas_call | solution.py:289
  3.4 17.6 %all-to-all-start = ((bf16[8,96,1024]{2,1,0:T(8,128)(2,1)}), bf16[8,96,1024]{2,1,0:T(8,128)(2,1)S(1)}, u32[]{:S(2)}, u32[]{:S(2)}) async-start(bf16[8,96,1024]{2,1,0:T(8,128)(2,1)} %get-tuple-element.17), calls=%async_computation | async-start | bytes 3145728 | tf_op jit(solution)/shard_map/all_to_all | solution.py:278
  21.0 32.9 %all_gather.3.refs_0_ = bf16[128,2304]{1,0:T(8,128)(2,1)S(1)} all-gather(bf16[8,2304]{1,0:T(8,128)(2,1)S(1)} %get-tuple-element.20), channel_id=1, replica_groups={{0,64,128,192,256,320,384,448,512,576,640,704,768,832,896,960},{961,897..., dimensions={0}, use_global_device_ids=true | all-gather | bytes 626688 | tf_op jit(solution)/shard_map/all_gather | solution.py:304
  53.9 0.0 all-to-all-done.rows_ref.refs_1_
  53.9 3.5 %collective-permute-start.1 = (bf16[128,2304]{1,0:T(8,128)(2,1)S(1)}, bf16[128,2304]{1,0:T(8,128)(2,1)S(1)}, u32[]{:S(2)}, u32[]{:S(2)}) collective-permute-start(bf16[128,2304]{1,0:T(8,128)(2,1)S(1)} %after.1.refs_0_.refs_6_), channel_id=1, source_target_pairs={{0,8},{1,25},{2,10},{3,27},{4,12},{5,29},{6,14},{7,31},{8,16},{9,1... | collective-permute-start | bytes 1769480 | tf_op jit(solution)/shard_map/ppermute | solution.py:281
  57.5 1.9 %collective-permute-start.5 = (bf16[128,2304]{1,0:T(8,128)(2,1)S(1)}, bf16[128,2304]{1,0:T(8,128)(2,1)S(1)}, u32[]{:S(2)}, u32[]{:S(2)}) collective-permute-start(bf16[128,2304]{1,0:T(8,128)(2,1)S(1)} %after.1.refs_0_.refs_6_), channel_id=1, source_target_pairs={{0,24},{1,9},{2,26},{3,11},{4,28},{5,13},{6,30},{7,15},{8,0},{9,17... | collective-permute-start | bytes 1769480 | tf_op jit(solution)/shard_map/ppermute | solution.py:281
  59.4 4.5 %collective-permute-start = (bf16[128,2304]{1,0:T(8,128)(2,1)S(1)}, bf16[128,2304]{1,0:T(8,128)(2,1)S(1)}, u32[]{:S(2)}, u32[]{:S(2)}) collective-permute-start(bf16[128,2304]{1,0:T(8,128)(2,1)S(1)} %after.1.refs_0_.refs_6_), channel_id=1, source_target_pairs={{0,32},{1,993},{2,34},{3,995},{4,36},{5,997},{6,38},{7,999},{8,40}... | collective-permute-start | bytes 1769480 | tf_op jit(solution)/shard_map/ppermute | solution.py:281
  64.0 0.6 collective-permute-done.1.refs_2_.refs_8_
  64.6 7.1 %collective-permute-start.4 = (bf16[128,2304]{1,0:T(8,128)(2,1)S(1)}, bf16[128,2304]{1,0:T(8,128)(2,1)S(1)}, u32[]{:S(2)}, u32[]{:S(2)}) collective-permute-start(bf16[128,2304]{1,0:T(8,128)(2,1)S(1)} %collective-permute-done.1.refs_2_.refs_8_), channel_id=1, source_target_pairs={{0,40},{1,1017},{2,42},{3,1019},{4,44},{5,1021},{6,46},{7,1023},{8... | collective-permute-start | bytes 1769480 | tf_op jit(solution)/shard_map/ppermute | solution.py:281
  71.7 1.9 %collective-permute-start.3 = (bf16[128,2304]{1,0:T(8,128)(2,1)S(1)}, bf16[128,2304]{1,0:T(8,128)(2,1)S(1)}, u32[]{:S(2)}, u32[]{:S(2)}) collective-permute-start(bf16[128,2304]{1,0:T(8,128)(2,1)S(1)} %collective-permute-done.1.refs_2_.refs_8_), channel_id=1, source_target_pairs={{0,8},{1,25},{2,10},{3,27},{4,12},{5,29},{6,14},{7,31},{8,16},{9,1... | collective-permute-start | bytes 1769480 | tf_op jit(solution)/shard_map/ppermute | solution.py:281
  73.6 2.9 %collective-permute-start.2 = (bf16[128,2304]{1,0:T(8,128)(2,1)S(1)}, bf16[128,2304]{1,0:T(8,128)(2,1)S(1)}, u32[]{:S(2)}, u32[]{:S(2)}) collective-permute-start(bf16[128,2304]{1,0:T(8,128)(2,1)S(1)} %collective-permute-done.1.refs_2_.refs_8_), channel_id=1, source_target_pairs={{0,32},{1,993},{2,34},{3,995},{4,36},{5,997},{6,38},{7,999},{8,40}... | collective-permute-start | bytes 1769480 | tf_op jit(solution)/shard_map/ppermute | solution.py:281
  76.5 0.0 collective-permute-done.5.refs_12_
  76.5 3.5 %collective-permute-start.6 = (bf16[128,2304]{1,0:T(8,128)(2,1)S(1)}, bf16[128,2304]{1,0:T(8,128)(2,1)S(1)}, u32[]{:S(2)}, u32[]{:S(2)}) collective-permute-start(bf16[128,2304]{1,0:T(8,128)(2,1)S(1)} %collective-permute-done.5.refs_12_), channel_id=1, source_target_pairs={{0,32},{1,993},{2,34},{3,995},{4,36},{5,997},{6,38},{7,999},{8,40}... | collective-permute-start | bytes 1769480 | tf_op jit(solution)/shard_map/ppermute | solution.py:281
  80.0 0.4 order.1.order_ref.refs_2_
  80.4 1.8 %turn.1 = (bf16[384,1024]{1,0:T(8,128)(2,1)S(1)}, bf16[384,1024]{1,0:T(8,128)(2,1)S(1)}) custom-call(bf16[8,96,1024]{2,1,0:T(8,128)(2,1)S(1)} %all-to-all-done.rows_ref.refs_1_, bf16[1024,1024]{1,0:T(8,128)(2,1)S(1)} %order.1.order_ref.refs_2_), custom_call_target="tpu_custom_call" | custom-call | tf_op jit(solution)/shard_map/turn/pallas_call | solution.py:17
  82.2 0.0 collective-permute-done.refs_1_.refs_7_
  82.2 0.0 collective-permute-done.4.refs_5_.refs_11_
  82.2 7.6 %collective-permute-done.3.refs_4_.refs_10_ = bf16[128,2304]{1,0:T(8,128)(2,1)S(1)} collective-permute-done((bf16[128,2304]{1,0:T(8,128)(2,1)S(1)}, bf16[128,2304]{1,0:T(8,128)(2,1)S(1)}, u32[]{:S(2)}, u32[]{:S(2)}) %collective-permute-start.3) | collective-permute-done | bytes 589856 | tf_op jit(solution)/shard_map/ppermute | solution.py:281
  89.8 0.0 collective-permute-done.2.refs_3_.refs_9_
  89.8 1.5 %partial.1 = (f32[384,768]{1,0:T(8,128)S(1)}, f32[384,768]{1,0:T(8,128)S(1)}, f32[384,768]{1,0:T(8,128)S(1)}) custom-call(bf16[384,1024]{1,0:T(8,128)(2,1)S(1)} %get-tuple-element.18.tok_ref.refs_0_, bf16[384,1024]{1,0:T(8,128)(2,1)S(1)} %get-tuple-element.19.grad_ref.refs_1_, bf16[128,2304]{1,0:T(8,128)(2,1)S(1)} %after.1.refs_0_.refs_6_, ...), custom_call_target="tpu_custom_call" | custom-call | tf_op jit(solution)/shard_map/partial/pallas_call | solution.py:17
  91.4 0.0 collective-permute-done.6.refs_13_
  91.4 5.3 %final.1 = (bf16[8,96,1024]{2,1,0:T(8,128)(2,1)}, f32[8,128]{1,0:T(8,128)S(1)}) custom-call(bf16[384,1024]{1,0:T(8,128)(2,1)S(1)} %get-tuple-element.18.tok_ref.refs_0_, bf16[384,1024]{1,0:T(8,128)(2,1)S(1)} %get-tuple-element.19.grad_ref.refs_1_, bf16[1024,1024]{1,0:T(8,128)(2,1)S(1)} %order.1.order_ref.refs_2_, f32[384,768]{1,0:T(8,128)S(1)} %get-tuple-element.21.refs_3_, ...), custom_call_target="tpu_custom_call" | custom-call | tf_op jit(solution)/shard_map/final/pallas_call | solution.py:314
  96.7 0.0 copy-start.1
  96.7 0.0 copy-start.2
  96.7 0.0 copy-start
  96.7 15.2 %all-to-all-start.1 = ((bf16[8,96,1024]{2,1,0:T(8,128)(2,1)}), bf16[8,96,1024]{2,1,0:T(8,128)(2,1)S(1)}, u32[]{:S(2)}, u32[]{:S(2)}) async-start(bf16[8,96,1024]{2,1,0:T(8,128)(2,1)} %get-tuple-element.27), calls=%async_computation.1 | async-start | bytes 3145728 | tf_op jit(solution)/shard_map/all_to_all | solution.py:278
  112.0 0.0 copy-done.1
  112.0 0.0 copy-done.2
  112.0 0.3 pick.1
  112.3 20.4 %all-to-all-done.1.back_ref = bf16[8,96,1024]{2,1,0:T(8,128)(2,1)S(1)} async-done(((bf16[8,96,1024]{2,1,0:T(8,128)(2,1)}), bf16[8,96,1024]{2,1,0:T(8,128)(2,1)S(1)}, u32[]{:S(2)}, u32[]{:S(2)}) %all-to-all-start.1) | async-done | bytes 1572896 | tf_op jit(solution)/shard_map/all_to_all | solution.py:278
  132.7 0.0 copy-done
  132.7 1.4 %post.1 = (bf16[128,1024]{1,0:T(8,128)(2,1)}, bf16[128,1024]{1,0:T(8,128)(2,1)}, f32[2,128]{1,0:T(2,128)}) custom-call(bf16[2,128,384]{2,1,0:T(8,128)(2,1)S(1)} %get-tuple-element.25.pick_ref, f32[128,128]{1,0:T(8,128)S(1)} %get-tuple-element.26.ccol_ref, bf16[128,1024]{1,0:T(8,128)(2,1)S(1)} %copy-done, bf16[8,96,1024]{2,1,0:T(8,128)(2,1)S(1)} %all-to-all-done.1.back_ref), custom_call_target="tpu_custom_call" | custom-call | tf_op jit(solution)/shard_map/post/pallas_call | solution.py:17
  (1 shorter events, 0.0 us)
Async XLA Ops:
  3.4 50.6 %all-to-all-start = ((bf16[8,96,1024]{2,1,0:T(8,128)(2,1)}), bf16[8,96,1024]{2,1,0:T(8,128)(2,1)S(1)}, u32[]{:S(2)}, u32[]{:S(2)}) async-start(bf16[8,96,1024]{2,1,0:T(8,128)(2,1)} %get-tuple-element.17), calls=%async_computation | async-start | bytes 3145728 | tf_op jit(solution)/shard_map/all_to_all | solution.py:278
  53.9 10.6 %collective-permute-start.1 = (bf16[128,2304]{1,0:T(8,128)(2,1)S(1)}, bf16[128,2304]{1,0:T(8,128)(2,1)S(1)}, u32[]{:S(2)}, u32[]{:S(2)}) collective-permute-start(bf16[128,2304]{1,0:T(8,128)(2,1)S(1)} %after.1.refs_0_.refs_6_), channel_id=1, source_target_pairs={{0,8},{1,25},{2,10},{3,27},{4,12},{5,29},{6,14},{7,31},{8,16},{9,1... | collective-permute-start | bytes 1769480 | tf_op jit(solution)/shard_map/ppermute | solution.py:281
  57.5 19.0 %collective-permute-start.5 = (bf16[128,2304]{1,0:T(8,128)(2,1)S(1)}, bf16[128,2304]{1,0:T(8,128)(2,1)S(1)}, u32[]{:S(2)}, u32[]{:S(2)}) collective-permute-start(bf16[128,2304]{1,0:T(8,128)(2,1)S(1)} %after.1.refs_0_.refs_6_), channel_id=1, source_target_pairs={{0,24},{1,9},{2,26},{3,11},{4,28},{5,13},{6,30},{7,15},{8,0},{9,17... | collective-permute-start | bytes 1769480 | tf_op jit(solution)/shard_map/ppermute | solution.py:281
  59.4 22.8 %collective-permute-start = (bf16[128,2304]{1,0:T(8,128)(2,1)S(1)}, bf16[128,2304]{1,0:T(8,128)(2,1)S(1)}, u32[]{:S(2)}, u32[]{:S(2)}) collective-permute-start(bf16[128,2304]{1,0:T(8,128)(2,1)S(1)} %after.1.refs_0_.refs_6_), channel_id=1, source_target_pairs={{0,32},{1,993},{2,34},{3,995},{4,36},{5,997},{6,38},{7,999},{8,40}... | collective-permute-start | bytes 1769480 | tf_op jit(solution)/shard_map/ppermute | solution.py:281
  64.6 17.7 %collective-permute-start.4 = (bf16[128,2304]{1,0:T(8,128)(2,1)S(1)}, bf16[128,2304]{1,0:T(8,128)(2,1)S(1)}, u32[]{:S(2)}, u32[]{:S(2)}) collective-permute-start(bf16[128,2304]{1,0:T(8,128)(2,1)S(1)} %collective-permute-done.1.refs_2_.refs_8_), channel_id=1, source_target_pairs={{0,40},{1,1017},{2,42},{3,1019},{4,44},{5,1021},{6,46},{7,1023},{8... | collective-permute-start | bytes 1769480 | tf_op jit(solution)/shard_map/ppermute | solution.py:281
  71.7 18.2 %collective-permute-start.3 = (bf16[128,2304]{1,0:T(8,128)(2,1)S(1)}, bf16[128,2304]{1,0:T(8,128)(2,1)S(1)}, u32[]{:S(2)}, u32[]{:S(2)}) collective-permute-start(bf16[128,2304]{1,0:T(8,128)(2,1)S(1)} %collective-permute-done.1.refs_2_.refs_8_), channel_id=1, source_target_pairs={{0,8},{1,25},{2,10},{3,27},{4,12},{5,29},{6,14},{7,31},{8,16},{9,1... | collective-permute-start | bytes 1769480 | tf_op jit(solution)/shard_map/ppermute | solution.py:281
  73.6 16.2 %collective-permute-start.2 = (bf16[128,2304]{1,0:T(8,128)(2,1)S(1)}, bf16[128,2304]{1,0:T(8,128)(2,1)S(1)}, u32[]{:S(2)}, u32[]{:S(2)}) collective-permute-start(bf16[128,2304]{1,0:T(8,128)(2,1)S(1)} %collective-permute-done.1.refs_2_.refs_8_), channel_id=1, source_target_pairs={{0,32},{1,993},{2,34},{3,995},{4,36},{5,997},{6,38},{7,999},{8,40}... | collective-permute-start | bytes 1769480 | tf_op jit(solution)/shard_map/ppermute | solution.py:281
  76.5 14.9 %collective-permute-start.6 = (bf16[128,2304]{1,0:T(8,128)(2,1)S(1)}, bf16[128,2304]{1,0:T(8,128)(2,1)S(1)}, u32[]{:S(2)}, u32[]{:S(2)}) collective-permute-start(bf16[128,2304]{1,0:T(8,128)(2,1)S(1)} %collective-permute-done.5.refs_12_), channel_id=1, source_target_pairs={{0,32},{1,993},{2,34},{3,995},{4,36},{5,997},{6,38},{7,999},{8,40}... | collective-permute-start | bytes 1769480 | tf_op jit(solution)/shard_map/ppermute | solution.py:281
  96.7 15.3 %copy-start.1 = (s32[128,2]{0,1:T(2,128)S(1)}, s32[128,2]{0,1:T(2,128)}, u32[]{:S(2)}) copy-start(s32[128,2]{0,1:T(2,128)} %param.8) | copy-start | bytes 3076
  96.7 15.3 %copy-start.2 = (f32[128,2]{0,1:T(2,128)S(1)}, f32[128,2]{0,1:T(2,128)}, u32[]{:S(2)}) copy-start(f32[128,2]{0,1:T(2,128)} %param.9) | copy-start | bytes 3076
  96.7 36.0 %copy-start = (bf16[128,1024]{1,0:T(8,128)(2,1)S(1)}, bf16[128,1024]{1,0:T(8,128)(2,1)}, u32[]{:S(2)}) copy-start(bf16[128,1024]{1,0:T(8,128)(2,1)} %cot_ref.1) | copy-start | bytes 786436
  96.7 36.0 %all-to-all-start.1 = ((bf16[8,96,1024]{2,1,0:T(8,128)(2,1)}), bf16[8,96,1024]{2,1,0:T(8,128)(2,1)S(1)}, u32[]{:S(2)}, u32[]{:S(2)}) async-start(bf16[8,96,1024]{2,1,0:T(8,128)(2,1)} %get-tuple-element.27), calls=%async_computation.1 | async-start | bytes 3145728 | tf_op jit(solution)/shard_map/all_to_all | solution.py:278

commit v6 on v4

--- a/solution.py
+++ b/solution.py
@@ -304,9 +304,8 @@
     own = lax.all_gather(joined, ALL, axis=0, tiled=True, axis_index_groups=far_groups)
     own = after(own, arrived)
     ahead, beside, behind = send(own, 0, 1), send(own, 1, 0), send(own, 0, -1)
-    across = send(ahead, 0, 1)
-    pieces = [own, beside, ahead, send(beside, 0, 1), behind, send(behind, 1, 0)]
-    pieces += [across, send(across, 1, 0)]
+    pieces = [own, beside, ahead, send(ahead, 1, 0), behind, send(own, 1, -1)]
+    pieces += [send(ahead, 0, 1), send(ahead, 1, 1)]
     count = len(pieces)
     order = call(lambda ref: order_kernel(zs, ref), "order", shape((width, width), BF16))
     rows_shape, sum_shape = shape((slots, width), BF16), shape((slots, ff), F32)

time: 135 us -> 141 us (1.044)
  waiting for transfers between devices: 28.5 us -> 36.8 us
  starting transfers between devices: 59.2 us -> 56.7 us
    ppermute x7, waiting for transfers between devices: 8.12 us -> 16.4 us  [send(): return lax.ppermute(values, ALL, shifted(dz, dy))]
    ppermute x7, starting transfers between devices: 27 us -> 23.9 us  [send(): return lax.ppermute(values, ALL, shifted(dz, dy))]
  transfers between devices with their start and end apart: 9 -> 9, of which waited for: 6 -> 4; matrix products, arithmetic and copies ran while one was open for 0% -> 0% of each run, Pallas kernels for 3% -> 3%
where the time goes in v6:
time: 141 us
  starting transfers between devices  56.7 us (40%)
  waiting for transfers between devices  36.8 us (26%)
  blocking collectives  32.9 us (23%)
  Pallas kernels  13.5 us (10%)
    all_gather x1, blocking collectives, on_device(): lax.all_gather(joined, ALL, axis=0, tiled=True, axis_index_groups=far_gro...  32.9 us
    all_to_all x2, starting transfers between devices, swap(): return lax.all_to_all(values, 'expert', 0, 0, tiled=True)  32.8 us
    ppermute x7, starting transfers between devices, send(): return lax.ppermute(values, ALL, shifted(dz, dy))  23.9 us
    all_to_all x2, waiting for transfers between devices, swap(): return lax.all_to_all(values, 'expert', 0, 0, tiled=True)  20.4 us
    ppermute x7, waiting for transfers between devices, send(): return lax.ppermute(values, ALL, shifted(dz, dy))  16.4 us
    pallas_call x1, Pallas kernels, on_device(): pl.pallas_call(lambda *refs: final_kernel(count, *refs), out_shape=(pltpu...  5.34 us
    pallas_call x4, Pallas kernels, call(): pl.pallas_call(body, out_shape=out_shape, in_specs=[spec] * len(args), ou...  5.13 us
  transfers between devices with their start and end apart: 9, of which 4 were waited for; matrix products, arithmetic and copies ran while one was open for 0% of the time, Pallas kernels for 3%

profile of v6, /device:TPU:1, one launch (start us, length us, event | category | flops | bytes accessed | tf_op | source)
XLA Modules:
  0.0 140.7 jit_solution(13993246641596812337)
XLA Ops:
  0.6 2.7 %pack.1 = (bf16[8,96,1024]{2,1,0:T(8,128)(2,1)}, bf16[8,2304]{1,0:T(8,128)(2,1)S(1)}) custom-call(bf16[1,8,768]{2,1,0:T(8,128)(2,1)} %refs_0_.1, bf16[1,8,768]{2,1,0:T(8,128)(2,1)} %refs_1_.1, bf16[1,8,768]{2,1,0:T(8,128)(2,1)} %refs_2_.1, s32[2,128]{1,0:T(2,128)} %bitcast.3, f32[2,128]{1,0:T(2,128)} %bitcast.5, bf16[128,1024]{1,0:T(8,128)(2,1)} %refs_5_.1, ...), custom_call_target="tpu_custom_call" | custom-call | tf_op jit(solution)/shard_map/pack/pallas_call | solution.py:289
  3.4 17.6 %all-to-all-start = ((bf16[8,96,1024]{2,1,0:T(8,128)(2,1)}), bf16[8,96,1024]{2,1,0:T(8,128)(2,1)S(1)}, u32[]{:S(2)}, u32[]{:S(2)}) async-start(bf16[8,96,1024]{2,1,0:T(8,128)(2,1)} %get-tuple-element.17), calls=%async_computation | async-start | bytes 3145728 | tf_op jit(solution)/shard_map/all_to_all | solution.py:278
  21.0 32.9 %all_gather.3.refs_0_ = bf16[128,2304]{1,0:T(8,128)(2,1)S(1)} all-gather(bf16[8,2304]{1,0:T(8,128)(2,1)S(1)} %get-tuple-element.20), channel_id=1, replica_groups={{0,64,128,192,256,320,384,448,512,576,640,704,768,832,896,960},{961,897..., dimensions={0}, use_global_device_ids=true | all-gather | bytes 626688 | tf_op jit(solution)/shard_map/all_gather | solution.py:304
  53.9 0.0 all-to-all-done.rows_ref.refs_1_
  53.9 3.5 %collective-permute-start.1 = (bf16[128,2304]{1,0:T(8,128)(2,1)S(1)}, bf16[128,2304]{1,0:T(8,128)(2,1)S(1)}, u32[]{:S(2)}, u32[]{:S(2)}) collective-permute-start(bf16[128,2304]{1,0:T(8,128)(2,1)S(1)} %after.1.refs_0_.refs_6_), channel_id=1, source_target_pairs={{0,8},{1,25},{2,10},{3,27},{4,12},{5,29},{6,14},{7,31},{8,16},{9,1... | collective-permute-start | bytes 1769480 | tf_op jit(solution)/shard_map/ppermute | solution.py:281
  57.5 2.9 %collective-permute-start.4 = (bf16[128,2304]{1,0:T(8,128)(2,1)S(1)}, bf16[128,2304]{1,0:T(8,128)(2,1)S(1)}, u32[]{:S(2)}, u32[]{:S(2)}) collective-permute-start(bf16[128,2304]{1,0:T(8,128)(2,1)S(1)} %after.1.refs_0_.refs_6_), channel_id=1, source_target_pairs={{0,56},{1,1001},{2,58},{3,1003},{4,60},{5,1005},{6,62},{7,1007},{8... | collective-permute-start | bytes 1769480 | tf_op jit(solution)/shard_map/ppermute | solution.py:281
  60.3 3.2 %collective-permute-start.3 = (bf16[128,2304]{1,0:T(8,128)(2,1)S(1)}, bf16[128,2304]{1,0:T(8,128)(2,1)S(1)}, u32[]{:S(2)}, u32[]{:S(2)}) collective-permute-start(bf16[128,2304]{1,0:T(8,128)(2,1)S(1)} %after.1.refs_0_.refs_6_), channel_id=1, source_target_pairs={{0,24},{1,9},{2,26},{3,11},{4,28},{5,13},{6,30},{7,15},{8,0},{9,17... | collective-permute-start | bytes 1769480 | tf_op jit(solution)/shard_map/ppermute | solution.py:281
  63.6 2.8 %collective-permute-start = (bf16[128,2304]{1,0:T(8,128)(2,1)S(1)}, bf16[128,2304]{1,0:T(8,128)(2,1)S(1)}, u32[]{:S(2)}, u32[]{:S(2)}) collective-permute-start(bf16[128,2304]{1,0:T(8,128)(2,1)S(1)} %after.1.refs_0_.refs_6_), channel_id=1, source_target_pairs={{0,32},{1,993},{2,34},{3,995},{4,36},{5,997},{6,38},{7,999},{8,40}... | collective-permute-start | bytes 1769480 | tf_op jit(solution)/shard_map/ppermute | solution.py:281
  66.4 0.0 collective-permute-done.1.refs_2_.refs_8_
  66.4 3.9 %collective-permute-start.2 = (bf16[128,2304]{1,0:T(8,128)(2,1)S(1)}, bf16[128,2304]{1,0:T(8,128)(2,1)S(1)}, u32[]{:S(2)}, u32[]{:S(2)}) collective-permute-start(bf16[128,2304]{1,0:T(8,128)(2,1)S(1)} %collective-permute-done.1.refs_2_.refs_8_), channel_id=1, source_target_pairs={{0,32},{1,993},{2,34},{3,995},{4,36},{5,997},{6,38},{7,999},{8,40}... | collective-permute-start | bytes 1769480 | tf_op jit(solution)/shard_map/ppermute | solution.py:281
  70.3 4.3 %collective-permute-start.6 = (bf16[128,2304]{1,0:T(8,128)(2,1)S(1)}, bf16[128,2304]{1,0:T(8,128)(2,1)S(1)}, u32[]{:S(2)}, u32[]{:S(2)}) collective-permute-start(bf16[128,2304]{1,0:T(8,128)(2,1)S(1)} %collective-permute-done.1.refs_2_.refs_8_), channel_id=1, source_target_pairs={{0,40},{1,1017},{2,42},{3,1019},{4,44},{5,1021},{6,46},{7,1023},{8... | collective-permute-start | bytes 1769480 | tf_op jit(solution)/shard_map/ppermute | solution.py:281
  74.6 0.0 collective-permute-done.4.refs_5_.refs_11_
  74.6 3.3 %collective-permute-start.5 = (bf16[128,2304]{1,0:T(8,128)(2,1)S(1)}, bf16[128,2304]{1,0:T(8,128)(2,1)S(1)}, u32[]{:S(2)}, u32[]{:S(2)}) collective-permute-start(bf16[128,2304]{1,0:T(8,128)(2,1)S(1)} %collective-permute-done.1.refs_2_.refs_8_), channel_id=1, source_target_pairs={{0,8},{1,25},{2,10},{3,27},{4,12},{5,29},{6,14},{7,31},{8,16},{9,1... | collective-permute-start | bytes 1769480 | tf_op jit(solution)/shard_map/ppermute | solution.py:281
  78.0 0.4 order.1.order_ref.refs_2_
  78.4 1.8 %turn.1 = (bf16[384,1024]{1,0:T(8,128)(2,1)S(1)}, bf16[384,1024]{1,0:T(8,128)(2,1)S(1)}) custom-call(bf16[8,96,1024]{2,1,0:T(8,128)(2,1)S(1)} %all-to-all-done.rows_ref.refs_1_, bf16[1024,1024]{1,0:T(8,128)(2,1)S(1)} %order.1.order_ref.refs_2_), custom_call_target="tpu_custom_call" | custom-call | tf_op jit(solution)/shard_map/turn/pallas_call | solution.py:17
  80.2 2.8 %collective-permute-done.3.refs_4_.refs_10_ = bf16[128,2304]{1,0:T(8,128)(2,1)S(1)} collective-permute-done((bf16[128,2304]{1,0:T(8,128)(2,1)S(1)}, bf16[128,2304]{1,0:T(8,128)(2,1)S(1)}, u32[]{:S(2)}, u32[]{:S(2)}) %collective-permute-start.3) | collective-permute-done | bytes 589856 | tf_op jit(solution)/shard_map/ppermute | solution.py:281
  83.0 0.0 collective-permute-done.refs_1_.refs_7_
  83.1 0.0 collective-permute-done.2.refs_3_.refs_9_
  83.1 1.5 %partial.1 = (f32[384,768]{1,0:T(8,128)S(1)}, f32[384,768]{1,0:T(8,128)S(1)}, f32[384,768]{1,0:T(8,128)S(1)}) custom-call(bf16[384,1024]{1,0:T(8,128)(2,1)S(1)} %get-tuple-element.18.tok_ref.refs_0_, bf16[384,1024]{1,0:T(8,128)(2,1)S(1)} %get-tuple-element.19.grad_ref.refs_1_, bf16[128,2304]{1,0:T(8,128)(2,1)S(1)} %after.1.refs_0_.refs_6_, ...), custom_call_target="tpu_custom_call" | custom-call | tf_op jit(solution)/shard_map/partial/pallas_call | solution.py:17
  84.6 3.5 %collective-permute-done.6.refs_13_ = bf16[128,2304]{1,0:T(8,128)(2,1)S(1)} collective-permute-done((bf16[128,2304]{1,0:T(8,128)(2,1)S(1)}, bf16[128,2304]{1,0:T(8,128)(2,1)S(1)}, u32[]{:S(2)}, u32[]{:S(2)}) %collective-permute-start.6) | collective-permute-done | bytes 589856 | tf_op jit(solution)/shard_map/ppermute | solution.py:281
  88.1 10.0 %collective-permute-done.5.refs_12_ = bf16[128,2304]{1,0:T(8,128)(2,1)S(1)} collective-permute-done((bf16[128,2304]{1,0:T(8,128)(2,1)S(1)}, bf16[128,2304]{1,0:T(8,128)(2,1)S(1)}, u32[]{:S(2)}, u32[]{:S(2)}) %collective-permute-start.5) | collective-permute-done | bytes 589856 | tf_op jit(solution)/shard_map/ppermute | solution.py:281
  98.1 5.3 %final.1 = (bf16[8,96,1024]{2,1,0:T(8,128)(2,1)}, f32[8,128]{1,0:T(8,128)S(1)}) custom-call(bf16[384,1024]{1,0:T(8,128)(2,1)S(1)} %get-tuple-element.18.tok_ref.refs_0_, bf16[384,1024]{1,0:T(8,128)(2,1)S(1)} %get-tuple-element.19.grad_ref.refs_1_, bf16[1024,1024]{1,0:T(8,128)(2,1)S(1)} %order.1.order_ref.refs_2_, f32[384,768]{1,0:T(8,128)S(1)} %get-tuple-element.21.refs_3_, ...), custom_call_target="tpu_custom_call" | custom-call | tf_op jit(solution)/shard_map/final/pallas_call | solution.py:314
  103.5 0.0 copy-start.1
  103.5 0.0 copy-start.2
  103.5 0.0 copy-start
  103.5 15.1 %all-to-all-start.1 = ((bf16[8,96,1024]{2,1,0:T(8,128)(2,1)}), bf16[8,96,1024]{2,1,0:T(8,128)(2,1)S(1)}, u32[]{:S(2)}, u32[]{:S(2)}) async-start(bf16[8,96,1024]{2,1,0:T(8,128)(2,1)} %get-tuple-element.27), calls=%async_computation.1 | async-start | bytes 3145728 | tf_op jit(solution)/shard_map/all_to_all | solution.py:278
  118.6 0.0 copy-done.1
  118.6 0.0 copy-done.2
  118.6 0.3 pick.1
  118.9 20.4 %all-to-all-done.1.back_ref = bf16[8,96,1024]{2,1,0:T(8,128)(2,1)S(1)} async-done(((bf16[8,96,1024]{2,1,0:T(8,128)(2,1)}), bf16[8,96,1024]{2,1,0:T(8,128)(2,1)S(1)}, u32[]{:S(2)}, u32[]{:S(2)}) %all-to-all-start.1) | async-done | bytes 1572896 | tf_op jit(solution)/shard_map/all_to_all | solution.py:278
  139.3 0.0 copy-done
  139.4 1.4 post.1
  (1 shorter events, 0.0 us)
Async XLA Ops:
  3.4 50.6 %all-to-all-start = ((bf16[8,96,1024]{2,1,0:T(8,128)(2,1)}), bf16[8,96,1024]{2,1,0:T(8,128)(2,1)S(1)}, u32[]{:S(2)}, u32[]{:S(2)}) async-start(bf16[8,96,1024]{2,1,0:T(8,128)(2,1)} %get-tuple-element.17), calls=%async_computation | async-start | bytes 3145728 | tf_op jit(solution)/shard_map/all_to_all | solution.py:278
  53.9 12.5 %collective-permute-start.1 = (bf16[128,2304]{1,0:T(8,128)(2,1)S(1)}, bf16[128,2304]{1,0:T(8,128)(2,1)S(1)}, u32[]{:S(2)}, u32[]{:S(2)}) collective-permute-start(bf16[128,2304]{1,0:T(8,128)(2,1)S(1)} %after.1.refs_0_.refs_6_), channel_id=1, source_target_pairs={{0,8},{1,25},{2,10},{3,27},{4,12},{5,29},{6,14},{7,31},{8,16},{9,1... | collective-permute-start | bytes 1769480 | tf_op jit(solution)/shard_map/ppermute | solution.py:281
  57.5 17.2 %collective-permute-start.4 = (bf16[128,2304]{1,0:T(8,128)(2,1)S(1)}, bf16[128,2304]{1,0:T(8,128)(2,1)S(1)}, u32[]{:S(2)}, u32[]{:S(2)}) collective-permute-start(bf16[128,2304]{1,0:T(8,128)(2,1)S(1)} %after.1.refs_0_.refs_6_), channel_id=1, source_target_pairs={{0,56},{1,1001},{2,58},{3,1003},{4,60},{5,1005},{6,62},{7,1007},{8... | collective-permute-start | bytes 1769480 | tf_op jit(solution)/shard_map/ppermute | solution.py:281
  60.3 22.7 %collective-permute-start.3 = (bf16[128,2304]{1,0:T(8,128)(2,1)S(1)}, bf16[128,2304]{1,0:T(8,128)(2,1)S(1)}, u32[]{:S(2)}, u32[]{:S(2)}) collective-permute-start(bf16[128,2304]{1,0:T(8,128)(2,1)S(1)} %after.1.refs_0_.refs_6_), channel_id=1, source_target_pairs={{0,24},{1,9},{2,26},{3,11},{4,28},{5,13},{6,30},{7,15},{8,0},{9,17... | collective-permute-start | bytes 1769480 | tf_op jit(solution)/shard_map/ppermute | solution.py:281
  63.6 19.5 %collective-permute-start = (bf16[128,2304]{1,0:T(8,128)(2,1)S(1)}, bf16[128,2304]{1,0:T(8,128)(2,1)S(1)}, u32[]{:S(2)}, u32[]{:S(2)}) collective-permute-start(bf16[128,2304]{1,0:T(8,128)(2,1)S(1)} %after.1.refs_0_.refs_6_), channel_id=1, source_target_pairs={{0,32},{1,993},{2,34},{3,995},{4,36},{5,997},{6,38},{7,999},{8,40}... | collective-permute-start | bytes 1769480 | tf_op jit(solution)/shard_map/ppermute | solution.py:281
  66.4 16.6 %collective-permute-start.2 = (bf16[128,2304]{1,0:T(8,128)(2,1)S(1)}, bf16[128,2304]{1,0:T(8,128)(2,1)S(1)}, u32[]{:S(2)}, u32[]{:S(2)}) collective-permute-start(bf16[128,2304]{1,0:T(8,128)(2,1)S(1)} %collective-permute-done.1.refs_2_.refs_8_), channel_id=1, source_target_pairs={{0,32},{1,993},{2,34},{3,995},{4,36},{5,997},{6,38},{7,999},{8,40}... | collective-permute-start | bytes 1769480 | tf_op jit(solution)/shard_map/ppermute | solution.py:281
  70.3 17.7 %collective-permute-start.6 = (bf16[128,2304]{1,0:T(8,128)(2,1)S(1)}, bf16[128,2304]{1,0:T(8,128)(2,1)S(1)}, u32[]{:S(2)}, u32[]{:S(2)}) collective-permute-start(bf16[128,2304]{1,0:T(8,128)(2,1)S(1)} %collective-permute-done.1.refs_2_.refs_8_), channel_id=1, source_target_pairs={{0,40},{1,1017},{2,42},{3,1019},{4,44},{5,1021},{6,46},{7,1023},{8... | collective-permute-start | bytes 1769480 | tf_op jit(solution)/shard_map/ppermute | solution.py:281
  74.6 23.5 %collective-permute-start.5 = (bf16[128,2304]{1,0:T(8,128)(2,1)S(1)}, bf16[128,2304]{1,0:T(8,128)(2,1)S(1)}, u32[]{:S(2)}, u32[]{:S(2)}) collective-permute-start(bf16[128,2304]{1,0:T(8,128)(2,1)S(1)} %collective-permute-done.1.refs_2_.refs_8_), channel_id=1, source_target_pairs={{0,8},{1,25},{2,10},{3,27},{4,12},{5,29},{6,14},{7,31},{8,16},{9,1... | collective-permute-start | bytes 1769480 | tf_op jit(solution)/shard_map/ppermute | solution.py:281
  103.5 15.2 %copy-start.1 = (s32[128,2]{0,1:T(2,128)S(1)}, s32[128,2]{0,1:T(2,128)}, u32[]{:S(2)}) copy-start(s32[128,2]{0,1:T(2,128)} %param.8) | copy-start | bytes 3076
  103.5 15.2 %copy-start.2 = (f32[128,2]{0,1:T(2,128)S(1)}, f32[128,2]{0,1:T(2,128)}, u32[]{:S(2)}) copy-start(f32[128,2]{0,1:T(2,128)} %param.9) | copy-start | bytes 3076
  103.5 35.9 %copy-start = (bf16[128,1024]{1,0:T(8,128)(2,1)S(1)}, bf16[128,1024]{1,0:T(8,128)(2,1)}, u32[]{:S(2)}) copy-start(bf16[128,1024]{1,0:T(8,128)(2,1)} %cot_ref.1) | copy-start | bytes 786436
  103.5 35.8 %all-to-all-start.1 = ((bf16[8,96,1024]{2,1,0:T(8,128)(2,1)}), bf16[8,96,1024]{2,1,0:T(8,128)(2,1)S(1)}, u32[]{:S(2)}, u32[]{:S(2)}) async-start(bf16[8,96,1024]{2,1,0:T(8,128)(2,1)} %get-tuple-element.27), calls=%async_computation.1 | async-start | bytes 3145728 | tf_op jit(solution)/shard_map/all_to_all | solution.py:278

commit v7 on v6

--- a/solution.py
+++ b/solution.py
@@ -147,10 +147,10 @@
     i = lax.broadcasted_iota(jnp.int32, (1, width), 1)
     r = lax.rem(i, depth)
     pos = lax.rem(i // depth, zs // PAR)
-    step = i // (depth * zs)
-    other = lax.rem(i // (depth * (zs // PAR)), PAR)
+    block = i // (depth * (zs // PAR))
+    other = jnp.where(block < 4, lax.rem(block, 2), block // 6)
     zi = jnp.where(core == 0, pos, zs // PAR - 1 - pos)
-    ahead = jnp.where(step == 1, -1, jnp.where(step == 2, 1, step - step // 3))
+    ahead = jnp.where(block < 2, 0, jnp.where(block < 4, 2, 2 * lax.rem(block, 2) - 1))
     y = lax.rem(my_y + NY + jnp.where(core == 0, ahead, -ahead), NY)
     z = zi * PAR + lax.rem(my_z + other, PAR)
     feature = (z * NY + y) * depth + r
@@ -203,7 +203,7 @@
         here = slice(t * tile, (t + 1) * tile)
         gate, up, hidden_grad = (
             sums[m][:, here]
-            + nn(rows_ref[:, last], pair(pieces[-2:], slice(m * ff + t * tile, m * ff + (t + 1) * tile)))
+            + nn(rows_ref[:, last], pair(pieces[-1:], slice(m * ff + t * tile, m * ff + (t + 1) * tile)))
             for m, rows_ref in enumerate((tok_ref, tok_ref, grad_ref))
         )
         sigma = 1.0 / (1.0 + jnp.exp(-gate))
@@ -213,7 +213,7 @@
         gate_grad_ref[:, here] = (hidden_grad * up * sigma * (1.0 + gate * (1.0 - sigma))).astype(BF16)
     copies = []
     for half, terms in enumerate((((hidden_ref, 2),), ((gate_grad_ref, 0), (up_grad_ref, 1)))):
-        for j in range(count // 2):
+        for j in range((count + 1) // 2):
             total = None
             for left_ref, m in terms:
                 part = nt(left_ref[...], pair(pieces[2 * j : 2 * j + 2], slice(m * ff, (m + 1) * ff)))
@@ -304,13 +304,13 @@
     own = lax.all_gather(joined, ALL, axis=0, tiled=True, axis_index_groups=far_groups)
     own = after(own, arrived)
     ahead, beside, behind = send(own, 0, 1), send(own, 1, 0), send(own, 0, -1)
-    pieces = [own, beside, ahead, send(ahead, 1, 0), behind, send(own, 1, -1)]
-    pieces += [send(ahead, 0, 1), send(ahead, 1, 1)]
+    pieces = [own, beside, send(ahead, 0, 1), send(ahead, 1, 1), ahead, behind]
+    pieces.append(send(after(jnp.concatenate([ahead, behind], axis=0), beside), 1, 0))
     count = len(pieces)
     order = call(lambda ref: order_kernel(zs, ref), "order", shape((width, width), BF16))
     rows_shape, sum_shape = shape((slots, width), BF16), shape((slots, ff), F32)
     turned = call(turn_kernel, "turn", (rows_shape,) * 2, arrived, order)
-    sums = call(partial_kernel, "partial", (sum_shape,) * 3, *turned, *pieces[:-2], mib=12)
+    sums = call(partial_kernel, "partial", (sum_shape,) * 3, *turned, *pieces[:-1], mib=12)
     results, late = pl.pallas_call(
         lambda *refs: final_kernel(count, *refs),
         out_shape=(pltpu.HBM(both.shape, BF16), shape((8, 128), F32)),

time: 141 us -> 144 us (1.021)
  waiting for transfers between devices: 36.8 us -> 39.8 us
    ppermute x7 -> x6, starting transfers between devices: 23.9 us -> 20.8 us  [send(): return lax.ppermute(values, ALL, shifted(dz, dy))]
    ppermute x7 -> x6, waiting for transfers between devices: 16.4 us -> 19.3 us  [send(): return lax.ppermute(values, ALL, shifted(dz, dy))]
    all_to_all x2, starting transfers between devices: 32.8 us -> 35.5 us  [swap(): return lax.all_to_all(values, 'expert', 0, 0, tiled=True)]
  transfers between devices with their start and end apart: 9 -> 8, of which waited for: 4 -> 6; matrix products, arithmetic and copies ran while one was open for 0% -> 0% of each run, Pallas kernels for 3% -> 3%
where the time goes in v7:
time: 144 us; the launch traced here: 143 us
  starting transfers between devices  56.3 us (39%)
  waiting for transfers between devices  39.8 us (28%)
  blocking collectives  32.9 us (23%)
  Pallas kernels  13.5 us (9%)
    all_to_all x2, starting transfers between devices, swap(): return lax.all_to_all(values, 'expert', 0, 0, tiled=True)  35.5 us
    all_gather x1, blocking collectives, on_device(): lax.all_gather(joined, ALL, axis=0, tiled=True, axis_index_groups=far_gro...  32.9 us
    ppermute x6, starting transfers between devices, send(): return lax.ppermute(values, ALL, shifted(dz, dy))  20.8 us
    all_to_all x2, waiting for transfers between devices, swap(): return lax.all_to_all(values, 'expert', 0, 0, tiled=True)  20.4 us
    ppermute x6, waiting for transfers between devices, send(): return lax.ppermute(values, ALL, shifted(dz, dy))  19.3 us
    pallas_call x1, Pallas kernels, on_device(): pl.pallas_call(lambda *refs: final_kernel(count, *refs), out_shape=(pltpu...  5.33 us
    pallas_call x4, Pallas kernels, call(): pl.pallas_call(body, out_shape=out_shape, in_specs=[spec] * len(args), ou...  5.13 us
  transfers between devices with their start and end apart: 8, of which 6 were waited for; matrix products, arithmetic and copies ran while one was open for 0% of the time, Pallas kernels for 3%

profile of v7, /device:TPU:1, one launch (start us, length us, event | category | flops | bytes accessed | tf_op | source)
XLA Modules:
  0.0 143.3 jit_solution(2188621341594161239)
XLA Ops:
  0.6 2.7 %pack.1 = (bf16[8,96,1024]{2,1,0:T(8,128)(2,1)}, bf16[8,2304]{1,0:T(8,128)(2,1)S(1)}) custom-call(bf16[1,8,768]{2,1,0:T(8,128)(2,1)} %refs_0_.1, bf16[1,8,768]{2,1,0:T(8,128)(2,1)} %refs_1_.1, bf16[1,8,768]{2,1,0:T(8,128)(2,1)} %refs_2_.1, s32[2,128]{1,0:T(2,128)} %bitcast.3, f32[2,128]{1,0:T(2,128)} %bitcast.5, bf16[128,1024]{1,0:T(8,128)(2,1)} %refs_5_.1, ...), custom_call_target="tpu_custom_call" | custom-call | tf_op jit(solution)/shard_map/pack/pallas_call | solution.py:289
  3.4 17.6 %all-to-all-start = ((bf16[8,96,1024]{2,1,0:T(8,128)(2,1)}), bf16[8,96,1024]{2,1,0:T(8,128)(2,1)S(1)}, u32[]{:S(2)}, u32[]{:S(2)}) async-start(bf16[8,96,1024]{2,1,0:T(8,128)(2,1)} %get-tuple-element.17), calls=%async_computation | async-start | bytes 3145728 | tf_op jit(solution)/shard_map/all_to_all | solution.py:278
  21.0 32.9 %all_gather.3.refs_0_ = bf16[128,2304]{1,0:T(8,128)(2,1)S(1)} all-gather(bf16[8,2304]{1,0:T(8,128)(2,1)S(1)} %get-tuple-element.20), channel_id=1, replica_groups={{0,64,128,192,256,320,384,448,512,576,640,704,768,832,896,960},{961,897..., dimensions={0}, use_global_device_ids=true | all-gather | bytes 626688 | tf_op jit(solution)/shard_map/all_gather | solution.py:304
  53.9 0.0 all-to-all-done.rows_ref.refs_1_
  53.9 3.0 %collective-permute-start.4 = (bf16[128,2304]{1,0:T(8,128)(2,1)S(1)}, bf16[128,2304]{1,0:T(8,128)(2,1)S(1)}, u32[]{:S(2)}, u32[]{:S(2)}) collective-permute-start(bf16[128,2304]{1,0:T(8,128)(2,1)S(1)} %after.2.refs_0_.refs_6_), channel_id=1, source_target_pairs={{0,24},{1,9},{2,26},{3,11},{4,28},{5,13},{6,30},{7,15},{8,0},{9,17... | collective-permute-start | bytes 1769480 | tf_op jit(solution)/shard_map/ppermute | solution.py:281
  56.9 3.5 %collective-permute-start.1 = (bf16[128,2304]{1,0:T(8,128)(2,1)S(1)}, bf16[128,2304]{1,0:T(8,128)(2,1)S(1)}, u32[]{:S(2)}, u32[]{:S(2)}) collective-permute-start(bf16[128,2304]{1,0:T(8,128)(2,1)S(1)} %after.2.refs_0_.refs_6_), channel_id=1, source_target_pairs={{0,8},{1,25},{2,10},{3,27},{4,12},{5,29},{6,14},{7,31},{8,16},{9,1... | collective-permute-start | bytes 1769480 | tf_op jit(solution)/shard_map/ppermute | solution.py:281
  60.4 3.5 %collective-permute-start = (bf16[128,2304]{1,0:T(8,128)(2,1)S(1)}, bf16[128,2304]{1,0:T(8,128)(2,1)S(1)}, u32[]{:S(2)}, u32[]{:S(2)}) collective-permute-start(bf16[128,2304]{1,0:T(8,128)(2,1)S(1)} %after.2.refs_0_.refs_6_), channel_id=1, source_target_pairs={{0,32},{1,993},{2,34},{3,995},{4,36},{5,997},{6,38},{7,999},{8,40}... | collective-permute-start | bytes 1769480 | tf_op jit(solution)/shard_map/ppermute | solution.py:281
  63.9 1.8 %collective-permute-done.4.refs_5_.refs_11_ = bf16[128,2304]{1,0:T(8,128)(2,1)S(1)} collective-permute-done((bf16[128,2304]{1,0:T(8,128)(2,1)S(1)}, bf16[128,2304]{1,0:T(8,128)(2,1)S(1)}, u32[]{:S(2)}, u32[]{:S(2)}) %collective-permute-start.4) | collective-permute-done | bytes 589856 | tf_op jit(solution)/shard_map/ppermute | solution.py:281
  65.8 2.3 %collective-permute-done.1.refs_4_.refs_10_ = bf16[128,2304]{1,0:T(8,128)(2,1)S(1)} collective-permute-done((bf16[128,2304]{1,0:T(8,128)(2,1)S(1)}, bf16[128,2304]{1,0:T(8,128)(2,1)S(1)}, u32[]{:S(2)}, u32[]{:S(2)}) %collective-permute-start.1) | collective-permute-done | bytes 589856 | tf_op jit(solution)/shard_map/ppermute | solution.py:281
  68.1 0.1 pad_maximum_fusion.refs_0_
  68.1 3.2 %collective-permute-done.refs_1_.refs_7_ = bf16[128,2304]{1,0:T(8,128)(2,1)S(1)} collective-permute-done((bf16[128,2304]{1,0:T(8,128)(2,1)S(1)}, bf16[128,2304]{1,0:T(8,128)(2,1)S(1)}, u32[]{:S(2)}, u32[]{:S(2)}) %collective-permute-start) | collective-permute-done | bytes 589856 | tf_op jit(solution)/shard_map/ppermute | solution.py:281
  71.4 4.7 %collective-permute-start.5 = (bf16[256,2304]{1,0:T(8,128)(2,1)S(1)}, bf16[256,2304]{1,0:T(8,128)(2,1)S(1)}, u32[]{:S(2)}, u32[]{:S(2)}) collective-permute-start(bf16[256,2304]{1,0:T(8,128)(2,1)S(1)} %after.3), channel_id=1, source_target_pairs={{0,32},{1,993},{2,34},{3,995},{4,36},{5,997},{6,38},{7,999},{8,40}... | collective-permute-start | bytes 3538952 | tf_op jit(solution)/shard_map/ppermute | solution.py:281
  76.1 3.1 %collective-permute-start.3 = (bf16[128,2304]{1,0:T(8,128)(2,1)S(1)}, bf16[128,2304]{1,0:T(8,128)(2,1)S(1)}, u32[]{:S(2)}, u32[]{:S(2)}) collective-permute-start(bf16[128,2304]{1,0:T(8,128)(2,1)S(1)} %collective-permute-done.1.refs_4_.refs_10_), channel_id=1, source_target_pairs={{0,40},{1,1017},{2,42},{3,1019},{4,44},{5,1021},{6,46},{7,1023},{8... | collective-permute-start | bytes 1769480 | tf_op jit(solution)/shard_map/ppermute | solution.py:281
  79.2 3.0 %collective-permute-start.2 = (bf16[128,2304]{1,0:T(8,128)(2,1)S(1)}, bf16[128,2304]{1,0:T(8,128)(2,1)S(1)}, u32[]{:S(2)}, u32[]{:S(2)}) collective-permute-start(bf16[128,2304]{1,0:T(8,128)(2,1)S(1)} %collective-permute-done.1.refs_4_.refs_10_), channel_id=1, source_target_pairs={{0,8},{1,25},{2,10},{3,27},{4,12},{5,29},{6,14},{7,31},{8,16},{9,1... | collective-permute-start | bytes 1769480 | tf_op jit(solution)/shard_map/ppermute | solution.py:281
  82.2 0.4 order.1.order_ref.refs_2_
  82.6 1.8 %turn.1 = (bf16[384,1024]{1,0:T(8,128)(2,1)S(1)}, bf16[384,1024]{1,0:T(8,128)(2,1)S(1)}) custom-call(bf16[8,96,1024]{2,1,0:T(8,128)(2,1)S(1)} %all-to-all-done.rows_ref.refs_1_, bf16[1024,1024]{1,0:T(8,128)(2,1)S(1)} %order.1.order_ref.refs_2_), custom_call_target="tpu_custom_call" | custom-call | tf_op jit(solution)/shard_map/turn/pallas_call | solution.py:17
  84.4 11.1 %collective-permute-done.3.refs_3_.refs_9_ = bf16[128,2304]{1,0:T(8,128)(2,1)S(1)} collective-permute-done((bf16[128,2304]{1,0:T(8,128)(2,1)S(1)}, bf16[128,2304]{1,0:T(8,128)(2,1)S(1)}, u32[]{:S(2)}, u32[]{:S(2)}) %collective-permute-start.3) | collective-permute-done | bytes 589856 | tf_op jit(solution)/shard_map/ppermute | solution.py:281
  95.5 0.9 collective-permute-done.2.refs_2_.refs_8_
  96.4 1.5 %partial.1 = (f32[384,768]{1,0:T(8,128)S(1)}, f32[384,768]{1,0:T(8,128)S(1)}, f32[384,768]{1,0:T(8,128)S(1)}) custom-call(bf16[384,1024]{1,0:T(8,128)(2,1)S(1)} %get-tuple-element.18.tok_ref.refs_0_, bf16[384,1024]{1,0:T(8,128)(2,1)S(1)} %get-tuple-element.19.grad_ref.refs_1_, bf16[128,2304]{1,0:T(8,128)(2,1)S(1)} %after.2.refs_0_.refs_6_, ...), custom_call_target="tpu_custom_call" | custom-call | tf_op jit(solution)/shard_map/partial/pallas_call | solution.py:17
  98.0 0.0 collective-permute-done.5.refs_12_
  98.0 5.3 %final.1 = (bf16[8,96,1024]{2,1,0:T(8,128)(2,1)}, f32[8,128]{1,0:T(8,128)S(1)}) custom-call(bf16[384,1024]{1,0:T(8,128)(2,1)S(1)} %get-tuple-element.18.tok_ref.refs_0_, bf16[384,1024]{1,0:T(8,128)(2,1)S(1)} %get-tuple-element.19.grad_ref.refs_1_, bf16[1024,1024]{1,0:T(8,128)(2,1)S(1)} %order.1.order_ref.refs_2_, f32[384,768]{1,0:T(8,128)S(1)} %get-tuple-element.21.refs_3_, ...), custom_call_target="tpu_custom_call" | custom-call | tf_op jit(solution)/shard_map/final/pallas_call | solution.py:314
  103.3 0.0 copy-start.1
  103.3 0.0 copy-start.2
  103.3 0.0 copy-start
  103.3 17.9 %all-to-all-start.1 = ((bf16[8,96,1024]{2,1,0:T(8,128)(2,1)}), bf16[8,96,1024]{2,1,0:T(8,128)(2,1)S(1)}, u32[]{:S(2)}, u32[]{:S(2)}) async-start(bf16[8,96,1024]{2,1,0:T(8,128)(2,1)} %get-tuple-element.27), calls=%async_computation.1 | async-start | bytes 3145728 | tf_op jit(solution)/shard_map/all_to_all | solution.py:278
  121.2 0.0 copy-done.1
  121.2 0.0 copy-done.2
  121.2 0.3 pick.1
  121.5 20.4 %all-to-all-done.1.back_ref = bf16[8,96,1024]{2,1,0:T(8,128)(2,1)S(1)} async-done(((bf16[8,96,1024]{2,1,0:T(8,128)(2,1)}), bf16[8,96,1024]{2,1,0:T(8,128)(2,1)S(1)}, u32[]{:S(2)}, u32[]{:S(2)}) %all-to-all-start.1) | async-done | bytes 1572896 | tf_op jit(solution)/shard_map/all_to_all | solution.py:278
  141.9 0.0 copy-done
  141.9 1.4 post.1
  (2 shorter events, 0.0 us)
Async XLA Ops:
  3.4 50.6 %all-to-all-start = ((bf16[8,96,1024]{2,1,0:T(8,128)(2,1)}), bf16[8,96,1024]{2,1,0:T(8,128)(2,1)S(1)}, u32[]{:S(2)}, u32[]{:S(2)}) async-start(bf16[8,96,1024]{2,1,0:T(8,128)(2,1)} %get-tuple-element.17), calls=%async_computation | async-start | bytes 3145728 | tf_op jit(solution)/shard_map/all_to_all | solution.py:278
  53.9 11.8 %collective-permute-start.4 = (bf16[128,2304]{1,0:T(8,128)(2,1)S(1)}, bf16[128,2304]{1,0:T(8,128)(2,1)S(1)}, u32[]{:S(2)}, u32[]{:S(2)}) collective-permute-start(bf16[128,2304]{1,0:T(8,128)(2,1)S(1)} %after.2.refs_0_.refs_6_), channel_id=1, source_target_pairs={{0,24},{1,9},{2,26},{3,11},{4,28},{5,13},{6,30},{7,15},{8,0},{9,17... | collective-permute-start | bytes 1769480 | tf_op jit(solution)/shard_map/ppermute | solution.py:281
  56.9 11.1 %collective-permute-start.1 = (bf16[128,2304]{1,0:T(8,128)(2,1)S(1)}, bf16[128,2304]{1,0:T(8,128)(2,1)S(1)}, u32[]{:S(2)}, u32[]{:S(2)}) collective-permute-start(bf16[128,2304]{1,0:T(8,128)(2,1)S(1)} %after.2.refs_0_.refs_6_), channel_id=1, source_target_pairs={{0,8},{1,25},{2,10},{3,27},{4,12},{5,29},{6,14},{7,31},{8,16},{9,1... | collective-permute-start | bytes 1769480 | tf_op jit(solution)/shard_map/ppermute | solution.py:281
  60.4 10.9 %collective-permute-start = (bf16[128,2304]{1,0:T(8,128)(2,1)S(1)}, bf16[128,2304]{1,0:T(8,128)(2,1)S(1)}, u32[]{:S(2)}, u32[]{:S(2)}) collective-permute-start(bf16[128,2304]{1,0:T(8,128)(2,1)S(1)} %after.2.refs_0_.refs_6_), channel_id=1, source_target_pairs={{0,32},{1,993},{2,34},{3,995},{4,36},{5,997},{6,38},{7,999},{8,40}... | collective-permute-start | bytes 1769480 | tf_op jit(solution)/shard_map/ppermute | solution.py:281
  71.4 26.6 %collective-permute-start.5 = (bf16[256,2304]{1,0:T(8,128)(2,1)S(1)}, bf16[256,2304]{1,0:T(8,128)(2,1)S(1)}, u32[]{:S(2)}, u32[]{:S(2)}) collective-permute-start(bf16[256,2304]{1,0:T(8,128)(2,1)S(1)} %after.3), channel_id=1, source_target_pairs={{0,32},{1,993},{2,34},{3,995},{4,36},{5,997},{6,38},{7,999},{8,40}... | collective-permute-start | bytes 3538952 | tf_op jit(solution)/shard_map/ppermute | solution.py:281
  76.1 19.4 %collective-permute-start.3 = (bf16[128,2304]{1,0:T(8,128)(2,1)S(1)}, bf16[128,2304]{1,0:T(8,128)(2,1)S(1)}, u32[]{:S(2)}, u32[]{:S(2)}) collective-permute-start(bf16[128,2304]{1,0:T(8,128)(2,1)S(1)} %collective-permute-done.1.refs_4_.refs_10_), channel_id=1, source_target_pairs={{0,40},{1,1017},{2,42},{3,1019},{4,44},{5,1021},{6,46},{7,1023},{8... | collective-permute-start | bytes 1769480 | tf_op jit(solution)/shard_map/ppermute | solution.py:281
  79.2 17.2 %collective-permute-start.2 = (bf16[128,2304]{1,0:T(8,128)(2,1)S(1)}, bf16[128,2304]{1,0:T(8,128)(2,1)S(1)}, u32[]{:S(2)}, u32[]{:S(2)}) collective-permute-start(bf16[128,2304]{1,0:T(8,128)(2,1)S(1)} %collective-permute-done.1.refs_4_.refs_10_), channel_id=1, source_target_pairs={{0,8},{1,25},{2,10},{3,27},{4,12},{5,29},{6,14},{7,31},{8,16},{9,1... | collective-permute-start | bytes 1769480 | tf_op jit(solution)/shard_map/ppermute | solution.py:281
  103.3 17.9 %copy-start.1 = (s32[128,2]{0,1:T(2,128)S(1)}, s32[128,2]{0,1:T(2,128)}, u32[]{:S(2)}) copy-start(s32[128,2]{0,1:T(2,128)} %param.8) | copy-start | bytes 3076
  103.3 17.9 %copy-start.2 = (f32[128,2]{0,1:T(2,128)S(1)}, f32[128,2]{0,1:T(2,128)}, u32[]{:S(2)}) copy-start(f32[128,2]{0,1:T(2,128)} %param.9) | copy-start | bytes 3076
  103.3 38.6 %copy-start = (bf16[128,1024]{1,0:T(8,128)(2,1)S(1)}, bf16[128,1024]{1,0:T(8,128)(2,1)}, u32[]{:S(2)}) copy-start(bf16[128,1024]{1,0:T(8,128)(2,1)} %cot_ref.1) | copy-start | bytes 786436
  103.3 38.6 %all-to-all-start.1 = ((bf16[8,96,1024]{2,1,0:T(8,128)(2,1)}), bf16[8,96,1024]{2,1,0:T(8,128)(2,1)S(1)}, u32[]{:S(2)}, u32[]{:S(2)}) async-start(bf16[8,96,1024]{2,1,0:T(8,128)(2,1)} %get-tuple-element.27), calls=%async_computation.1 | async-start | bytes 3145728 | tf_op jit(solution)/shard_map/all_to_all | solution.py:278
